TPU v7x, 32 devices: a whole 2x2x4 slice. The times are simulated.
32 devices in a mesh: row: 8 (over z, y), col: 4 (over x, core).
Axes of the slice: x: 2, y: 2, z: 4, core: 2. Of those that a mesh axis runs over, the one named last changes fastest.
Arguments:
- grid_values: bfloat16 [128, 256, 384], P(('row', 'col')), may hold values from -0.21875 to 0.21875
- external: float32 [128, 256], P(('row', 'col')), may hold values from 0 to 6
- tiles: int32 [128, 3], P(('row', 'col')), may hold values from 0 to 31, as said below
- kinetic: bfloat16 [16384, 16384], P('row', 'col'), may hold values from -0.046875 to 0.046875
- orbitals: bfloat16 [16384, 256], P(('row', 'col')), may hold values from -6 to 6
Outputs:
- filtered: float32 [16384, 256], P(('row', 'col'))
Inputs may be any that keep to these rules, and one draw needn't show every extreme that they name: Each batch names 3 distinct tiles in increasing order. Among the 4 batches of one device no tile is named more than 2 times; in every draw some tile is named exactly 2 times by the batches of every device.
All inputs are finite; a program needn't handle non-finite values.
Results may differ from a plain program's by a relative error of at most 0.0064.
Values may be sent and summed in bfloat16 or wider, within the bound.
No kernel may reach another device: no remote copies, remote signals or barrier semaphores. Data moves between devices by JAX's collectives and lax.ppermute only.
A program may use at most 128 MiB of HBM per device.

v0:
```python
import jax
import jax.numpy as jnp
from jax import lax
from jax.sharding import PartitionSpec as P

TILE = 128
LISTED = 3
CAP = 2
LIST = 384


center = 1.0
spread = 2.5


def body(grid_values, external, tiles, kinetic, orbitals):
    row_count = lax.axis_size("row")
    shard_rows, orbital_count = orbitals.shape
    per_shard = shard_rows // TILE
    group_tiles = row_count * per_shard
    batch_count = tiles.shape[0]
    group_orbitals = lax.all_gather(orbitals, "row", axis=0, tiled=True)
    listed_orbitals = group_orbitals.reshape(group_tiles, TILE, orbital_count)[tiles].reshape(
        batch_count, LIST, orbital_count
    )
    waves = jnp.einsum(
        "bpl,blk->bpk", grid_values, listed_orbitals, preferred_element_type=jnp.float32
    )
    density = jnp.sum(waves * waves, axis=2)
    potential = external - jnp.cbrt(3.0 * density / jnp.pi)
    weighted = (potential[:, :, None] * grid_values).astype(jnp.bfloat16)
    integrals = jnp.einsum(
        "bpl,bpm->blm", grid_values, weighted, preferred_element_type=jnp.float32
    )
    flat_tiles = tiles.reshape(-1)
    batch_of = jnp.arange(flat_tiles.shape[0], dtype=jnp.int32) // LISTED
    earlier = jnp.sum(
        (flat_tiles[:, None] == flat_tiles[None, :]) & (batch_of[None, :] < batch_of[:, None]),
        axis=1,
    )
    target = flat_tiles * CAP + earlier
    strips = integrals.reshape(flat_tiles.shape[0], TILE, LIST)
    outgoing = jnp.zeros((group_tiles * CAP, TILE, LIST), jnp.float32).at[target].set(strips)
    column_tiles = (
        jnp.zeros((group_tiles * CAP, LISTED), jnp.int32)
        .at[target]
        .set(jnp.repeat(tiles, LISTED, axis=0))
    )
    arrived, arrived_tiles = (
        lax.all_to_all(
            outgoing.reshape(row_count, per_shard * CAP, TILE, LIST),
            "row",
            split_axis=0,
            concat_axis=0,
            tiled=True,
        ),
        lax.all_to_all(
            column_tiles.reshape(row_count, per_shard * CAP, LISTED),
            "row",
            split_axis=0,
            concat_axis=0,
            tiled=True,
        ),
    )
    slot_total = row_count * per_shard * CAP
    local_tile = jnp.arange(slot_total, dtype=jnp.int32) % (per_shard * CAP) // CAP
    pieces = arrived.reshape(slot_total, TILE, LISTED, TILE).transpose(0, 2, 1, 3)
    summed = (
        jnp.zeros((per_shard, group_tiles, TILE, TILE), jnp.float32)
        .at[local_tile[:, None], arrived_tiles.reshape(slot_total, LISTED)]
        .add(pieces)
    )
    grid_rows = summed.transpose(0, 2, 1, 3).reshape(shard_rows, group_tiles * TILE)
    row_start = lax.axis_index("col") * shard_rows
    updated = (
        lax.dynamic_slice_in_dim(kinetic, row_start, shard_rows, 0).astype(jnp.float32) + grid_rows
    )
    hamiltonian = lax.dynamic_update_slice_in_dim(
        kinetic, updated.astype(jnp.bfloat16), row_start, 0
    )

    def add_piece(piece):
        return jnp.dot(hamiltonian, piece, preferred_element_type=jnp.float32)

    def times_ham(vectors):
        return add_piece(lax.all_gather(vectors, "row", axis=0, tiled=True))

    def filter_step(partial_value, vectors):
        reduced = lax.psum_scatter(partial_value, "col", scatter_dimension=0, tiled=True)
        return reduced / spread - center / spread * vectors.astype(jnp.float32)

    first_term = filter_step(
        jnp.dot(hamiltonian, group_orbitals, preferred_element_type=jnp.float32), orbitals
    ).astype(jnp.bfloat16)
    second_term = (
        2.0 * filter_step(times_ham(first_term), first_term) - orbitals.astype(jnp.float32)
    ).astype(jnp.bfloat16)
    return 2.0 * filter_step(times_ham(second_term), second_term) - first_term.astype(jnp.float32)


def solution(mesh):
    return jax.shard_map(
        body,
        mesh=mesh,
        in_specs=(
            P(("row", "col"), None, None),
            P(("row", "col"), None),
            P(("row", "col"), None),
            P("row", "col"),
            P(("row", "col"), None),
        ),
        out_specs=P(("row", "col"), None),
        check_vma=False,
    )
```

profile of v0, /device:TPU:0, one launch (start us, length us, event | category | flops | bytes accessed | tf_op | source)
XLA Modules:
  0.0 689.2 jit_solution(16975187709251839917)
XLA Ops:
  6.5 14.1 %copy.62 = bf16[2048,4096]{1,0:T(8,128)(2,1)} copy(bf16[2048,4096]{1,0:T(8,128)(2,1)} %param.8) | data formatting | bytes 33554432
  21.2 0.2 convert_reduce_fusion
  21.4 0.6 scatter_custom_fusion
  22.0 0.7 copy.44
  22.7 7.3 %all-to-all-start = ((s32[8,8,3]{1,2,0:T(4,128)}), s32[8,8,3]{1,2,0:T(4,128)S(1)}, u32[]{:S(2)}, u32[]{:S(2)}) async-start(s32[8,8,3]{1,2,0:T(4,128)} %copy.44), calls=%async_computation | async-start | bytes 32768 | tf_op jit(solution)/shard_map/all_to_all | solution.py:57
  30.1 42.6 %all-gather.4.cloned.1.call-done = bf16[4096,256]{1,0:T(8,128)(2,1)} async-done(((bf16[512,256]{1,0:T(8,128)(2,1)}), bf16[4096,256]{1,0:T(8,128)(2,1)}) %all-gather.4.cloned.1.call-update) | async-done | bytes 2097168 | tf_op jit(solution)/shard_map/all_gather | solution.py:22
  72.8 2.2 gather_fusion
  75.0 0.5 fusion.2
  75.5 0.8 fusion.3
  76.3 6.0 broadcast_in_dim.13
  82.3 5.7 scatter_fusion
  88.0 12.6 %copy.49 = f32[8,8,128,384]{2,3,1,0:T(8,128)} copy(f32[8,8,128,384]{3,2,1,0:T(8,128)} %bitcast.45) | data formatting | bytes 25165824 | tf_op jit(solution)/shard_map/reshape | solution.py:51
  100.6 5.4 all-to-all-start.1
  106.2 0.1 copy.46
  106.3 0.1 reshape.179
  106.4 271.7 %all-to-all-done.1 = f32[8,8,128,384]{2,3,1,0:T(8,128)} async-done(((f32[8,8,128,384]{2,3,1,0:T(8,128)}), f32[8,8,128,384]{2,3,1,0:T(8,128)}, u32[]{:S(2)}, u32[]{:S(2)}) %all-to-all-start.1) | async-done | bytes 12582944 | tf_op jit(solution)/shard_map/all_to_all | solution.py:50
  378.1 12.6 %copy.50 = f32[64,3,128,128]{3,2,1,0:T(8,128)} copy(f32[64,3,128,128]{2,3,1,0:T(8,128)} %bitcast.9) | data formatting | bytes 25165824 | tf_op jit(solution)/shard_map/transpose | solution.py:67
  390.7 4.4 broadcast_in_dim.10
  395.1 39.3 %scatter_fusion.1 = f32[4,32,128,128]{3,2,1,0:T(8,128)} fusion(f32[4,32,128,128]{3,2,1,0:T(8,128)} %broadcast_in_dim.10, s32[192]{0:T(256)S(1)} %reshape.179, f32[192,128,128]{2,1,0:T(8,128)} %bitcast.44), kind=kCustom, calls=%fused_computation.3 | custom fusion | flops 3145728 | bytes 37750272 | tf_op jit(solution)/shard_map/scatter-add | solution.py:71
  434.4 8.2 %copy.51 = f32[4,128,32,128]{3,2,1,0:T(8,128)S(1)} copy(f32[4,128,32,128]{3,1,2,0:T(8,128)} %bitcast.43) | data formatting | bytes 16777216 | tf_op jit(solution)/shard_map/transpose | solution.py:73
  442.6 9.5 %fusion.1 = bf16[2048,4096]{1,0:T(8,128)(2,1)} fusion(bf16[2048,4096]{1,0:T(8,128)(2,1)} %copy.62, s32[]{:T(128)S(6)} %select_n.69, f32[64,8,32,128]{3,2,1,0:T(8,128)S(1)} %bitcast.46), kind=kLoop, calls=%fused_computation.6 | loop fusion | flops 6291456 | bytes 16777220 | tf_op jit(solution)/shard_map/dynamic_update_slice | solution.py:78
  452.1 9.5 %fusion.16 = f32[2048,256]{1,0:T(8,128)} fusion(bf16[2048,4096]{1,0:T(8,128)(2,1)} %fusion.1, bf16[4096,256]{1,0:T(8,128)(2,1)S(1)} %copy-done.4), kind=kOutput, calls=%fused_computation.49 | convolution fusion | flops 4294967296 | bytes 20971520 | tf_op jit(solution)/shard_map/dot_general | solution.py:93
  461.7 30.7 %reduce-scatter.4.cloned.1.call-done = f32[512,256]{1,0:T(8,128)} async-done(((f32[2048,256]{1,0:T(8,128)}), f32[512,256]{1,0:T(8,128)}) %reduce-scatter.4.cloned.1.call-update) | async-done | bytes 524304 | tf_op jit(solution)/shard_map/reduce_scatter | solution.py:89
  492.4 1.8 fusion.6
  494.3 49.8 %all-gather.6.cloned.1.call-done = bf16[4096,256]{1,0:T(8,128)(2,1)} async-done(((bf16[512,256]{1,0:T(8,128)(2,1)}), bf16[4096,256]{1,0:T(8,128)(2,1)}) %all-gather.6.cloned.1.call-update) | async-done | bytes 2097168 | tf_op jit(solution)/shard_map/all_gather | solution.py:86
  544.1 12.4 %fusion.17 = f32[2048,256]{1,0:T(8,128)} fusion(bf16[2048,4096]{1,0:T(8,128)(2,1)} %fusion.1, bf16[4096,256]{1,0:T(8,128)(2,1)} %all-gather.6.cloned.1.call-done), kind=kOutput, calls=%fused_computation.50 | convolution fusion | flops 4294967296 | bytes 20971520 | tf_op jit(solution)/shard_map/dot_general | solution.py:83
  556.6 30.0 %reduce-scatter.6.cloned.1.call-done = f32[512,256]{1,0:T(8,128)} async-done(((f32[2048,256]{1,0:T(8,128)}), f32[512,256]{1,0:T(8,128)}) %reduce-scatter.6.cloned.1.call-update) | async-done | bytes 524304 | tf_op jit(solution)/shard_map/reduce_scatter | solution.py:89
  586.6 1.9 fusion.7
  588.5 49.4 %all-gather.8.cloned.1.call-done = bf16[4096,256]{1,0:T(8,128)(2,1)} async-done(((bf16[512,256]{1,0:T(8,128)(2,1)}), bf16[4096,256]{1,0:T(8,128)(2,1)}) %all-gather.8.cloned.1.call-update) | async-done | bytes 2097168 | tf_op jit(solution)/shard_map/all_gather | solution.py:86
  637.9 12.4 %fusion.18 = f32[2048,256]{1,0:T(8,128)} fusion(bf16[2048,4096]{1,0:T(8,128)(2,1)} %fusion.1, bf16[4096,256]{1,0:T(8,128)(2,1)} %all-gather.8.cloned.1.call-done), kind=kOutput, calls=%fused_computation.51 | convolution fusion | flops 4294967296 | bytes 20971520 | tf_op jit(solution)/shard_map/dot_general | solution.py:83
  650.4 30.1 %reduce-scatter.8.cloned.1.call-done = f32[512,256]{1,0:T(8,128)} async-done(((f32[2048,256]{1,0:T(8,128)}), f32[512,256]{1,0:T(8,128)}) %reduce-scatter.8.cloned.1.call-update) | async-done | bytes 524304 | tf_op jit(solution)/shard_map/reduce_scatter | solution.py:89
  680.4 2.0 convert_subtract_fusion
  (44 shorter events, 1.1 us)
Async XLA Ops:
  6.5 14.1 %copy-start.5 = (s32[4,3]{1,0:T(4,128)S(1)}, s32[4,3]{1,0:T(4,128)}, u32[]{:S(2)}) copy-start(s32[4,3]{1,0:T(4,128)} %param.7) | copy-start | bytes 148
  6.5 68.4 %copy-start.1 = (bf16[4,256,384]{2,1,0:T(8,128)(2,1)S(1)}, bf16[4,256,384]{2,1,0:T(8,128)(2,1)}, u32[]{:S(2)}) copy-start(bf16[4,256,384]{2,1,0:T(8,128)(2,1)} %param.5) | copy-start | bytes 2359300
  6.5 68.9 %copy-start.6 = (f32[4,256]{1,0:T(4,128)S(1)}, f32[4,256]{1,0:T(4,128)}, u32[]{:S(2)}) copy-start(f32[4,256]{1,0:T(4,128)} %param.6) | copy-start | bytes 12292
  6.5 66.2 %all-gather.4.cloned.1.call-start = ((), (), s32[]{:S(2)}) async-start(), calls=%async_computation.5 | async-start | bytes 2359296 | tf_op jit(solution)/shard_map/all_gather | solution.py:22
  22.7 77.9 %all-to-all-start = ((s32[8,8,3]{1,2,0:T(4,128)}), s32[8,8,3]{1,2,0:T(4,128)S(1)}, u32[]{:S(2)}, u32[]{:S(2)}) async-start(s32[8,8,3]{1,2,0:T(4,128)} %copy.44), calls=%async_computation | async-start | bytes 32768 | tf_op jit(solution)/shard_map/all_to_all | solution.py:57
  100.6 277.5 %all-to-all-start.1 = ((f32[8,8,128,384]{2,3,1,0:T(8,128)}), f32[8,8,128,384]{2,3,1,0:T(8,128)}, u32[]{:S(2)}, u32[]{:S(2)}) async-start(f32[8,8,128,384]{2,3,1,0:T(8,128)} %copy.49), calls=%async_computation.1 | async-start | bytes 25165824 | tf_op jit(solution)/shard_map/all_to_all | solution.py:50
  106.0 386.4 %reduce-scatter.4.cloned.1.call-start = ((), (), s32[]{:S(2)}) async-start(), calls=%async_computation.6 | async-start | bytes 2621440 | tf_op jit(solution)/shard_map/reduce_scatter | solution.py:89
  442.6 9.5 %copy-start.4 = (bf16[4096,256]{1,0:T(8,128)(2,1)S(1)}, bf16[4096,256]{1,0:T(8,128)(2,1)}, u32[]{:S(2)}) copy-start(bf16[4096,256]{1,0:T(8,128)(2,1)} %all-gather.4.cloned.1.call-done) | copy-start | bytes 6291460
  452.1 40.3 %copy-start.2 = (bf16[512,256]{1,0:T(8,128)(2,1)S(1)}, bf16[512,256]{1,0:T(8,128)(2,1)}, u32[]{:S(2)}) copy-start(bf16[512,256]{1,0:T(8,128)(2,1)} %param.9) | copy-start | bytes 786436
  461.6 82.4 %all-gather.6.cloned.1.call-start = ((), (), s32[]{:S(2)}) async-start(), calls=%async_computation.7 | async-start | bytes 2359296 | tf_op jit(solution)/shard_map/all_gather | solution.py:86
  494.2 92.4 %copy-start = (bf16[512,256]{1,0:T(8,128)(2,1)S(1)}, bf16[512,256]{1,0:T(8,128)(2,1)}, u32[]{:S(2)}) copy-start(bf16[512,256]{1,0:T(8,128)(2,1)} %fusion.6) | copy-start | bytes 786436
  494.2 92.3 %reduce-scatter.6.cloned.1.call-start = ((), (), s32[]{:S(2)}) async-start(), calls=%async_computation.8 | async-start | bytes 2621440 | tf_op jit(solution)/shard_map/reduce_scatter | solution.py:89
  556.5 81.4 %all-gather.8.cloned.1.call-start = ((), (), s32[]{:S(2)}) async-start(), calls=%async_computation.9 | async-start | bytes 2359296 | tf_op jit(solution)/shard_map/all_gather | solution.py:86
  588.5 92.0 %copy-start.3 = (bf16[512,256]{1,0:T(8,128)(2,1)S(1)}, bf16[512,256]{1,0:T(8,128)(2,1)}, u32[]{:S(2)}) copy-start(bf16[512,256]{1,0:T(8,128)(2,1)} %fusion.7) | copy-start | bytes 786436
  588.5 91.9 %reduce-scatter.8.cloned.1.call-start = ((), (), s32[]{:S(2)}) async-start(), calls=%async_computation.10 | async-start | bytes 2621440 | tf_op jit(solution)/shard_map/reduce_scatter | solution.py:89
Sparse Core Ops, SparseCore 0:
  20.7 51.9 all-gather.3
  461.8 30.5 reduce-scatter.3
  494.7 49.2 all-gather.5
  556.6 29.9 reduce-scatter.5
  588.6 49.2 all-gather.7
  650.5 29.8 reduce-scatter.7
where the time goes:
time: 691 us; the launch traced here: 689 us
  waiting for transfers between devices  504 us (73%)
  local copies, waits for them, and re-layouts  68.1 us (10%)
  other arithmetic  54.7 us (8%)
  matrix products  35.6 us (5%)
  between operations  13.6 us (2%)
  starting transfers between devices  12.9 us (2%)
    all_to_all x1, waiting for transfers between devices, body(): lax.all_to_all(outgoing.reshape(row_count, per_shard * CAP, TILE, LIST),...  272 us
    all_gather x2, waiting for transfers between devices, times_ham(): return add_piece(lax.all_gather(vectors, 'row', axis=0, tiled=True))  99.2 us
    reduce_scatter x3, waiting for transfers between devices, filter_step(): lax.psum_scatter(partial_value, 'col', scatter_dimension=0, tiled=True)  90.8 us
    all_gather x1, waiting for transfers between devices, body(): group_orbitals = lax.all_gather(orbitals, 'row', axis=0, tiled=True)  42.6 us
    scatter-add x1, other arithmetic, body(): summed = jnp.zeros((per_shard, group_tiles, TILE, TILE), jnp.float32).at[...  39.3 us
    dot_general x2, matrix products, add_piece(): return jnp.dot(hamiltonian, piece, preferred_element_type=jnp.float32)  24.8 us
    unnamed x16, local copies, waits for them, and re-layouts  14.2 us
  transfers between devices with their start and end apart: 8, of which 7 were waited for; matrix products, arithmetic and copies ran while one was open for 4% of the time, Pallas kernels for 0%

commit v1 on v0

v1 whole, which is shorter than its diff:
```python
import functools

import jax
import jax.numpy as jnp
from jax import lax
from jax.experimental import pallas as pl
from jax.experimental.pallas import tpu as pltpu
from jax.sharding import PartitionSpec as P

TILE = 128
center = 1.0
spread = 2.5


def own_rows_kernel(listed, per_shard, batches, where_ref, tiles_ref, values_ref, potential_ref, kinetic_ref, out_ref, total):
    batch = pl.program_id(0)

    @pl.when(batch == 0)
    def _():
        total[...] = kinetic_ref[...].astype(jnp.float32)

    first = where_ref[1] * per_shard
    spots = [tiles_ref[batch * listed + i] for i in range(listed)]
    owned = [(s >= first) & (s < first + per_shard) for s in spots]

    @pl.when(functools.reduce(jnp.logical_or, owned))
    def _():
        values = values_ref[0]
        lane = lax.broadcasted_iota(jnp.int32, potential_ref.shape, 1)
        potential = jnp.sum(jnp.where(lane == batch, potential_ref[...], 0.0), axis=1, keepdims=True)
        weighted = (potential * values.astype(jnp.float32)).astype(jnp.bfloat16)
        for i in range(listed):

            @pl.when(owned[i])
            def _(i=i):
                strip = lax.dot_general(
                    values[:, i * TILE : (i + 1) * TILE],
                    weighted,
                    (((0,), (0,)), ((), ())),
                    preferred_element_type=jnp.float32,
                )
                rows = pl.ds(pl.multiple_of((spots[i] - first) * TILE, TILE), TILE)
                for j in range(listed):
                    columns = pl.ds(pl.multiple_of(spots[j] * TILE, TILE), TILE)
                    total[rows, columns] += strip[:, j * TILE : (j + 1) * TILE]

    @pl.when(batch == batches - 1)
    def _():
        out_ref[...] = total[...].astype(jnp.bfloat16)


def own_rows(where, tiles, values, potential, kinetic, shard_rows):
    batches, points, length = values.shape
    listed = length // TILE
    width = kinetic.shape[1]
    return pl.pallas_call(
        functools.partial(own_rows_kernel, listed, shard_rows // TILE, batches),
        out_shape=jax.ShapeDtypeStruct((shard_rows, width), jnp.bfloat16),
        grid_spec=pltpu.PrefetchScalarGridSpec(
            num_scalar_prefetch=2,
            grid=(batches,),
            in_specs=[
                pl.BlockSpec((1, points, length), lambda b, w, t: (b, 0, 0)),
                pl.BlockSpec((points, batches), lambda b, w, t: (0, 0)),
                pl.BlockSpec((shard_rows, width), lambda b, w, t: (w[0], 0)),
            ],
            out_specs=pl.BlockSpec((shard_rows, width), lambda b, w, t: (0, 0)),
            scratch_shapes=[pltpu.VMEM((shard_rows, width), jnp.float32)],
        ),
        compiler_params=pltpu.CompilerParams(vmem_limit_bytes=48 * 2**20),
        cost_estimate=pl.CostEstimate(
            flops=batches * 2 * points * length * TILE,
            bytes_accessed=values.size * 2 + shard_rows * width * 4,
            transcendentals=0,
        ),
    )(where, tiles, values, potential, kinetic)


def product_kernel(where_ref, kinetic_ref, own_ref, vectors_ref, partial_ref, mine_ref):
    block = pl.program_id(0)

    @pl.when(block != where_ref[0])
    def _():
        partial_ref[...] = jnp.dot(
            kinetic_ref[...], vectors_ref[...], preferred_element_type=jnp.float32
        ).astype(jnp.bfloat16)

    @pl.when(block == where_ref[0])
    def _():
        partial_ref[...] = jnp.zeros_like(partial_ref)
        mine_ref[...] = jnp.dot(
            own_ref[...], vectors_ref[...], preferred_element_type=jnp.float32
        )


def product(where, kinetic, own, vectors):
    rows, width = kinetic.shape
    shard_rows, count = own.shape[0], vectors.shape[1]
    return pl.pallas_call(
        product_kernel,
        out_shape=(
            jax.ShapeDtypeStruct((rows, count), jnp.bfloat16),
            jax.ShapeDtypeStruct((shard_rows, count), jnp.float32),
        ),
        grid_spec=pltpu.PrefetchScalarGridSpec(
            num_scalar_prefetch=1,
            grid=(rows // shard_rows,),
            in_specs=[
                pl.BlockSpec((shard_rows, width), lambda b, w: (b, 0)),
                pl.BlockSpec((shard_rows, width), lambda b, w: (0, 0)),
                pl.BlockSpec((width, count), lambda b, w: (0, 0)),
            ],
            out_specs=(
                pl.BlockSpec((shard_rows, count), lambda b, w: (b, 0)),
                pl.BlockSpec((shard_rows, count), lambda b, w: (0, 0)),
            ),
        ),
        compiler_params=pltpu.CompilerParams(vmem_limit_bytes=48 * 2**20),
        cost_estimate=pl.CostEstimate(
            flops=2 * rows * width * count,
            bytes_accessed=(rows + shard_rows) * width * 2 + width * count * 2 + rows * count * 2,
            transcendentals=0,
        ),
    )(where, kinetic, own, vectors)


def body(grid_values, external, tiles, kinetic, orbitals):
    shard_rows, orbital_count = orbitals.shape
    batch_count, points, length = grid_values.shape
    where = jnp.stack([lax.axis_index("col"), lax.axis_index("row")]).astype(jnp.int32)

    def gather(array):
        return lax.all_gather(array, "row", axis=0, tiled=True)

    group_orbitals = gather(orbitals)
    group_values = gather(grid_values)
    group_tiles = gather(tiles)
    listed_orbitals = group_orbitals.reshape(-1, TILE, orbital_count)[tiles].reshape(
        batch_count, length, orbital_count
    )
    waves = jnp.einsum(
        "bpl,blk->bpk", grid_values, listed_orbitals, preferred_element_type=jnp.float32
    )
    density = jnp.sum(waves * waves, axis=2)
    potential = external - jnp.cbrt(3.0 * density / jnp.pi)
    group_potential = gather(potential)
    own = own_rows(
        where, group_tiles.reshape(-1), group_values, group_potential.T, kinetic, shard_rows
    )

    def filter_step(group_vectors, vectors):
        partial, mine = product(where, kinetic, own, group_vectors)
        arrived = lax.all_to_all(
            partial.reshape(-1, shard_rows, orbital_count), "col", split_axis=0, concat_axis=0
        )
        reduced = jnp.sum(arrived.astype(jnp.float32), axis=0) + mine
        return reduced / spread - center / spread * vectors.astype(jnp.float32)

    first_term = filter_step(group_orbitals, orbitals).astype(jnp.bfloat16)
    second_term = (
        2.0 * filter_step(gather(first_term), first_term) - orbitals.astype(jnp.float32)
    ).astype(jnp.bfloat16)
    return 2.0 * filter_step(gather(second_term), second_term) - first_term.astype(jnp.float32)


def solution(mesh):
    return jax.shard_map(
        body,
        mesh=mesh,
        in_specs=(
            P(("row", "col"), None, None),
            P(("row", "col"), None),
            P(("row", "col"), None),
            P("row", "col"),
            P(("row", "col"), None),
        ),
        out_specs=P(("row", "col"), None),
        check_vma=False,
    )
```

time: 691 us -> 376 us (0.54)
  waiting for transfers between devices: 504 us -> 188 us
  blocking collectives: 0 us -> 111 us
  local copies, waits for them, and re-layouts: 68.1 us -> 7.65 us
  Pallas kernels: 0 us -> 51.9 us
  other arithmetic: 54.7 us -> 3.82 us
  matrix products: 35.6 us -> 0.5 us
  starting transfers between devices: 12.9 us -> 0.12 us
    all_to_all x2 -> x0, waiting for transfers between devices: 272 us -> none  [the longest x1 272 us: body(): lax.all_to_all(outgoing.reshape(row_count, per_shard * CAP, TILE, LIST),...]
    reduce_scatter x3 -> x0, waiting for transfers between devices: 90.8 us -> none  [filter_step(): lax.psum_scatter(partial_value, 'col', scatter_dimension=0, tiled=True)]
    all_gather x0 -> x2, blocking collectives: none -> 58.9 us  [gather(): return lax.all_gather(array, 'row', axis=0, tiled=True)]
    pallas_call x0 -> x4, Pallas kernels: none -> 51.9 us  [the longest x3 30.9 us: product(): pl.pallas_call(product_kernel, out_shape=(jax.ShapeDtypeStruct((rows, cou...]
    all_to_all x0 -> x3, blocking collectives: none -> 51.7 us  [filter_step(): lax.all_to_all(partial.reshape(-1, shard_rows, orbital_count), 'col', spl...]
    all_gather x3 -> x4, waiting for transfers between devices: 142 us -> 186 us  [gather(): return lax.all_gather(array, 'row', axis=0, tiled=True)]
    scatter-add x1 -> x0, other arithmetic: 39.3 us -> none  [body(): summed = jnp.zeros((per_shard, group_tiles, TILE, TILE), jnp.float32).at[...]
    dot_general x4 -> x0, matrix products: 35.1 us -> none  [the longest x2 24.8 us: add_piece(): return jnp.dot(hamiltonian, piece, preferred_element_type=jnp.float32)]
  transfers between devices with their start and end apart: 8 -> 4, of which waited for: 7 -> 4; matrix products, arithmetic and copies ran while one was open for 4% -> 1% of each run, Pallas kernels for 0% -> 0%
where the time goes in v1:
time: 376 us
  waiting for transfers between devices  188 us (50%)
  blocking collectives  111 us (30%)
  Pallas kernels  51.9 us (14%)
  between operations  13.3 us (4%)
  local copies, waits for them, and re-layouts  7.65 us (2%)
  other arithmetic  3.82 us (1%)
    all_gather x4, waiting for transfers between devices, gather(): return lax.all_gather(array, 'row', axis=0, tiled=True)  186 us
    all_gather x2, blocking collectives, gather(): return lax.all_gather(array, 'row', axis=0, tiled=True)  58.9 us
    all_to_all x3, blocking collectives, filter_step(): lax.all_to_all(partial.reshape(-1, shard_rows, orbital_count), 'col', spl...  51.7 us
    pallas_call x3, Pallas kernels, product(): pl.pallas_call(product_kernel, out_shape=(jax.ShapeDtypeStruct((rows, cou...  30.9 us
    pallas_call x1, Pallas kernels, own_rows(): pl.pallas_call(functools.partial(own_rows_kernel, listed, shard_rows // T...  21 us
  transfers between devices with their start and end apart: 4, of which 4 were waited for; matrix products, arithmetic and copies ran while one was open for 1% of the time, Pallas kernels for 0%

profile of v1, /device:TPU:0, one launch (start us, length us, event | category | flops | bytes accessed | tf_op | source)
XLA Modules:
  0.0 375.9 jit_solution(15101922081012689095)
XLA Ops:
  6.5 0.7 all-gather.9.cloned.1.call-update
  7.3 0.7 all-gather.7.cloned.1.call-update
  8.1 0.7 compare_select_fusion
  8.8 0.1 reshape.26
  8.8 28.0 %all-gather = s32[8,4,3]{2,1,0:T(4,128)S(1)} all-gather(s32[1,4,3]{2,1,0:T(4,128)} %bitcast.19), channel_id=1, replica_groups=mesh['row'=8,'col'=4] {'row'}, dimensions={0}, use_global_device_ids=true | all-gather | bytes 432 | tf_op jit(solution)/shard_map/all_gather | solution.py:133
  36.9 0.1 reshape.18.tiles_ref
  37.0 0.1 pad_add_fusion.where_ref
  37.1 24.5 %all-gather.9.cloned.1.call-done.vectors_ref = bf16[4096,256]{1,0:T(8,128)(2,1)} async-done(((bf16[512,256]{1,0:T(8,128)(2,1)}), bf16[4096,256]{1,0:T(8,128)(2,1)}) %all-gather.9.cloned.1.call-update) | async-done | bytes 2097168 | tf_op jit(solution)/shard_map/all_gather | solution.py:133
  61.6 2.2 gather_fusion
  63.8 0.5 fusion
  64.3 30.9 %all-gather.1 = f32[8,4,256]{2,1,0:T(4,128)S(1)} all-gather(f32[1,4,256]{2,1,0:T(4,128)S(1)} %subtract_bitcast_fusion), channel_id=1, replica_groups=mesh['row'=8,'col'=4] {'row'}, dimensions={0}, use_global_device_ids=true | all-gather | bytes 36864 | tf_op jit(solution)/shard_map/all_gather | solution.py:133
  95.2 0.1 copy.10
  95.3 66.2 %all-gather.7.cloned.1.call-done.values_ref = bf16[32,256,384]{2,1,0:T(8,128)(2,1)} async-done(((bf16[4,256,384]{2,1,0:T(8,128)(2,1)}), bf16[32,256,384]{2,1,0:T(8,128)(2,1)}) %all-gather.7.cloned.1.call-update) | async-done | bytes 6291472 | tf_op jit(solution)/shard_map/all_gather | solution.py:133
  161.5 21.0 %shard_map.55.own_ref = bf16[512,4096]{1,0:T(8,128)(2,1)S(1)} custom-call(s32[2]{0:T(128)S(1)} %pad_add_fusion.where_ref, s32[96]{0:T(128)S(1)} %reshape.18.tiles_ref, bf16[32,256,384]{2,1,0:T(8,128)(2,1)} %all-gather.7.cloned.1.call-done.values_ref, f32[256,32]{1,0:T(8,128)S(1)} %bitcast.17, bf16[2048,4096]{1,0:T(8,128)(2,1)} %kinetic_ref.7), custom_call_target="tpu_custom_call" | custom-call | flops 805306368 | bytes 14680064 | tf_op jit(solution)/shard_map/pallas_call | solution.py:56
  182.5 1.9 copy-done
  184.4 10.3 %shard_map.56 = (bf16[2048,256]{1,0:T(8,128)(2,1)S(1)}, f32[512,256]{1,0:T(8,128)S(1)}) custom-call(s32[2]{0:T(128)S(1)} %pad_add_fusion.where_ref, bf16[2048,4096]{1,0:T(8,128)(2,1)} %kinetic_ref.7, bf16[512,4096]{1,0:T(8,128)(2,1)} %copy-done, bf16[4096,256]{1,0:T(8,128)(2,1)S(1)} %copy-done.1), custom_call_target="tpu_custom_call" | custom-call | flops 4294967296 | bytes 24117248 | tf_op jit(solution)/shard_map/pallas_call | solution.py:99
  194.8 17.5 %all_to_all.15 = bf16[4,512,256]{2,1,0:T(8,128)(2,1)S(1)} all-to-all(bf16[4,512,256]{2,1,0:T(8,128)(2,1)S(1)} %bitcast.15), channel_id=1, replica_groups=mesh['row'=8,'col'=4] {'col'}, dimensions={0} | all-to-all | bytes 2097152 | tf_op jit(solution)/shard_map/all_to_all | solution.py:153
  212.3 0.1 convert_reduce_fusion.2
  212.4 0.8 fusion.2
  213.3 0.0 all-gather.13.cloned.1.call-start
  213.3 48.8 %all-gather.11.cloned.1.call-done.vectors_ref = bf16[4096,256]{1,0:T(8,128)(2,1)} async-done(((bf16[512,256]{1,0:T(8,128)(2,1)}), bf16[4096,256]{1,0:T(8,128)(2,1)}) %all-gather.11.cloned.1.call-update) | async-done | bytes 2097168 | tf_op jit(solution)/shard_map/all_gather | solution.py:133
  262.1 1.6 copy-done.2
  263.7 10.3 %shard_map.57 = (bf16[2048,256]{1,0:T(8,128)(2,1)S(1)}, f32[512,256]{1,0:T(8,128)S(1)}) custom-call(s32[2]{0:T(128)S(1)} %pad_add_fusion.where_ref, bf16[2048,4096]{1,0:T(8,128)(2,1)} %kinetic_ref.7, bf16[512,4096]{1,0:T(8,128)(2,1)} %copy-done, bf16[4096,256]{1,0:T(8,128)(2,1)S(1)} %copy-done.2), custom_call_target="tpu_custom_call" | custom-call | flops 4294967296 | bytes 24117248 | tf_op jit(solution)/shard_map/pallas_call | solution.py:99
  274.0 17.1 %all_to_all.16 = bf16[4,512,256]{2,1,0:T(8,128)(2,1)S(1)} all-to-all(bf16[4,512,256]{2,1,0:T(8,128)(2,1)S(1)} %bitcast.16), channel_id=1, replica_groups=mesh['row'=8,'col'=4] {'col'}, dimensions={0} | all-to-all | bytes 2097152 | tf_op jit(solution)/shard_map/all_to_all | solution.py:153
  291.2 0.1 convert_reduce_fusion.1
  291.3 0.9 fusion.3
  292.2 47.0 %all-gather.13.cloned.1.call-done.vectors_ref = bf16[4096,256]{1,0:T(8,128)(2,1)} async-done(((bf16[512,256]{1,0:T(8,128)(2,1)}), bf16[4096,256]{1,0:T(8,128)(2,1)}) %all-gather.13.cloned.1.call-update) | async-done | bytes 2097168 | tf_op jit(solution)/shard_map/all_gather | solution.py:133
  339.2 1.6 copy-done.3
  340.8 10.3 %shard_map.58 = (bf16[2048,256]{1,0:T(8,128)(2,1)S(1)}, f32[512,256]{1,0:T(8,128)S(1)}) custom-call(s32[2]{0:T(128)S(1)} %pad_add_fusion.where_ref, bf16[2048,4096]{1,0:T(8,128)(2,1)} %kinetic_ref.7, bf16[512,4096]{1,0:T(8,128)(2,1)} %copy-done, bf16[4096,256]{1,0:T(8,128)(2,1)S(1)} %copy-done.3), custom_call_target="tpu_custom_call" | custom-call | flops 4294967296 | bytes 24117248 | tf_op jit(solution)/shard_map/pallas_call | solution.py:99
  351.1 17.1 %all_to_all.17 = bf16[4,512,256]{2,1,0:T(8,128)(2,1)S(1)} all-to-all(bf16[4,512,256]{2,1,0:T(8,128)(2,1)S(1)} %bitcast.14), channel_id=1, replica_groups=mesh['row'=8,'col'=4] {'col'}, dimensions={0} | all-to-all | bytes 2097152 | tf_op jit(solution)/shard_map/all_to_all | solution.py:153
  368.3 0.1 convert_reduce_fusion
  368.4 0.9 convert_subtract_fusion
  (23 shorter events, 0.2 us)
Async XLA Ops:
  6.5 57.2 %copy-start.7 = (bf16[4,256,384]{2,1,0:T(8,128)(2,1)S(1)}, bf16[4,256,384]{2,1,0:T(8,128)(2,1)}, u32[]{:S(2)}) copy-start(bf16[4,256,384]{2,1,0:T(8,128)(2,1)} %param.5) | copy-start | bytes 2359300
  6.5 55.0 %all-gather.9.cloned.1.call-start = ((), (), s32[]{:S(2)}) async-start(), calls=%async_computation.4 | async-start | bytes 2359296 | tf_op jit(solution)/shard_map/all_gather | solution.py:133
  7.3 57.0 %copy-start.8 = (f32[4,256]{1,0:T(4,128)S(1)}, f32[4,256]{1,0:T(4,128)}, u32[]{:S(2)}) copy-start(f32[4,256]{1,0:T(4,128)} %param.6) | copy-start | bytes 12292
  7.3 154.2 %all-gather.7.cloned.1.call-start = ((), (), s32[]{:S(2)}) async-start(), calls=%async_computation.3 | async-start | bytes 7077888 | tf_op jit(solution)/shard_map/all_gather | solution.py:133
  8.0 254.1 %all-gather.11.cloned.1.call-start = ((), (), s32[]{:S(2)}) async-start(), calls=%async_computation.5 | async-start | bytes 2359296 | tf_op jit(solution)/shard_map/all_gather | solution.py:133
  161.5 23.0 %copy-start.1 = (bf16[4096,256]{1,0:T(8,128)(2,1)S(1)}, bf16[4096,256]{1,0:T(8,128)(2,1)}, u32[]{:S(2)}) copy-start(bf16[4096,256]{1,0:T(8,128)(2,1)} %all-gather.9.cloned.1.call-done.vectors_ref) | copy-start | bytes 6291460
  182.5 2.0 copy-start
  194.8 17.6 %copy-start.5 = (bf16[512,256]{1,0:T(8,128)(2,1)S(1)}, bf16[512,256]{1,0:T(8,128)(2,1)}, u32[]{:S(2)}) copy-start(bf16[512,256]{1,0:T(8,128)(2,1)} %param.9) | copy-start | bytes 786436
  213.3 126.0 %all-gather.13.cloned.1.call-start = ((), (), s32[]{:S(2)}) async-start(), calls=%async_computation.6 | async-start | bytes 2359296 | tf_op jit(solution)/shard_map/all_gather | solution.py:133
  262.1 1.6 copy-start.2
  274.0 17.3 %copy-start.4 = (bf16[512,256]{1,0:T(8,128)(2,1)S(1)}, bf16[512,256]{1,0:T(8,128)(2,1)}, u32[]{:S(2)}) copy-start(bf16[512,256]{1,0:T(8,128)(2,1)} %fusion.2) | copy-start | bytes 786436
  339.2 1.6 copy-start.3
  351.1 17.3 %copy-start.6 = (bf16[512,256]{1,0:T(8,128)(2,1)S(1)}, bf16[512,256]{1,0:T(8,128)(2,1)}, u32[]{:S(2)}) copy-start(bf16[512,256]{1,0:T(8,128)(2,1)} %fusion.3) | copy-start | bytes 786436
Sparse Core Ops, SparseCore 0:
  9.5 52.0 all-gather.8
  63.7 97.7 all-gather.6
  213.4 48.6 all-gather.10
  292.3 46.8 all-gather.12

commit v2 on v0

v2 whole, which is shorter than its diff:
```python
import functools

import jax
import jax.numpy as jnp
from jax import lax
from jax.experimental import pallas as pl
from jax.experimental.pallas import tpu as pltpu
from jax.sharding import PartitionSpec as P

TILE = 128
VMEM_LIMIT = 40 * 2**20
center = 1.0
spread = 2.5


def routes(count):
    found, depth = [], {0: 0}

    def add(mask, source, step):
        depth[mask] = depth[source] + 1
        found.append((mask, source, step))

    for k in sorted(range(1, count // 2), key=lambda k: (k & (k + 1)) != 0):
        full = (1 << k.bit_length()) - 1
        add(2 * k, 0 if k == full else 2 * full, 2 * k if k == full else 2 * (full ^ k))
    if count > 1:
        add(1, 0, 1)
    for k in sorted(range(1, count // 2), key=lambda k: (k & (k + 1)) != 0):
        full = (1 << k.bit_length()) - 1
        add(2 * k + 1, 2 * k if k == full else 2 * full + 1, 1 if k == full else 2 * (full ^ k))
    return sorted(found, key=lambda route: depth[route[0]]), depth


def swap(array, axis, mask):
    return lax.ppermute(array, axis, [(i, i ^ mask) for i in range(lax.axis_size(axis))])


def spread_out(array):
    pieces = {0: array}
    for mask, source, step in routes(lax.axis_size("row"))[0]:
        pieces[mask] = swap(pieces[source], "row", step)
    return pieces


def rows_kernel(listed, masks, batches, first_call, last_call, where_ref, tiles_ref, *refs):
    values_refs, (potential_ref, start_ref), (out_ref, total) = (
        refs[: len(masks)],
        refs[len(masks) : len(masks) + 2],
        refs[len(masks) + 2 :],
    )
    target = total if last_call else out_ref
    target[...] = start_ref[...].astype(jnp.float32)
    per_shard = start_ref.shape[0] // TILE
    first = where_ref[1] * per_shard

    for values_ref, mask in zip(values_refs, masks):

        def one_batch(b, carry, values_ref=values_ref, mask=mask):
            number = mask * batches + b
            spots = [tiles_ref[number * listed + i] for i in range(listed)]
            owned = [(s >= first) & (s < first + per_shard) for s in spots]

            @pl.when(functools.reduce(jnp.logical_or, owned))
            def _():
                values = values_ref[b]
                lane = lax.broadcasted_iota(jnp.int32, potential_ref.shape, 1)
                potential = jnp.sum(
                    jnp.where(lane == number, potential_ref[...], 0.0), axis=1, keepdims=True
                )
                weighted = (potential * values.astype(jnp.float32)).astype(jnp.bfloat16)
                for i in range(listed):

                    @pl.when(owned[i])
                    def _(i=i):
                        strip = lax.dot_general(
                            values[:, i * TILE : (i + 1) * TILE],
                            weighted,
                            (((0,), (0,)), ((), ())),
                            preferred_element_type=jnp.float32,
                        )
                        rows = pl.ds(pl.multiple_of((spots[i] - first) * TILE, TILE), TILE)
                        for j in range(listed):
                            columns = pl.ds(pl.multiple_of(spots[j] * TILE, TILE), TILE)
                            target[rows, columns] += strip[:, j * TILE : (j + 1) * TILE]

            return carry

        lax.fori_loop(0, batches, one_batch, 0)
    if last_call:
        out_ref[...] = total[...].astype(jnp.bfloat16)


def add_rows(where, tiles, pieces, masks, potential, start, shard_rows, first_call, last_call):
    batches, points, length = pieces[0].shape
    listed = length // TILE
    width = start.shape[1]
    whole = pl.BlockSpec((batches, points, length), lambda i, w, t: (0, 0, 0))
    return pl.pallas_call(
        functools.partial(rows_kernel, listed, masks, batches, first_call, last_call),
        out_shape=jax.ShapeDtypeStruct((shard_rows, width), jnp.bfloat16 if last_call else jnp.float32),
        grid_spec=pltpu.PrefetchScalarGridSpec(
            num_scalar_prefetch=2,
            grid=(1,),
            in_specs=[whole for _ in masks]
            + [
                pl.BlockSpec(potential.shape, lambda i, w, t: (0, 0)),
                pl.BlockSpec(
                    (shard_rows, width),
                    (lambda i, w, t: (w[0], 0)) if first_call else (lambda i, w, t: (0, 0)),
                ),
            ],
            out_specs=pl.BlockSpec((shard_rows, width), lambda i, w, t: (0, 0)),
            scratch_shapes=[
                pltpu.VMEM((shard_rows, width) if last_call else (8, TILE), jnp.float32)
            ],
        ),
        compiler_params=pltpu.CompilerParams(vmem_limit_bytes=VMEM_LIMIT),
        cost_estimate=pl.CostEstimate(
            flops=len(masks) * batches * 2 * points * length * TILE,
            bytes_accessed=len(masks) * pieces[0].size * 2 + shard_rows * width * 8,
            transcendentals=0,
        ),
    )(where, tiles, *pieces, potential, start)


def early_kernel(count, where_ref, *refs):
    out_ref = refs[-1]
    total = jnp.dot(refs[0][...], refs[count][...], preferred_element_type=jnp.float32)
    for i in range(1, count):
        total += jnp.dot(refs[i][...], refs[count + i][...], preferred_element_type=jnp.float32)
    out_ref[0] = total


def early_product(where, kinetic, pieces, masks, partners):
    shard_rows, count = pieces[0].shape
    return pl.pallas_call(
        functools.partial(early_kernel, len(masks)),
        out_shape=jax.ShapeDtypeStruct((partners, shard_rows, count), jnp.float32),
        grid_spec=pltpu.PrefetchScalarGridSpec(
            num_scalar_prefetch=1,
            grid=(partners,),
            in_specs=[
                pl.BlockSpec(
                    (shard_rows, shard_rows),
                    lambda s, w, mask=mask: (w[0] ^ (s + 1), w[1] ^ mask),
                )
                for mask in masks
            ]
            + [pl.BlockSpec((shard_rows, count), lambda s, w: (0, 0)) for _ in masks],
            out_specs=pl.BlockSpec((1, shard_rows, count), lambda s, w: (s, 0, 0)),
        ),
        compiler_params=pltpu.CompilerParams(vmem_limit_bytes=VMEM_LIMIT),
        cost_estimate=pl.CostEstimate(
            flops=2 * partners * shard_rows * shard_rows * len(masks) * count,
            bytes_accessed=2 * partners * shard_rows * shard_rows * len(masks),
            transcendentals=0,
        ),
    )(where, *[kinetic] * len(masks), *pieces)


def late_kernel(count, where_ref, *refs):
    early_ref, out_ref = refs[-2:]
    total = early_ref[0]
    for i in range(count):
        total += jnp.dot(refs[i][...], refs[count + i][...], preferred_element_type=jnp.float32)
    out_ref[...] = total.astype(jnp.bfloat16)


def late_product(where, kinetic, pieces, masks, early, partner):
    shard_rows, count = pieces[0].shape
    return pl.pallas_call(
        functools.partial(late_kernel, len(masks)),
        out_shape=jax.ShapeDtypeStruct((shard_rows, count), jnp.bfloat16),
        grid_spec=pltpu.PrefetchScalarGridSpec(
            num_scalar_prefetch=1,
            grid=(1,),
            in_specs=[
                pl.BlockSpec(
                    (shard_rows, shard_rows),
                    lambda s, w, mask=mask: (w[0] ^ partner, w[1] ^ mask),
                )
                for mask in masks
            ]
            + [pl.BlockSpec((shard_rows, count), lambda s, w: (0, 0)) for _ in masks]
            + [pl.BlockSpec((1, shard_rows, count), lambda s, w: (partner - 1, 0, 0))],
            out_specs=pl.BlockSpec((shard_rows, count), lambda s, w: (0, 0)),
        ),
        compiler_params=pltpu.CompilerParams(vmem_limit_bytes=VMEM_LIMIT),
        cost_estimate=pl.CostEstimate(
            flops=2 * shard_rows * shard_rows * len(masks) * count,
            bytes_accessed=2 * shard_rows * shard_rows * len(masks),
            transcendentals=0,
        ),
    )(where, *[kinetic] * len(masks), *pieces, early)


def own_kernel(count, where_ref, *refs):
    out_ref = refs[-1]
    total = jnp.dot(refs[0][...], refs[count][...], preferred_element_type=jnp.float32)
    for i in range(1, count):
        total += jnp.dot(refs[i][...], refs[count + i][...], preferred_element_type=jnp.float32)
    out_ref[...] = total


def own_product(where, own, pieces):
    shard_rows, count = pieces[0].shape
    masks = sorted(pieces)
    return pl.pallas_call(
        functools.partial(own_kernel, len(masks)),
        out_shape=jax.ShapeDtypeStruct((shard_rows, count), jnp.float32),
        grid_spec=pltpu.PrefetchScalarGridSpec(
            num_scalar_prefetch=1,
            grid=(1,),
            in_specs=[
                pl.BlockSpec((shard_rows, shard_rows), lambda s, w, mask=mask: (0, w[1] ^ mask))
                for mask in masks
            ]
            + [pl.BlockSpec((shard_rows, count), lambda s, w: (0, 0)) for _ in masks],
            out_specs=pl.BlockSpec((shard_rows, count), lambda s, w: (0, 0)),
        ),
        compiler_params=pltpu.CompilerParams(vmem_limit_bytes=VMEM_LIMIT),
        cost_estimate=pl.CostEstimate(
            flops=2 * shard_rows * shard_rows * len(masks) * count,
            bytes_accessed=2 * shard_rows * shard_rows * len(masks),
            transcendentals=0,
        ),
    )(where, *[own] * len(masks), *[pieces[mask] for mask in masks])


def body(grid_values, external, tiles, kinetic, orbitals):
    shard_rows, orbital_count = orbitals.shape
    batch_count, points, length = grid_values.shape
    row_count, col_count = lax.axis_size("row"), lax.axis_size("col")
    row = lax.axis_index("row")
    per_shard = shard_rows // TILE
    where = jnp.stack([lax.axis_index("col"), row]).astype(jnp.int32)
    order, depth = routes(row_count)
    masks = sorted(depth)
    soon = [mask for mask in masks if depth[mask] <= 1]
    later = [mask for mask in masks if depth[mask] > 1]

    orbital_pieces = spread_out(orbitals)
    grid_values_later, _ = lax.optimization_barrier(
        (grid_values, [orbital_pieces[mask] for mask in masks if depth[mask] <= 2])
    )
    half = batch_count // 2
    value_pieces = [spread_out(grid_values_later[:half]), spread_out(grid_values_later[half:])]

    by_mask = jnp.stack([orbital_pieces[mask] for mask in masks]).reshape(-1, TILE, orbital_count)
    slots = ((tiles // per_shard) ^ row) * per_shard + tiles % per_shard
    listed_orbitals = by_mask[slots].reshape(batch_count, length, orbital_count)
    waves = jnp.einsum(
        "bpl,blk->bpk", grid_values, listed_orbitals, preferred_element_type=jnp.float32
    )
    density = jnp.sum(waves * waves, axis=2)
    potential = external - jnp.cbrt(3.0 * density / jnp.pi)
    notes = jnp.concatenate(
        [potential, jnp.pad(tiles.astype(jnp.float32), ((0, 0), (0, TILE - tiles.shape[1])))], axis=1
    )[None]
    step = 1
    while step < row_count:
        notes = jnp.concatenate([notes, swap(notes, "row", step)], axis=0)
        step *= 2
    group_potential = notes[:, :, :points].reshape(-1, points).T
    group_tiles = notes[:, :, points : points + tiles.shape[1]].astype(jnp.int32)

    def rows_of(part, chosen, start, first_call, last_call):
        return add_rows(
            where,
            group_tiles[:, part * half : (part + 1) * half].reshape(-1),
            [value_pieces[part][mask] for mask in chosen],
            chosen,
            group_potential.reshape(points, row_count, batch_count)[
                :, :, part * half : (part + 1) * half
            ].reshape(points, -1),
            start,
            shard_rows,
            first_call,
            last_call,
        )

    def send(pieces):
        early = early_product(where, kinetic, [pieces[m] for m in soon], soon, col_count - 1)
        arrived = []
        for partner in range(col_count - 1, 0, -1):
            part = late_product(where, kinetic, [pieces[m] for m in later], later, early, partner)
            arrived.append(swap(part, "col", partner))
        return arrived

    def finish(pieces, arrived, vectors):
        reduced = own_product(where, own, pieces)
        for part in arrived:
            reduced = reduced + part.astype(jnp.float32)
        return reduced / spread - center / spread * vectors.astype(jnp.float32)

    arrived = send(orbital_pieces)
    total = rows_of(0, masks, kinetic, True, False)
    own = rows_of(1, masks, total, False, True)
    first_term = finish(orbital_pieces, arrived, orbitals).astype(jnp.bfloat16)
    first_pieces = spread_out(first_term)
    second_term = (
        2.0 * finish(first_pieces, send(first_pieces), first_term) - orbitals.astype(jnp.float32)
    ).astype(jnp.bfloat16)
    second_pieces = spread_out(second_term)
    return 2.0 * finish(second_pieces, send(second_pieces), second_term) - first_term.astype(
        jnp.float32
    )


def solution(mesh):
    return jax.shard_map(
        body,
        mesh=mesh,
        in_specs=(
            P(("row", "col"), None, None),
            P(("row", "col"), None),
            P(("row", "col"), None),
            P("row", "col"),
            P(("row", "col"), None),
        ),
        out_specs=P(("row", "col"), None),
        check_vma=False,
    )
```

time: 691 us -> 246 us (0.36)
  waiting for transfers between devices: 504 us -> 89 us
  Pallas kernels: 0 us -> 62.1 us
  starting transfers between devices: 12.9 us -> 67.9 us
  other arithmetic: 54.7 us -> 3.47 us
  local copies, waits for them, and re-layouts: 68.1 us -> 17.1 us
  matrix products: 35.6 us -> 1.87 us
  between operations: 13.6 us -> 0.36 us
    all_to_all x2 -> x0, waiting for transfers between devices: 272 us -> none  [the longest x1 272 us: body(): lax.all_to_all(outgoing.reshape(row_count, per_shard * CAP, TILE, LIST),...]
    all_gather x3 -> x0, waiting for transfers between devices: 142 us -> none  [the longest x2 99.2 us: times_ham(): return add_piece(lax.all_gather(vectors, 'row', axis=0, tiled=True))]
    reduce_scatter x3 -> x0, waiting for transfers between devices: 90.8 us -> none  [filter_step(): lax.psum_scatter(partial_value, 'col', scatter_dimension=0, tiled=True)]
    ppermute x0 -> x47, waiting for transfers between devices: none -> 89 us  [swap(): lax.ppermute(array, axis, [(i, i ^ mask) for i in range(lax.axis_size(axi...]
    ppermute x0 -> x47, starting transfers between devices: none -> 67.9 us  [swap(): lax.ppermute(array, axis, [(i, i ^ mask) for i in range(lax.axis_size(axi...]
    pallas_call x0 -> x17, Pallas kernels: none -> 62.1 us  [the longest x9 27.2 us: late_product(): pl.pallas_call(functools.partial(late_kernel, len(masks)), out_shape=jax....]
    scatter-add x1 -> x0, other arithmetic: 39.3 us -> none  [body(): summed = jnp.zeros((per_shard, group_tiles, TILE, TILE), jnp.float32).at[...]
    dot_general x4 -> x0, matrix products: 35.1 us -> none  [the longest x2 24.8 us: add_piece(): return jnp.dot(hamiltonian, piece, preferred_element_type=jnp.float32)]
  transfers between devices with their start and end apart: 8 -> 47, of which waited for: 7 -> 18; matrix products, arithmetic and copies ran while one was open for 4% -> 7% of each run, Pallas kernels for 0% -> 23%
where the time goes in v2:
time: 246 us; the launch traced here: 242 us
  waiting for transfers between devices  89 us (36%)
  starting transfers between devices  67.9 us (28%)
  Pallas kernels  62.1 us (25%)
  local copies, waits for them, and re-layouts  17.1 us (7%)
  other arithmetic  3.47 us (1%)
    ppermute x47, waiting for transfers between devices, swap(): lax.ppermute(array, axis, [(i, i ^ mask) for i in range(lax.axis_size(axi...  89 us
    ppermute x47, starting transfers between devices, swap(): lax.ppermute(array, axis, [(i, i ^ mask) for i in range(lax.axis_size(axi...  67.9 us
    pallas_call x9, Pallas kernels, late_product(): pl.pallas_call(functools.partial(late_kernel, len(masks)), out_shape=jax....  27.2 us
    pallas_call x3, Pallas kernels, early_product(): pl.pallas_call(functools.partial(early_kernel, len(masks)), out_shape=jax...  15.7 us
    pallas_call x2, Pallas kernels, add_rows(): pl.pallas_call(functools.partial(rows_kernel, listed, masks, batches, fir...  13.9 us
    unnamed x23, local copies, waits for them, and re-layouts  10.1 us
    pallas_call x3, Pallas kernels, own_product(): pl.pallas_call(functools.partial(own_kernel, len(masks)), out_shape=jax.S...  5.42 us
  transfers between devices with their start and end apart: 47, of which 18 were waited for; matrix products, arithmetic and copies ran while one was open for 7% of the time, Pallas kernels for 23%

profile of v2, /device:TPU:0, one launch (start us, length us, event | category | flops | bytes accessed | tf_op | source)
XLA Modules:
  0.0 241.9 jit_solution(11693366369289372795)
XLA Ops:
  0.0 3.0 %collective-permute-start.1 = (bf16[512,256]{1,0:T(8,128)(2,1)}, bf16[512,256]{1,0:T(8,128)(2,1)S(1)}, u32[]{:S(2)}, u32[]{:S(2)}) collective-permute-start(bf16[512,256]{1,0:T(8,128)(2,1)} %refs_4_.1), channel_id=1, source_target_pairs={{0,8},{4,12},{8,0},{12,4},{16,24},{20,28},{24,16},{28,20},{1,9},{5... | collective-permute-start | bytes 786440 | tf_op jit(solution)/shard_map/ppermute | solution.py:35
  9.6 7.9 %collective-permute-done.3.refs_14_.refs_7_ = bf16[512,256]{1,0:T(8,128)(2,1)S(1)} collective-permute-done((bf16[512,256]{1,0:T(8,128)(2,1)}, bf16[512,256]{1,0:T(8,128)(2,1)S(1)}, u32[]{:S(2)}, u32[]{:S(2)}) %collective-permute-start.3) | collective-permute-done | bytes 262176 | tf_op jit(solution)/shard_map/ppermute | solution.py:35
  22.8 7.6 %collective-permute-done.2.refs_11_.refs_4_ = bf16[512,256]{1,0:T(8,128)(2,1)S(1)} collective-permute-done((bf16[512,256]{1,0:T(8,128)(2,1)S(1)}, bf16[512,256]{1,0:T(8,128)(2,1)S(1)}, u32[]{:S(2)}, u32[]{:S(2)}) %collective-permute-start.2) | collective-permute-done | bytes 262176 | tf_op jit(solution)/shard_map/ppermute | solution.py:35
  30.5 3.5 %collective-permute-start.20 = (bf16[2,256,384]{2,1,0:T(8,128)(2,1)S(1)}, bf16[2,256,384]{2,1,0:T(8,128)(2,1)S(1)}, u32[]{:S(2)}, u32[]{:S(2)}) collective-permute-start(bf16[2,256,384]{2,1,0:T(8,128)(2,1)S(1)} %get-tuple-element.7.refs_0_), channel_id=1, source_target_pairs={{0,24},{4,28},{8,16},{12,20},{16,8},{20,12},{24,0},{28,4},{1,25},{... | collective-permute-start | bytes 1179656 | tf_op jit(solution)/shard_map/ppermute | solution.py:35
  38.3 24.7 %collective-permute-done.6.refs_13_.refs_6_ = bf16[512,256]{1,0:T(8,128)(2,1)S(1)} collective-permute-done((bf16[512,256]{1,0:T(8,128)(2,1)S(1)}, bf16[512,256]{1,0:T(8,128)(2,1)S(1)}, u32[]{:S(2)}, u32[]{:S(2)}) %collective-permute-start.6) | collective-permute-done | bytes 262176 | tf_op jit(solution)/shard_map/ppermute | solution.py:35
  65.1 3.1 %gather_fusion = bf16[12,128,256]{2,1,0:T(8,128)(2,1)} fusion(bf16[32,128,256]{2,1,0:T(8,128)(2,1)} %bitcast.10, s32[1024]{0:T(1024)S(1)} %pad_clamp_fusion), kind=kCustom, calls=%fused_computation | custom fusion | bytes 1572912 | tf_op jit(solution)/shard_map/gather | solution.py:251
  78.2 4.3 %collective-permute-done.9 = f32[4,4,384]{2,1,0:T(4,128)S(1)} collective-permute-done((f32[4,4,384]{2,1,0:T(4,128)S(1)}, f32[4,4,384]{2,1,0:T(4,128)S(1)}, u32[]{:S(2)}, u32[]{:S(2)}) %collective-permute-start.9) | collective-permute-done | bytes 24608 | tf_op jit(solution)/shard_map/ppermute | solution.py:35
  88.1 5.3 %shard_map.58.refs_8_ = f32[3,512,256]{2,1,0:T(8,128)S(1)} custom-call(s32[2]{0:T(128)S(1)} %pad_add_fusion.where_ref, bf16[2048,4096]{1,0:T(8,128)(2,1)} %refs_3_.23, bf16[2048,4096]{1,0:T(8,128)(2,1)} %refs_3_.23, bf16[2048,4096]{1,0:T(8,128)(2,1)} %refs_3_.23, bf16[2048,4096]{1,0:T(8,128)(2,1)} %refs_3_.23, bf16[512,256]{1,0:T(8,128)(2,1)S(1)} %copy-done.1, ...), custom_call_target="tpu_custom_call" | custom-call | flops 1610612736 | bytes 6291456 | tf_op jit(solution)/shard_map/pallas_call | solution.py:136
  93.4 3.5 %shard_map.59 = bf16[512,256]{1,0:T(8,128)(2,1)} custom-call(s32[2]{0:T(128)S(1)} %pad_add_fusion.where_ref, bf16[2048,4096]{1,0:T(8,128)(2,1)} %refs_3_.23, bf16[2048,4096]{1,0:T(8,128)(2,1)} %refs_3_.23, bf16[2048,4096]{1,0:T(8,128)(2,1)} %refs_3_.23, bf16[2048,4096]{1,0:T(8,128)(2,1)} %refs_3_.23, ...), custom_call_target="tpu_custom_call" | custom-call | flops 536870912 | bytes 2097152 | tf_op jit(solution)/shard_map/pallas_call | solution.py:171
  96.9 3.5 %shard_map.60 = bf16[512,256]{1,0:T(8,128)(2,1)} custom-call(s32[2]{0:T(128)S(1)} %pad_add_fusion.where_ref, bf16[2048,4096]{1,0:T(8,128)(2,1)} %refs_3_.23, bf16[2048,4096]{1,0:T(8,128)(2,1)} %refs_3_.23, bf16[2048,4096]{1,0:T(8,128)(2,1)} %refs_3_.23, bf16[2048,4096]{1,0:T(8,128)(2,1)} %refs_3_.23, ...), custom_call_target="tpu_custom_call" | custom-call | flops 536870912 | bytes 2097152 | tf_op jit(solution)/shard_map/pallas_call | solution.py:171
  100.4 3.5 %shard_map.61 = bf16[512,256]{1,0:T(8,128)(2,1)} custom-call(s32[2]{0:T(128)S(1)} %pad_add_fusion.where_ref, bf16[2048,4096]{1,0:T(8,128)(2,1)} %refs_3_.23, bf16[2048,4096]{1,0:T(8,128)(2,1)} %refs_3_.23, bf16[2048,4096]{1,0:T(8,128)(2,1)} %refs_3_.23, bf16[2048,4096]{1,0:T(8,128)(2,1)} %refs_3_.23, ...), custom_call_target="tpu_custom_call" | custom-call | flops 536870912 | bytes 2097152 | tf_op jit(solution)/shard_map/pallas_call | solution.py:171
  112.6 6.3 %collective-permute-done.19.refs_3_ = bf16[2,256,384]{2,1,0:T(8,128)(2,1)} collective-permute-done((bf16[2,256,384]{2,1,0:T(8,128)(2,1)}, bf16[2,256,384]{2,1,0:T(8,128)(2,1)}, u32[]{:S(2)}, u32[]{:S(2)}) %collective-permute-start.19) | collective-permute-done | bytes 393248 | tf_op jit(solution)/shard_map/ppermute | solution.py:35
  125.8 7.7 %shard_map.55.refs_9_ = f32[512,4096]{1,0:T(8,128)S(1)} custom-call(s32[2]{0:T(128)S(1)} %pad_add_fusion.where_ref, s32[48]{0:T(128)S(1)} %reshape.31.tiles_ref, bf16[2,256,384]{2,1,0:T(8,128)(2,1)S(1)} %get-tuple-element.7.refs_0_, bf16[2,256,384]{2,1,0:T(8,128)(2,1)} %collective-permute-done.17.refs_1_, ...), custom_call_target="tpu_custom_call" | custom-call | flops 402653184 | bytes 19922944 | tf_op jit(solution)/shard_map/pallas_call | solution.py:98
  133.6 3.3 %copy-done = f32[512,4096]{1,0:T(8,128)} copy-done((f32[512,4096]{1,0:T(8,128)}, f32[512,4096]{1,0:T(8,128)S(1)}, u32[]{:S(2)}) %copy-start) | copy-done | bytes 8388632
  136.9 6.1 %shard_map.56.refs_0_.refs_1_.refs_2_.refs_3_.refs_4_.refs_5_.refs_6_.refs_7_ = bf16[512,4096]{1,0:T(8,128)(2,1)S(1)} custom-call(s32[2]{0:T(128)S(1)} %pad_add_fusion.where_ref, s32[48]{0:T(128)S(1)} %reshape.27.tiles_ref, bf16[2,256,384]{2,1,0:T(8,128)(2,1)S(1)} %get-tuple-element.8.refs_0_, bf16[2,256,384]{2,1,0:T(8,128)(2,1)S(1)} %copy-done.5, ...), custom_call_target="tpu_custom_call" | custom-call | flops 402653184 | bytes 19922944 | tf_op jit(solution)/shard_map/pallas_call | solution.py:98
  146.2 3.2 %collective-permute-start.30 = (bf16[512,256]{1,0:T(8,128)(2,1)S(1)}, bf16[512,256]{1,0:T(8,128)(2,1)S(1)}, u32[]{:S(2)}, u32[]{:S(2)}) collective-permute-start(bf16[512,256]{1,0:T(8,128)(2,1)S(1)} %fusion.2.refs_8_.refs_4_), channel_id=1, source_target_pairs={{0,24},{4,28},{8,16},{12,20},{16,8},{20,12},{24,0},{28,4},{1,25},{... | collective-permute-start | bytes 786440 | tf_op jit(solution)/shard_map/ppermute | solution.py:35
  149.4 7.9 %collective-permute-done.30.refs_14_.refs_7_ = bf16[512,256]{1,0:T(8,128)(2,1)S(1)} collective-permute-done((bf16[512,256]{1,0:T(8,128)(2,1)S(1)}, bf16[512,256]{1,0:T(8,128)(2,1)S(1)}, u32[]{:S(2)}, u32[]{:S(2)}) %collective-permute-start.30) | collective-permute-done | bytes 262176 | tf_op jit(solution)/shard_map/ppermute | solution.py:35
  159.3 3.2 %collective-permute-start.31 = (bf16[512,256]{1,0:T(8,128)(2,1)S(1)}, bf16[512,256]{1,0:T(8,128)(2,1)S(1)}, u32[]{:S(2)}, u32[]{:S(2)}) collective-permute-start(bf16[512,256]{1,0:T(8,128)(2,1)S(1)} %collective-permute-done.30.refs_14_.refs_7_), channel_id=1, source_target_pairs={{0,8},{4,12},{8,0},{12,4},{16,24},{20,28},{24,16},{28,20},{1,9},{5... | collective-permute-start | bytes 786440 | tf_op jit(solution)/shard_map/ppermute | solution.py:35
  166.5 3.1 %collective-permute-start.33 = (bf16[512,256]{1,0:T(8,128)(2,1)S(1)}, bf16[512,256]{1,0:T(8,128)(2,1)S(1)}, u32[]{:S(2)}, u32[]{:S(2)}) collective-permute-start(bf16[512,256]{1,0:T(8,128)(2,1)S(1)} %collective-permute-done.32.refs_15_.refs_7_), channel_id=1, source_target_pairs={{0,8},{4,12},{8,0},{12,4},{16,24},{20,28},{24,16},{28,20},{1,9},{5... | collective-permute-start | bytes 786440 | tf_op jit(solution)/shard_map/ppermute | solution.py:35
  172.1 5.3 %shard_map.63.refs_8_ = f32[3,512,256]{2,1,0:T(8,128)S(1)} custom-call(s32[2]{0:T(128)S(1)} %pad_add_fusion.where_ref, bf16[2048,4096]{1,0:T(8,128)(2,1)} %refs_3_.23, bf16[2048,4096]{1,0:T(8,128)(2,1)} %refs_3_.23, bf16[2048,4096]{1,0:T(8,128)(2,1)} %refs_3_.23, bf16[2048,4096]{1,0:T(8,128)(2,1)} %refs_3_.23, bf16[512,256]{1,0:T(8,128)(2,1)S(1)} %fusion.2.refs_8_.refs_4_, ...), custom_call_target="tpu_custom_call" | custom-call | flops 1610612736 | bytes 6291456 | tf_op jit(solution)/shard_map/pallas_call | solution.py:136
  177.6 2.8 %shard_map.64 = bf16[512,256]{1,0:T(8,128)(2,1)S(1)} custom-call(s32[2]{0:T(128)S(1)} %pad_add_fusion.where_ref, bf16[2048,4096]{1,0:T(8,128)(2,1)} %refs_3_.23, bf16[2048,4096]{1,0:T(8,128)(2,1)} %refs_3_.23, bf16[2048,4096]{1,0:T(8,128)(2,1)} %refs_3_.23, bf16[2048,4096]{1,0:T(8,128)(2,1)} %refs_3_.23, ...), custom_call_target="tpu_custom_call" | custom-call | flops 536870912 | bytes 2097152 | tf_op jit(solution)/shard_map/pallas_call | solution.py:171
  180.4 2.8 %shard_map.65 = bf16[512,256]{1,0:T(8,128)(2,1)S(1)} custom-call(s32[2]{0:T(128)S(1)} %pad_add_fusion.where_ref, bf16[2048,4096]{1,0:T(8,128)(2,1)} %refs_3_.23, bf16[2048,4096]{1,0:T(8,128)(2,1)} %refs_3_.23, bf16[2048,4096]{1,0:T(8,128)(2,1)} %refs_3_.23, bf16[2048,4096]{1,0:T(8,128)(2,1)} %refs_3_.23, ...), custom_call_target="tpu_custom_call" | custom-call | flops 536870912 | bytes 2097152 | tf_op jit(solution)/shard_map/pallas_call | solution.py:171
  185.7 2.8 %shard_map.66 = bf16[512,256]{1,0:T(8,128)(2,1)S(1)} custom-call(s32[2]{0:T(128)S(1)} %pad_add_fusion.where_ref, bf16[2048,4096]{1,0:T(8,128)(2,1)} %refs_3_.23, bf16[2048,4096]{1,0:T(8,128)(2,1)} %refs_3_.23, bf16[2048,4096]{1,0:T(8,128)(2,1)} %refs_3_.23, bf16[2048,4096]{1,0:T(8,128)(2,1)} %refs_3_.23, ...), custom_call_target="tpu_custom_call" | custom-call | flops 536870912 | bytes 2097152 | tf_op jit(solution)/shard_map/pallas_call | solution.py:171
  190.5 4.2 %collective-permute-done.35 = bf16[512,256]{1,0:T(8,128)(2,1)S(1)} collective-permute-done((bf16[512,256]{1,0:T(8,128)(2,1)S(1)}, bf16[512,256]{1,0:T(8,128)(2,1)S(1)}, u32[]{:S(2)}, u32[]{:S(2)}) %collective-permute-start.35) | collective-permute-done | bytes 262176 | tf_op jit(solution)/shard_map/ppermute | solution.py:35
  194.9 3.0 %collective-permute-start.40 = (bf16[512,256]{1,0:T(8,128)(2,1)S(1)}, bf16[512,256]{1,0:T(8,128)(2,1)S(1)}, u32[]{:S(2)}, u32[]{:S(2)}) collective-permute-start(bf16[512,256]{1,0:T(8,128)(2,1)S(1)} %fusion.3.refs_8_.refs_4_), channel_id=1, source_target_pairs={{0,24},{4,28},{8,16},{12,20},{16,8},{20,12},{24,0},{28,4},{1,25},{... | collective-permute-start | bytes 786440 | tf_op jit(solution)/shard_map/ppermute | solution.py:35
  197.9 8.1 %collective-permute-done.40.refs_14_.refs_7_ = bf16[512,256]{1,0:T(8,128)(2,1)S(1)} collective-permute-done((bf16[512,256]{1,0:T(8,128)(2,1)S(1)}, bf16[512,256]{1,0:T(8,128)(2,1)S(1)}, u32[]{:S(2)}, u32[]{:S(2)}) %collective-permute-start.40) | collective-permute-done | bytes 262176 | tf_op jit(solution)/shard_map/ppermute | solution.py:35
  208.0 4.6 %collective-permute-start.41 = (bf16[512,256]{1,0:T(8,128)(2,1)S(1)}, bf16[512,256]{1,0:T(8,128)(2,1)S(1)}, u32[]{:S(2)}, u32[]{:S(2)}) collective-permute-start(bf16[512,256]{1,0:T(8,128)(2,1)S(1)} %collective-permute-done.40.refs_14_.refs_7_), channel_id=1, source_target_pairs={{0,8},{4,12},{8,0},{12,4},{16,24},{20,28},{24,16},{28,20},{1,9},{5... | collective-permute-start | bytes 786440 | tf_op jit(solution)/shard_map/ppermute | solution.py:35
  215.3 4.6 %collective-permute-start.43 = (bf16[512,256]{1,0:T(8,128)(2,1)S(1)}, bf16[512,256]{1,0:T(8,128)(2,1)S(1)}, u32[]{:S(2)}, u32[]{:S(2)}) collective-permute-start(bf16[512,256]{1,0:T(8,128)(2,1)S(1)} %collective-permute-done.42.refs_15_.refs_7_), channel_id=1, source_target_pairs={{0,8},{4,12},{8,0},{12,4},{16,24},{20,28},{24,16},{28,20},{1,9},{5... | collective-permute-start | bytes 786440 | tf_op jit(solution)/shard_map/ppermute | solution.py:35
  220.7 5.1 %shard_map.68.refs_8_ = f32[3,512,256]{2,1,0:T(8,128)S(1)} custom-call(s32[2]{0:T(128)S(1)} %pad_add_fusion.where_ref, bf16[2048,4096]{1,0:T(8,128)(2,1)} %refs_3_.23, bf16[2048,4096]{1,0:T(8,128)(2,1)} %refs_3_.23, bf16[2048,4096]{1,0:T(8,128)(2,1)} %refs_3_.23, bf16[2048,4096]{1,0:T(8,128)(2,1)} %refs_3_.23, bf16[512,256]{1,0:T(8,128)(2,1)S(1)} %fusion.3.refs_8_.refs_4_, ...), custom_call_target="tpu_custom_call" | custom-call | flops 1610612736 | bytes 6291456 | tf_op jit(solution)/shard_map/pallas_call | solution.py:136
  225.8 2.8 %shard_map.69 = bf16[512,256]{1,0:T(8,128)(2,1)S(1)} custom-call(s32[2]{0:T(128)S(1)} %pad_add_fusion.where_ref, bf16[2048,4096]{1,0:T(8,128)(2,1)} %refs_3_.23, bf16[2048,4096]{1,0:T(8,128)(2,1)} %refs_3_.23, bf16[2048,4096]{1,0:T(8,128)(2,1)} %refs_3_.23, bf16[2048,4096]{1,0:T(8,128)(2,1)} %refs_3_.23, ...), custom_call_target="tpu_custom_call" | custom-call | flops 536870912 | bytes 2097152 | tf_op jit(solution)/shard_map/pallas_call | solution.py:171
  228.7 2.8 %shard_map.70 = bf16[512,256]{1,0:T(8,128)(2,1)S(1)} custom-call(s32[2]{0:T(128)S(1)} %pad_add_fusion.where_ref, bf16[2048,4096]{1,0:T(8,128)(2,1)} %refs_3_.23, bf16[2048,4096]{1,0:T(8,128)(2,1)} %refs_3_.23, bf16[2048,4096]{1,0:T(8,128)(2,1)} %refs_3_.23, bf16[2048,4096]{1,0:T(8,128)(2,1)} %refs_3_.23, ...), custom_call_target="tpu_custom_call" | custom-call | flops 536870912 | bytes 2097152 | tf_op jit(solution)/shard_map/pallas_call | solution.py:171
  238.0 2.8 %collective-permute-done.45 = bf16[512,256]{1,0:T(8,128)(2,1)S(1)} collective-permute-done((bf16[512,256]{1,0:T(8,128)(2,1)S(1)}, bf16[512,256]{1,0:T(8,128)(2,1)S(1)}, u32[]{:S(2)}, u32[]{:S(2)}) %collective-permute-start.45) | collective-permute-done | bytes 262176 | tf_op jit(solution)/shard_map/ppermute | solution.py:35
  (129 shorter events, 79.2 us)
Async XLA Ops:
  0.0 19.8 %collective-permute-start.1 = (bf16[512,256]{1,0:T(8,128)(2,1)}, bf16[512,256]{1,0:T(8,128)(2,1)S(1)}, u32[]{:S(2)}, u32[]{:S(2)}) collective-permute-start(bf16[512,256]{1,0:T(8,128)(2,1)} %refs_4_.1), channel_id=1, source_target_pairs={{0,8},{4,12},{8,0},{12,4},{16,24},{20,28},{24,16},{28,20},{1,9},{5... | collective-permute-start | bytes 786440 | tf_op jit(solution)/shard_map/ppermute | solution.py:35
  3.0 18.3 %collective-permute-start = (bf16[512,256]{1,0:T(8,128)(2,1)}, bf16[512,256]{1,0:T(8,128)(2,1)S(1)}, u32[]{:S(2)}, u32[]{:S(2)}) collective-permute-start(bf16[512,256]{1,0:T(8,128)(2,1)} %refs_4_.1), channel_id=1, source_target_pairs={{0,4},{4,0},{8,12},{12,8},{16,20},{20,16},{24,28},{28,24},{1,5},{5... | collective-permute-start | bytes 786440 | tf_op jit(solution)/shard_map/ppermute | solution.py:35
  4.5 12.9 %collective-permute-start.3 = (bf16[512,256]{1,0:T(8,128)(2,1)}, bf16[512,256]{1,0:T(8,128)(2,1)S(1)}, u32[]{:S(2)}, u32[]{:S(2)}) collective-permute-start(bf16[512,256]{1,0:T(8,128)(2,1)} %refs_4_.1), channel_id=1, source_target_pairs={{0,24},{4,28},{8,16},{12,20},{16,8},{20,12},{24,0},{28,4},{1,25},{... | collective-permute-start | bytes 786440 | tf_op jit(solution)/shard_map/ppermute | solution.py:35
  17.5 12.9 %collective-permute-start.4 = (bf16[512,256]{1,0:T(8,128)(2,1)S(1)}, bf16[512,256]{1,0:T(8,128)(2,1)S(1)}, u32[]{:S(2)}, u32[]{:S(2)}) collective-permute-start(bf16[512,256]{1,0:T(8,128)(2,1)S(1)} %collective-permute-done.3.refs_14_.refs_7_), channel_id=1, source_target_pairs={{0,8},{4,12},{8,0},{12,4},{16,24},{20,28},{24,16},{28,20},{1,9},{5... | collective-permute-start | bytes 786440 | tf_op jit(solution)/shard_map/ppermute | solution.py:35
  30.5 53.9 %collective-permute-start.20 = (bf16[2,256,384]{2,1,0:T(8,128)(2,1)S(1)}, bf16[2,256,384]{2,1,0:T(8,128)(2,1)S(1)}, u32[]{:S(2)}, u32[]{:S(2)}) collective-permute-start(bf16[2,256,384]{2,1,0:T(8,128)(2,1)S(1)} %get-tuple-element.7.refs_0_), channel_id=1, source_target_pairs={{0,24},{4,28},{8,16},{12,20},{16,8},{20,12},{24,0},{28,4},{1,25},{... | collective-permute-start | bytes 1179656 | tf_op jit(solution)/shard_map/ppermute | solution.py:35
  34.0 50.4 %collective-permute-start.18 = (bf16[2,256,384]{2,1,0:T(8,128)(2,1)S(1)}, bf16[2,256,384]{2,1,0:T(8,128)(2,1)}, u32[]{:S(2)}, u32[]{:S(2)}) collective-permute-start(bf16[2,256,384]{2,1,0:T(8,128)(2,1)S(1)} %get-tuple-element.7.refs_0_), channel_id=1, source_target_pairs={{0,8},{4,12},{8,0},{12,4},{16,24},{20,28},{24,16},{28,20},{1,9},{5... | collective-permute-start | bytes 1179656 | tf_op jit(solution)/shard_map/ppermute | solution.py:35
  34.0 52.5 %collective-permute-start.17 = (bf16[2,256,384]{2,1,0:T(8,128)(2,1)S(1)}, bf16[2,256,384]{2,1,0:T(8,128)(2,1)}, u32[]{:S(2)}, u32[]{:S(2)}) collective-permute-start(bf16[2,256,384]{2,1,0:T(8,128)(2,1)S(1)} %get-tuple-element.7.refs_0_), channel_id=1, source_target_pairs={{0,4},{4,0},{8,12},{12,8},{16,20},{20,16},{24,28},{28,24},{1,5},{5... | collective-permute-start | bytes 1179656 | tf_op jit(solution)/shard_map/ppermute | solution.py:35
  34.3 52.3 %collective-permute-start.13 = (bf16[2,256,384]{2,1,0:T(8,128)(2,1)S(1)}, bf16[2,256,384]{2,1,0:T(8,128)(2,1)}, u32[]{:S(2)}, u32[]{:S(2)}) collective-permute-start(bf16[2,256,384]{2,1,0:T(8,128)(2,1)S(1)} %get-tuple-element.8.refs_0_), channel_id=1, source_target_pairs={{0,24},{4,28},{8,16},{12,20},{16,8},{20,12},{24,0},{28,4},{1,25},{... | collective-permute-start | bytes 1179656 | tf_op jit(solution)/shard_map/ppermute | solution.py:35
  36.5 26.4 %collective-permute-start.6 = (bf16[512,256]{1,0:T(8,128)(2,1)S(1)}, bf16[512,256]{1,0:T(8,128)(2,1)S(1)}, u32[]{:S(2)}, u32[]{:S(2)}) collective-permute-start(bf16[512,256]{1,0:T(8,128)(2,1)S(1)} %collective-permute-done.5.refs_15_.refs_7_), channel_id=1, source_target_pairs={{0,8},{4,12},{8,0},{12,4},{16,24},{20,28},{24,16},{28,20},{1,9},{5... | collective-permute-start | bytes 786440 | tf_op jit(solution)/shard_map/ppermute | solution.py:35
  82.5 21.4 %collective-permute-start.11 = (bf16[2,256,384]{2,1,0:T(8,128)(2,1)S(1)}, bf16[2,256,384]{2,1,0:T(8,128)(2,1)S(1)}, u32[]{:S(2)}, u32[]{:S(2)}) collective-permute-start(bf16[2,256,384]{2,1,0:T(8,128)(2,1)S(1)} %get-tuple-element.8.refs_0_), channel_id=1, source_target_pairs={{0,8},{4,12},{8,0},{12,4},{16,24},{20,28},{24,16},{28,20},{1,9},{5... | collective-permute-start | bytes 1179656 | tf_op jit(solution)/shard_map/ppermute | solution.py:35
  84.4 20.0 %collective-permute-start.10 = (bf16[2,256,384]{2,1,0:T(8,128)(2,1)S(1)}, bf16[2,256,384]{2,1,0:T(8,128)(2,1)S(1)}, u32[]{:S(2)}, u32[]{:S(2)}) collective-permute-start(bf16[2,256,384]{2,1,0:T(8,128)(2,1)S(1)} %get-tuple-element.8.refs_0_), channel_id=1, source_target_pairs={{0,4},{4,0},{8,12},{12,8},{16,20},{20,16},{24,28},{28,24},{1,5},{5... | collective-permute-start | bytes 1179656 | tf_op jit(solution)/shard_map/ppermute | solution.py:35
  84.4 22.7 %collective-permute-start.22 = (bf16[2,256,384]{2,1,0:T(8,128)(2,1)S(1)}, bf16[2,256,384]{2,1,0:T(8,128)(2,1)}, u32[]{:S(2)}, u32[]{:S(2)}) collective-permute-start(bf16[2,256,384]{2,1,0:T(8,128)(2,1)S(1)} %collective-permute-done.20.refs_6_), channel_id=1, source_target_pairs={{0,4},{4,0},{8,12},{12,8},{16,20},{20,16},{24,28},{28,24},{1,5},{5... | collective-permute-start | bytes 1179656 | tf_op jit(solution)/shard_map/ppermute | solution.py:35
  86.5 20.7 %collective-permute-start.21 = (bf16[2,256,384]{2,1,0:T(8,128)(2,1)S(1)}, bf16[2,256,384]{2,1,0:T(8,128)(2,1)}, u32[]{:S(2)}, u32[]{:S(2)}) collective-permute-start(bf16[2,256,384]{2,1,0:T(8,128)(2,1)S(1)} %collective-permute-done.20.refs_6_), channel_id=1, source_target_pairs={{0,8},{4,12},{8,0},{12,4},{16,24},{20,28},{24,16},{28,20},{1,9},{5... | collective-permute-start | bytes 1179656 | tf_op jit(solution)/shard_map/ppermute | solution.py:35
  86.6 24.3 %collective-permute-start.15 = (bf16[2,256,384]{2,1,0:T(8,128)(2,1)}, bf16[2,256,384]{2,1,0:T(8,128)(2,1)}, u32[]{:S(2)}, u32[]{:S(2)}) collective-permute-start(bf16[2,256,384]{2,1,0:T(8,128)(2,1)} %collective-permute-done.13.refs_6_), channel_id=1, source_target_pairs={{0,4},{4,0},{8,12},{12,8},{16,20},{20,16},{24,28},{28,24},{1,5},{5... | collective-permute-start | bytes 1179656 | tf_op jit(solution)/shard_map/ppermute | solution.py:35
  103.9 15.0 %collective-permute-start.14 = (bf16[2,256,384]{2,1,0:T(8,128)(2,1)}, bf16[2,256,384]{2,1,0:T(8,128)(2,1)}, u32[]{:S(2)}, u32[]{:S(2)}) collective-permute-start(bf16[2,256,384]{2,1,0:T(8,128)(2,1)} %collective-permute-done.13.refs_6_), channel_id=1, source_target_pairs={{0,8},{4,12},{8,0},{12,4},{16,24},{20,28},{24,16},{28,20},{1,9},{5... | collective-permute-start | bytes 1179656 | tf_op jit(solution)/shard_map/ppermute | solution.py:35
  105.1 13.8 %collective-permute-start.19 = (bf16[2,256,384]{2,1,0:T(8,128)(2,1)}, bf16[2,256,384]{2,1,0:T(8,128)(2,1)}, u32[]{:S(2)}, u32[]{:S(2)}) collective-permute-start(bf16[2,256,384]{2,1,0:T(8,128)(2,1)} %collective-permute-done.18.refs_2_), channel_id=1, source_target_pairs={{0,4},{4,0},{8,12},{12,8},{16,20},{20,16},{24,28},{28,24},{1,5},{5... | collective-permute-start | bytes 1179656 | tf_op jit(solution)/shard_map/ppermute | solution.py:35
  107.0 15.7 %collective-permute-start.23 = (bf16[2,256,384]{2,1,0:T(8,128)(2,1)}, bf16[2,256,384]{2,1,0:T(8,128)(2,1)}, u32[]{:S(2)}, u32[]{:S(2)}) collective-permute-start(bf16[2,256,384]{2,1,0:T(8,128)(2,1)} %collective-permute-done.22.refs_7_), channel_id=1, source_target_pairs={{0,8},{4,12},{8,0},{12,4},{16,24},{20,28},{24,16},{28,20},{1,9},{5... | collective-permute-start | bytes 1179656 | tf_op jit(solution)/shard_map/ppermute | solution.py:35
  107.2 29.6 %collective-permute-start.12 = (bf16[2,256,384]{2,1,0:T(8,128)(2,1)}, bf16[2,256,384]{2,1,0:T(8,128)(2,1)}, u32[]{:S(2)}, u32[]{:S(2)}) collective-permute-start(bf16[2,256,384]{2,1,0:T(8,128)(2,1)} %copy-done.2), channel_id=1, source_target_pairs={{0,4},{4,0},{8,12},{12,8},{16,20},{20,16},{24,28},{28,24},{1,5},{5... | collective-permute-start | bytes 1179656 | tf_op jit(solution)/shard_map/ppermute | solution.py:35
  110.9 26.0 %collective-permute-start.16 = (bf16[2,256,384]{2,1,0:T(8,128)(2,1)}, bf16[2,256,384]{2,1,0:T(8,128)(2,1)}, u32[]{:S(2)}, u32[]{:S(2)}) collective-permute-start(bf16[2,256,384]{2,1,0:T(8,128)(2,1)} %collective-permute-done.15.refs_7_), channel_id=1, source_target_pairs={{0,8},{4,12},{8,0},{12,4},{16,24},{20,28},{24,16},{28,20},{1,9},{5... | collective-permute-start | bytes 1179656 | tf_op jit(solution)/shard_map/ppermute | solution.py:35
  118.9 26.0 %collective-permute-start.24 = (bf16[512,256]{1,0:T(8,128)(2,1)}, bf16[512,256]{1,0:T(8,128)(2,1)}, u32[]{:S(2)}, u32[]{:S(2)}) collective-permute-start(bf16[512,256]{1,0:T(8,128)(2,1)} %shard_map.59), channel_id=1, source_target_pairs={{0,3},{1,2},{2,1},{3,0},{4,7},{5,6},{6,5},{7,4},{8,11},{9,10},{10,... | collective-permute-start | bytes 786440 | tf_op jit(solution)/shard_map/ppermute | solution.py:35
  118.9 26.0 %collective-permute-start.25 = (bf16[512,256]{1,0:T(8,128)(2,1)}, bf16[512,256]{1,0:T(8,128)(2,1)}, u32[]{:S(2)}, u32[]{:S(2)}) collective-permute-start(bf16[512,256]{1,0:T(8,128)(2,1)} %shard_map.60), channel_id=1, source_target_pairs={{0,2},{1,3},{2,0},{3,1},{4,6},{5,7},{6,4},{7,5},{8,10},{9,11},{10,... | collective-permute-start | bytes 786440 | tf_op jit(solution)/shard_map/ppermute | solution.py:35
  122.8 22.1 %collective-permute-start.26 = (bf16[512,256]{1,0:T(8,128)(2,1)}, bf16[512,256]{1,0:T(8,128)(2,1)}, u32[]{:S(2)}, u32[]{:S(2)}) collective-permute-start(bf16[512,256]{1,0:T(8,128)(2,1)} %shard_map.61), channel_id=1, source_target_pairs={{0,1},{1,0},{2,3},{3,2},{4,5},{5,4},{6,7},{7,6},{8,9},{9,8},{10,11... | collective-permute-start | bytes 786440 | tf_op jit(solution)/shard_map/ppermute | solution.py:35
  149.4 13.1 %collective-permute-start.28 = (bf16[512,256]{1,0:T(8,128)(2,1)S(1)}, bf16[512,256]{1,0:T(8,128)(2,1)S(1)}, u32[]{:S(2)}, u32[]{:S(2)}) collective-permute-start(bf16[512,256]{1,0:T(8,128)(2,1)S(1)} %fusion.2.refs_8_.refs_4_), channel_id=1, source_target_pairs={{0,8},{4,12},{8,0},{12,4},{16,24},{20,28},{24,16},{28,20},{1,9},{5... | collective-permute-start | bytes 786440 | tf_op jit(solution)/shard_map/ppermute | solution.py:35
  158.1 14.0 %collective-permute-start.27 = (bf16[512,256]{1,0:T(8,128)(2,1)S(1)}, bf16[512,256]{1,0:T(8,128)(2,1)S(1)}, u32[]{:S(2)}, u32[]{:S(2)}) collective-permute-start(bf16[512,256]{1,0:T(8,128)(2,1)S(1)} %fusion.2.refs_8_.refs_4_), channel_id=1, source_target_pairs={{0,4},{4,0},{8,12},{12,8},{16,20},{20,16},{24,28},{28,24},{1,5},{5... | collective-permute-start | bytes 786440 | tf_op jit(solution)/shard_map/ppermute | solution.py:35
  159.3 18.2 %collective-permute-start.31 = (bf16[512,256]{1,0:T(8,128)(2,1)S(1)}, bf16[512,256]{1,0:T(8,128)(2,1)S(1)}, u32[]{:S(2)}, u32[]{:S(2)}) collective-permute-start(bf16[512,256]{1,0:T(8,128)(2,1)S(1)} %collective-permute-done.30.refs_14_.refs_7_), channel_id=1, source_target_pairs={{0,8},{4,12},{8,0},{12,4},{16,24},{20,28},{24,16},{28,20},{1,9},{5... | collective-permute-start | bytes 786440 | tf_op jit(solution)/shard_map/ppermute | solution.py:35
  162.5 15.1 %collective-permute-start.29 = (bf16[512,256]{1,0:T(8,128)(2,1)S(1)}, bf16[512,256]{1,0:T(8,128)(2,1)S(1)}, u32[]{:S(2)}, u32[]{:S(2)}) collective-permute-start(bf16[512,256]{1,0:T(8,128)(2,1)S(1)} %collective-permute-done.28.refs_10_.refs_6_), channel_id=1, source_target_pairs={{0,4},{4,0},{8,12},{12,8},{16,20},{20,16},{24,28},{28,24},{1,5},{5... | collective-permute-start | bytes 786440 | tf_op jit(solution)/shard_map/ppermute | solution.py:35
  183.2 11.4 %collective-permute-start.35 = (bf16[512,256]{1,0:T(8,128)(2,1)S(1)}, bf16[512,256]{1,0:T(8,128)(2,1)S(1)}, u32[]{:S(2)}, u32[]{:S(2)}) collective-permute-start(bf16[512,256]{1,0:T(8,128)(2,1)S(1)} %shard_map.65), channel_id=1, source_target_pairs={{0,2},{1,3},{2,0},{3,1},{4,6},{5,7},{6,4},{7,5},{8,10},{9,11},{10,... | collective-permute-start | bytes 786440 | tf_op jit(solution)/shard_map/ppermute | solution.py:35
  194.9 11.1 %collective-permute-start.40 = (bf16[512,256]{1,0:T(8,128)(2,1)S(1)}, bf16[512,256]{1,0:T(8,128)(2,1)S(1)}, u32[]{:S(2)}, u32[]{:S(2)}) collective-permute-start(bf16[512,256]{1,0:T(8,128)(2,1)S(1)} %fusion.3.refs_8_.refs_4_), channel_id=1, source_target_pairs={{0,24},{4,28},{8,16},{12,20},{16,8},{20,12},{24,0},{28,4},{1,25},{... | collective-permute-start | bytes 786440 | tf_op jit(solution)/shard_map/ppermute | solution.py:35
  197.8 14.9 %collective-permute-start.38 = (bf16[512,256]{1,0:T(8,128)(2,1)S(1)}, bf16[512,256]{1,0:T(8,128)(2,1)S(1)}, u32[]{:S(2)}, u32[]{:S(2)}) collective-permute-start(bf16[512,256]{1,0:T(8,128)(2,1)S(1)} %fusion.3.refs_8_.refs_4_), channel_id=1, source_target_pairs={{0,8},{4,12},{8,0},{12,4},{16,24},{20,28},{24,16},{28,20},{1,9},{5... | collective-permute-start | bytes 786440 | tf_op jit(solution)/shard_map/ppermute | solution.py:35
  206.3 14.4 %collective-permute-start.37 = (bf16[512,256]{1,0:T(8,128)(2,1)S(1)}, bf16[512,256]{1,0:T(8,128)(2,1)S(1)}, u32[]{:S(2)}, u32[]{:S(2)}) collective-permute-start(bf16[512,256]{1,0:T(8,128)(2,1)S(1)} %fusion.3.refs_8_.refs_4_), channel_id=1, source_target_pairs={{0,4},{4,0},{8,12},{12,8},{16,20},{20,16},{24,28},{28,24},{1,5},{5... | collective-permute-start | bytes 786440 | tf_op jit(solution)/shard_map/ppermute | solution.py:35
  208.0 17.7 %collective-permute-start.41 = (bf16[512,256]{1,0:T(8,128)(2,1)S(1)}, bf16[512,256]{1,0:T(8,128)(2,1)S(1)}, u32[]{:S(2)}, u32[]{:S(2)}) collective-permute-start(bf16[512,256]{1,0:T(8,128)(2,1)S(1)} %collective-permute-done.40.refs_14_.refs_7_), channel_id=1, source_target_pairs={{0,8},{4,12},{8,0},{12,4},{16,24},{20,28},{24,16},{28,20},{1,9},{5... | collective-permute-start | bytes 786440 | tf_op jit(solution)/shard_map/ppermute | solution.py:35
  212.7 13.1 %collective-permute-start.39 = (bf16[512,256]{1,0:T(8,128)(2,1)S(1)}, bf16[512,256]{1,0:T(8,128)(2,1)S(1)}, u32[]{:S(2)}, u32[]{:S(2)}) collective-permute-start(bf16[512,256]{1,0:T(8,128)(2,1)S(1)} %collective-permute-done.38.refs_10_.refs_6_), channel_id=1, source_target_pairs={{0,4},{4,0},{8,12},{12,8},{16,20},{20,16},{24,28},{28,24},{1,5},{5... | collective-permute-start | bytes 786440 | tf_op jit(solution)/shard_map/ppermute | solution.py:35
  (23 other events, 215.5 us)

commit v3 on v2

v3 whole, which is shorter than its diff:
```python
import functools

import jax
import jax.numpy as jnp
from jax import lax
from jax.experimental import pallas as pl
from jax.experimental.pallas import tpu as pltpu
from jax.sharding import PartitionSpec as P

TILE = 128
SMALL_LIMIT = 16 * 2**20
ROWS_LIMIT = 30 * 2**20
center = 1.0
spread = 2.5


def routes(count):
    found, depth = [], {0: 0}

    def add(mask, source, step):
        depth[mask] = depth[source] + 1
        found.append((mask, source, step))

    for k in sorted(range(1, count // 2), key=lambda k: (k & (k + 1)) != 0):
        full = (1 << k.bit_length()) - 1
        add(2 * k, 0 if k == full else 2 * full, 2 * k if k == full else 2 * (full ^ k))
    if count > 1:
        add(1, 0, 1)
    for k in sorted(range(1, count // 2), key=lambda k: (k & (k + 1)) != 0):
        full = (1 << k.bit_length()) - 1
        add(2 * k + 1, 2 * k if k == full else 2 * full + 1, 1 if k == full else 2 * (full ^ k))
    return sorted(found, key=lambda route: depth[route[0]]), depth


def swap(array, axis, mask):
    return lax.ppermute(array, axis, [(i, i ^ mask) for i in range(lax.axis_size(axis))])


def spread_out(array, between=None):
    order, depth = routes(lax.axis_size("row"))
    pieces, result = {0: array}, None
    for mask, source, step in order:
        outgoing = pieces[source]
        if between is not None and depth[mask] > 2:
            if result is None:
                result = between(pieces)
            outgoing, result = lax.optimization_barrier((outgoing, result))
        pieces[mask] = swap(outgoing, "row", step)
    if between is None:
        return pieces
    return pieces, between(pieces) if result is None else result


def hop(pieces, hops, after):
    order, depth = routes(lax.axis_size("row"))
    chosen = [route for route in order if depth[route[0]] == hops]
    sources = sorted({source for _, source, _ in chosen})
    held, after = lax.optimization_barrier(([pieces[source] for source in sources], after))
    held = dict(zip(sources, held))
    for mask, source, step in chosen:
        pieces[mask] = swap(held[source], "row", step)
    return after


def noted(orbitals, external, tiles):
    parts, rest = [], external
    for _ in range(3):
        part = lax.reduce_precision(rest, exponent_bits=8, mantissa_bits=7)
        parts.append(part.reshape(-1))
        rest = rest - part
    flat = jnp.concatenate(parts + [tiles.astype(jnp.float32).reshape(-1)])
    count = orbitals.shape[1]
    flat = jnp.pad(flat, (0, -flat.size % (16 * count))).astype(jnp.bfloat16)
    return jnp.concatenate([orbitals, flat.reshape(-1, count)], axis=0)


def stack_kernel(count, *refs):
    held_ref, notes_ref = refs[count:]
    rows = held_ref.shape[1]
    for i in range(count):
        held_ref[i] = refs[i][:rows]
        notes_ref[i] = refs[i][rows:].astype(jnp.float32)


def stacked(pieces, shard_rows):
    masks = sorted(pieces)
    rows, count = pieces[0].shape
    return pl.pallas_call(
        functools.partial(stack_kernel, len(masks)),
        out_shape=(
            jax.ShapeDtypeStruct((len(masks), shard_rows, count), jnp.bfloat16),
            jax.ShapeDtypeStruct((len(masks), rows - shard_rows, count), jnp.float32),
        ),
        compiler_params=pltpu.CompilerParams(vmem_limit_bytes=SMALL_LIMIT),
        cost_estimate=pl.CostEstimate(
            flops=0, bytes_accessed=4 * len(masks) * rows * count, transcendentals=0
        ),
    )(*[pieces[mask] for mask in masks])


def rows_kernel(listed, firsts, last_call, where_ref, tiles_ref, *refs):
    values_refs, (external_ref, held_ref, start_ref), (out_ref, total) = (
        refs[: len(firsts)],
        refs[len(firsts) : len(firsts) + 3],
        refs[len(firsts) + 3 :],
    )
    target = total if last_call else out_ref
    target[...] = start_ref[...].astype(jnp.float32)
    per_shard = start_ref.shape[0] // TILE
    mine = where_ref[1] * per_shard

    for values_ref, first in zip(values_refs, firsts):

        def one_batch(b, carry, values_ref=values_ref, first=first):
            spots = [tiles_ref[(first + b) * listed + i] for i in range(listed)]
            owned = [(s >= mine) & (s < mine + per_shard) for s in spots]

            @pl.when(functools.reduce(jnp.logical_or, owned))
            def _():
                values = values_ref[b]
                waves = None
                for i in range(listed):
                    orbital_rows = pl.ds(pl.multiple_of(spots[i] % per_shard * TILE, TILE), TILE)
                    part = jnp.dot(
                        values[:, i * TILE : (i + 1) * TILE],
                        held_ref[(spots[i] // per_shard) ^ where_ref[1], orbital_rows, :],
                        preferred_element_type=jnp.float32,
                    )
                    waves = part if waves is None else waves + part
                lifted = jnp.sum(waves * waves, axis=1, keepdims=True) * (3.0 / jnp.pi)
                root = jnp.where(lifted > 0.0, jnp.exp(jnp.log(lifted) * (1.0 / 3.0)), 0.0)
                lane = lax.broadcasted_iota(jnp.int32, external_ref.shape, 1)
                external = jnp.sum(
                    jnp.where(lane == first + b, external_ref[...], 0.0), axis=1, keepdims=True
                )
                potential = external - root
                weighted = (potential * values.astype(jnp.float32)).astype(jnp.bfloat16)
                for i in range(listed):

                    @pl.when(owned[i])
                    def _(i=i):
                        strip = lax.dot_general(
                            values[:, i * TILE : (i + 1) * TILE],
                            weighted,
                            (((0,), (0,)), ((), ())),
                            preferred_element_type=jnp.float32,
                        )
                        rows = pl.ds(pl.multiple_of((spots[i] - mine) * TILE, TILE), TILE)
                        for j in range(listed):
                            columns = pl.ds(pl.multiple_of(spots[j] * TILE, TILE), TILE)
                            target[rows, columns] += strip[:, j * TILE : (j + 1) * TILE]

            return carry

        lax.fori_loop(0, values_ref.shape[0], one_batch, 0)
    if last_call:
        out_ref[...] = total[...].astype(jnp.bfloat16)


def add_rows(
    where, tiles, pieces, firsts, external, held, start, shard_rows, first_call, last_call
):
    batches, points, length = pieces[0].shape
    listed = length // TILE
    width = start.shape[1]
    once = pl.Buffered(1)
    whole = pl.BlockSpec(
        (batches, points, length), lambda i, w, t: (0, 0, 0), pipeline_mode=once
    )
    return pl.pallas_call(
        functools.partial(rows_kernel, listed, firsts, last_call),
        out_shape=jax.ShapeDtypeStruct((shard_rows, width), jnp.bfloat16 if last_call else jnp.float32),
        grid_spec=pltpu.PrefetchScalarGridSpec(
            num_scalar_prefetch=2,
            grid=(1,),
            in_specs=[whole for _ in firsts]
            + [
                pl.BlockSpec(external.shape, lambda i, w, t: (0, 0)),
                pl.BlockSpec(held.shape, lambda i, w, t: (0, 0, 0), pipeline_mode=once),
                pl.BlockSpec(
                    (shard_rows, width),
                    (lambda i, w, t: (w[0], 0)) if first_call else (lambda i, w, t: (0, 0)),
                    pipeline_mode=once,
                ),
            ],
            out_specs=pl.BlockSpec((shard_rows, width), lambda i, w, t: (0, 0), pipeline_mode=once),
            scratch_shapes=[
                pltpu.VMEM((shard_rows, width) if last_call else (8, TILE), jnp.float32)
            ],
        ),
        compiler_params=pltpu.CompilerParams(vmem_limit_bytes=ROWS_LIMIT),
        cost_estimate=pl.CostEstimate(
            flops=len(firsts) * batches * 2 * points * length * TILE,
            bytes_accessed=len(firsts) * pieces[0].size * 2 + shard_rows * width * 8,
            transcendentals=0,
        ),
    )(where, tiles, *pieces, external, held, start)


def early_kernel(count, where_ref, *refs):
    out_ref = refs[-1]
    total = jnp.dot(refs[0][...], refs[count][...], preferred_element_type=jnp.float32)
    for i in range(1, count):
        total += jnp.dot(refs[i][...], refs[count + i][...], preferred_element_type=jnp.float32)
    if len(refs) > 2 * count + 1:
        total += refs[2 * count][0]
    out_ref[0] = total


def early_product(where, kinetic, pieces, masks, partners, before=None):
    shard_rows, count = kinetic.shape[0] // (partners + 1), pieces[0].shape[1]
    whole = pl.BlockSpec((1, shard_rows, count), lambda s, w: (s, 0, 0))
    return pl.pallas_call(
        functools.partial(early_kernel, len(masks)),
        out_shape=jax.ShapeDtypeStruct((partners, shard_rows, count), jnp.float32),
        grid_spec=pltpu.PrefetchScalarGridSpec(
            num_scalar_prefetch=1,
            grid=(partners,),
            in_specs=[
                pl.BlockSpec(
                    (shard_rows, shard_rows),
                    lambda s, w, mask=mask: (w[0] ^ (s + 1), w[1] ^ mask),
                )
                for mask in masks
            ]
            + [pl.BlockSpec((shard_rows, count), lambda s, w: (0, 0)) for _ in masks]
            + [whole] * (before is not None),
            out_specs=whole,
        ),
        compiler_params=pltpu.CompilerParams(vmem_limit_bytes=SMALL_LIMIT),
        cost_estimate=pl.CostEstimate(
            flops=2 * partners * shard_rows * shard_rows * len(masks) * count,
            bytes_accessed=2 * partners * shard_rows * shard_rows * len(masks),
            transcendentals=0,
        ),
    )(where, *[kinetic] * len(masks), *pieces, *([] if before is None else [before]))


def late_kernel(count, where_ref, *refs):
    early_ref, out_ref = refs[-2:]
    total = early_ref[0]
    for i in range(count):
        total += jnp.dot(refs[i][...], refs[count + i][...], preferred_element_type=jnp.float32)
    out_ref[...] = total.astype(jnp.bfloat16)


def late_product(where, kinetic, pieces, masks, early, partner):
    shard_rows, count = early.shape[1:]
    return pl.pallas_call(
        functools.partial(late_kernel, len(masks)),
        out_shape=jax.ShapeDtypeStruct((shard_rows, count), jnp.bfloat16),
        grid_spec=pltpu.PrefetchScalarGridSpec(
            num_scalar_prefetch=1,
            grid=(1,),
            in_specs=[
                pl.BlockSpec(
                    (shard_rows, shard_rows),
                    lambda s, w, mask=mask: (w[0] ^ partner, w[1] ^ mask),
                )
                for mask in masks
            ]
            + [pl.BlockSpec((shard_rows, count), lambda s, w: (0, 0)) for _ in masks]
            + [pl.BlockSpec((1, shard_rows, count), lambda s, w: (partner - 1, 0, 0))],
            out_specs=pl.BlockSpec((shard_rows, count), lambda s, w: (0, 0)),
        ),
        compiler_params=pltpu.CompilerParams(vmem_limit_bytes=SMALL_LIMIT),
        cost_estimate=pl.CostEstimate(
            flops=2 * shard_rows * shard_rows * len(masks) * count,
            bytes_accessed=2 * shard_rows * shard_rows * len(masks),
            transcendentals=0,
        ),
    )(where, *[kinetic] * len(masks), *pieces, early)


def own_kernel(count, where_ref, *refs):
    out_ref = refs[-1]
    total = jnp.dot(refs[0][...], refs[count][...], preferred_element_type=jnp.float32)
    for i in range(1, count):
        total += jnp.dot(refs[i][...], refs[count + i][...], preferred_element_type=jnp.float32)
    out_ref[...] = total


def own_product(where, own, pieces):
    shard_rows, count = own.shape[0], pieces[0].shape[1]
    masks = sorted(pieces)
    return pl.pallas_call(
        functools.partial(own_kernel, len(masks)),
        out_shape=jax.ShapeDtypeStruct((shard_rows, count), jnp.float32),
        grid_spec=pltpu.PrefetchScalarGridSpec(
            num_scalar_prefetch=1,
            grid=(1,),
            in_specs=[
                pl.BlockSpec((shard_rows, shard_rows), lambda s, w, mask=mask: (0, w[1] ^ mask))
                for mask in masks
            ]
            + [pl.BlockSpec((shard_rows, count), lambda s, w: (0, 0)) for _ in masks],
            out_specs=pl.BlockSpec((shard_rows, count), lambda s, w: (0, 0)),
        ),
        compiler_params=pltpu.CompilerParams(vmem_limit_bytes=SMALL_LIMIT),
        cost_estimate=pl.CostEstimate(
            flops=2 * shard_rows * shard_rows * len(masks) * count,
            bytes_accessed=2 * shard_rows * shard_rows * len(masks),
            transcendentals=0,
        ),
    )(where, *[own] * len(masks), *[pieces[mask] for mask in masks])


def body(grid_values, external, tiles, kinetic, orbitals):
    shard_rows, orbital_count = orbitals.shape
    batch_count, points, length = grid_values.shape
    row_count, col_count = lax.axis_size("row"), lax.axis_size("col")
    row = lax.axis_index("row")
    per_shard = shard_rows // TILE
    where = jnp.stack([lax.axis_index("col"), row]).astype(jnp.int32)
    _, depth = routes(row_count)
    masks = sorted(depth)
    soon = [mask for mask in masks if depth[mask] <= 1]
    middle = [mask for mask in masks if depth[mask] == 2]
    last = [mask for mask in masks if depth[mask] > 2]

    def first_products(pieces):
        return early_product(where, kinetic, [pieces[m] for m in soon], soon, col_count - 1)

    def send(pieces, early):
        early = early_product(
            where, kinetic, [pieces[m] for m in middle], middle, col_count - 1, early
        )
        arrived = []
        for partner in range(col_count - 1, 0, -1):
            part = late_product(where, kinetic, [pieces[m] for m in last], last, early, partner)
            arrived.append(swap(part, "col", partner))
        return arrived

    orbital_pieces = spread_out(noted(orbitals, external, tiles))
    held, notes = stacked(orbital_pieces, shard_rows)
    notes = notes.reshape(row_count, -1)
    group_external = (
        notes[:, : external.size]
        + notes[:, external.size : 2 * external.size]
        + notes[:, 2 * external.size : 3 * external.size]
    )
    group_external = group_external.reshape(-1, points).T
    group_tiles = notes[:, 3 * external.size : 3 * external.size + tiles.size]
    group_tiles = group_tiles.astype(jnp.int32).reshape(-1)

    half = batch_count // 2

    def rows_of(chosen, start, first_call, last_call):
        return add_rows(
            where,
            group_tiles,
            [value_pieces[part][mask] for mask, part in chosen],
            [mask * batch_count + part * half for mask, part in chosen],
            group_external,
            held,
            start,
            shard_rows,
            first_call,
            last_call,
        )

    def finish(pieces, arrived, vectors):
        reduced = own_product(where, own, pieces)
        for part in arrived:
            reduced = reduced + part.astype(jnp.float32)
        return reduced / spread - center / spread * vectors.astype(jnp.float32)

    arrived = send(orbital_pieces, first_products(orbital_pieces))
    value_pieces = [{0: grid_values[:half]}, {0: grid_values[half:]}]
    most = max(depth.values())
    taken, total = [], kinetic

    def arrived_values():
        return [(m, p) for p in range(2) for m in sorted(value_pieces[p])]

    for turn in range(1, most + 2):
        after = [orbital_pieces, [value_pieces[p][m] for m, p in arrived_values()]]
        if turn == most:
            taken = arrived_values()
            total = rows_of(taken, kinetic, True, False)
        if turn == most + 1:
            after, total = lax.optimization_barrier((after, total))
        if turn <= most:
            after = hop(value_pieces[0], turn, after)
        if turn > 1:
            hop(value_pieces[1], turn - 1, after)
    rest = [(m, p) for p in range(2) for m in masks if (m, p) not in taken]
    own = rows_of(rest, total, False, True)
    first_term = finish(orbital_pieces, arrived, orbitals).astype(jnp.bfloat16)
    first_pieces, early = spread_out(first_term, first_products)
    second_term = (
        2.0 * finish(first_pieces, send(first_pieces, early), first_term)
        - orbitals.astype(jnp.float32)
    ).astype(jnp.bfloat16)
    second_pieces, early = spread_out(second_term, first_products)
    return 2.0 * finish(second_pieces, send(second_pieces, early), second_term) - first_term.astype(
        jnp.float32
    )


def solution(mesh):
    return jax.shard_map(
        body,
        mesh=mesh,
        in_specs=(
            P(("row", "col"), None, None),
            P(("row", "col"), None),
            P(("row", "col"), None),
            P("row", "col"),
            P(("row", "col"), None),
        ),
        out_specs=P(("row", "col"), None),
        check_vma=False,
    )
```

time: 246 us -> 220 us (0.89); the launches traced: 242 us -> 220 us
  waiting for transfers between devices: 89 us -> 67.4 us
  Pallas kernels: 62.1 us -> 46.7 us
  starting transfers between devices: 67.9 us -> 76.2 us
  local copies, waits for them, and re-layouts: 17.1 us -> 24 us
    ppermute x47 -> x44, waiting for transfers between devices: 89 us -> 67.4 us  [swap(): lax.ppermute(array, axis, [(i, i ^ mask) for i in range(lax.axis_size(axi...]
    pallas_call x9, Pallas kernels: 27.2 us -> 9.68 us  [late_product(): pl.pallas_call(functools.partial(late_kernel, len(masks)), out_shape=jax....]
    unnamed x23 -> x71, local copies, waits for them, and re-layouts: 10.1 us -> 21.9 us
    ppermute x47 -> x44, starting transfers between devices: 67.9 us -> 76.2 us  [swap(): lax.ppermute(array, axis, [(i, i ^ mask) for i in range(lax.axis_size(axi...]
    gather x1 -> x0, local copies, waits for them, and re-layouts: 3.11 us -> none  [body(): listed_orbitals = by_mask[slots].reshape(batch_count, length, orbital_count)]
    pallas_call x3 -> x6, Pallas kernels: 15.7 us -> 18 us  [early_product(): pl.pallas_call(functools.partial(early_kernel, len(masks)), out_shape=jax...]
    pallas_call x2 -> x3, Pallas kernels: 13.9 us -> 13.6 us  [the longest x2 13.5 us: add_rows(): pl.pallas_call(functools.partial(rows_kernel, listed, firsts, last_call),...]
  transfers between devices with their start and end apart: 47 -> 44, of which waited for: 18 -> 19; matrix products, arithmetic and copies ran while one was open for 7% -> 1% of each run, Pallas kernels for 23% -> 21%
where the time goes in v3:
time: 220 us
  starting transfers between devices  76.2 us (35%)
  waiting for transfers between devices  67.4 us (31%)
  Pallas kernels  46.7 us (21%)
  local copies, waits for them, and re-layouts  24 us (11%)
  other arithmetic  4.6 us (2%)
    ppermute x44, starting transfers between devices, swap(): lax.ppermute(array, axis, [(i, i ^ mask) for i in range(lax.axis_size(axi...  76.2 us
    ppermute x44, waiting for transfers between devices, swap(): lax.ppermute(array, axis, [(i, i ^ mask) for i in range(lax.axis_size(axi...  67.4 us
    unnamed x71, local copies, waits for them, and re-layouts  21.9 us
    pallas_call x6, Pallas kernels, early_product(): pl.pallas_call(functools.partial(early_kernel, len(masks)), out_shape=jax...  18 us
    pallas_call x2, Pallas kernels, add_rows(): pl.pallas_call(functools.partial(rows_kernel, listed, firsts, last_call),...  13.5 us
    pallas_call x9, Pallas kernels, late_product(): pl.pallas_call(functools.partial(late_kernel, len(masks)), out_shape=jax....  9.68 us
    pallas_call x3, Pallas kernels, own_product(): pl.pallas_call(functools.partial(own_kernel, len(masks)), out_shape=jax.S...  5.42 us
  transfers between devices with their start and end apart: 44, of which 19 were waited for; matrix products, arithmetic and copies ran while one was open for 1% of the time, Pallas kernels for 21%

profile of v3, /device:TPU:0, one launch (start us, length us, event | category | flops | bytes accessed | tf_op | source)
XLA Modules:
  0.0 219.5 jit_solution(11571410718761582952)
XLA Ops:
  2.5 5.1 %collective-permute-start.3 = (bf16[528,256]{1,0:T(8,128)(2,1)S(1)}, bf16[528,256]{1,0:T(8,128)(2,1)S(1)}, u32[]{:S(2)}, u32[]{:S(2)}) collective-permute-start(bf16[528,256]{1,0:T(8,128)(2,1)S(1)} %constant_dynamic-update-slice_fusion.refs_0_.refs_8_.refs_4_), channel_id=1, source_target_pairs={{0,24},{4,28},{8,16},{12,20},{16,8},{20,12},{24,0},{28,4},{1,25},{... | collective-permute-start | bytes 811016 | tf_op jit(solution)/shard_map/ppermute | solution.py:36
  7.6 7.4 %collective-permute-done.3.refs_6_.refs_14_.refs_7_ = bf16[528,256]{1,0:T(8,128)(2,1)S(1)} collective-permute-done((bf16[528,256]{1,0:T(8,128)(2,1)S(1)}, bf16[528,256]{1,0:T(8,128)(2,1)S(1)}, u32[]{:S(2)}, u32[]{:S(2)}) %collective-permute-start.3) | collective-permute-done | bytes 270368 | tf_op jit(solution)/shard_map/ppermute | solution.py:36
  17.0 4.6 %collective-permute-start.4 = (bf16[528,256]{1,0:T(8,128)(2,1)S(1)}, bf16[528,256]{1,0:T(8,128)(2,1)S(1)}, u32[]{:S(2)}, u32[]{:S(2)}) collective-permute-start(bf16[528,256]{1,0:T(8,128)(2,1)S(1)} %collective-permute-done.3.refs_6_.refs_14_.refs_7_), channel_id=1, source_target_pairs={{0,8},{4,12},{8,0},{12,4},{16,24},{20,28},{24,16},{28,20},{1,9},{5... | collective-permute-start | bytes 811016 | tf_op jit(solution)/shard_map/ppermute | solution.py:36
  24.4 4.6 %collective-permute-start.6 = (bf16[528,256]{1,0:T(8,128)(2,1)S(1)}, bf16[528,256]{1,0:T(8,128)(2,1)S(1)}, u32[]{:S(2)}, u32[]{:S(2)}) collective-permute-start(bf16[528,256]{1,0:T(8,128)(2,1)S(1)} %collective-permute-done.5.refs_7_.refs_15_.refs_5_), channel_id=1, source_target_pairs={{0,8},{4,12},{8,0},{12,4},{16,24},{20,28},{24,16},{28,20},{1,9},{5... | collective-permute-start | bytes 811016 | tf_op jit(solution)/shard_map/ppermute | solution.py:36
  30.4 3.3 %collective-permute-start.15 = (bf16[2,256,384]{2,1,0:T(8,128)(2,1)S(1)}, bf16[2,256,384]{2,1,0:T(8,128)(2,1)}, u32[]{:S(2)}, u32[]{:S(2)}) collective-permute-start(bf16[2,256,384]{2,1,0:T(8,128)(2,1)S(1)} %get-tuple-element.31.refs_7_), channel_id=1, source_target_pairs={{0,24},{4,28},{8,16},{12,20},{16,8},{20,12},{24,0},{28,4},{1,25},{... | collective-permute-start | bytes 1179656 | tf_op jit(solution)/shard_map/ppermute | solution.py:36
  33.8 2.7 %collective-permute-done.6.refs_5_.refs_13_.refs_1_ = bf16[528,256]{1,0:T(8,128)(2,1)S(1)} collective-permute-done((bf16[528,256]{1,0:T(8,128)(2,1)S(1)}, bf16[528,256]{1,0:T(8,128)(2,1)S(1)}, u32[]{:S(2)}, u32[]{:S(2)}) %collective-permute-start.6) | collective-permute-done | bytes 270368 | tf_op jit(solution)/shard_map/ppermute | solution.py:36
  36.4 2.3 %collective-permute-start.7 = (bf16[2,256,384]{2,1,0:T(8,128)(2,1)S(1)}, bf16[2,256,384]{2,1,0:T(8,128)(2,1)}, u32[]{:S(2)}, u32[]{:S(2)}) collective-permute-start(bf16[2,256,384]{2,1,0:T(8,128)(2,1)S(1)} %get-tuple-element.19.refs_0_), channel_id=1, source_target_pairs={{0,8},{4,12},{8,0},{12,4},{16,24},{20,28},{24,16},{28,20},{1,9},{5... | collective-permute-start | bytes 1179656 | tf_op jit(solution)/shard_map/ppermute | solution.py:36
  38.7 2.3 %collective-permute-start.8 = (bf16[2,256,384]{2,1,0:T(8,128)(2,1)S(1)}, bf16[2,256,384]{2,1,0:T(8,128)(2,1)}, u32[]{:S(2)}, u32[]{:S(2)}) collective-permute-start(bf16[2,256,384]{2,1,0:T(8,128)(2,1)S(1)} %get-tuple-element.19.refs_0_), channel_id=1, source_target_pairs={{0,24},{4,28},{8,16},{12,20},{16,8},{20,12},{24,0},{28,4},{1,25},{... | collective-permute-start | bytes 1179656 | tf_op jit(solution)/shard_map/ppermute | solution.py:36
  42.5 7.3 %collective-permute-done.14.refs_9_ = bf16[2,256,384]{2,1,0:T(8,128)(2,1)} collective-permute-done((bf16[2,256,384]{2,1,0:T(8,128)(2,1)S(1)}, bf16[2,256,384]{2,1,0:T(8,128)(2,1)}, u32[]{:S(2)}, u32[]{:S(2)}) %collective-permute-start.14) | collective-permute-done | bytes 393248 | tf_op jit(solution)/shard_map/ppermute | solution.py:36
  51.3 4.7 %collective-permute-done.15.refs_10_ = bf16[2,256,384]{2,1,0:T(8,128)(2,1)} collective-permute-done((bf16[2,256,384]{2,1,0:T(8,128)(2,1)S(1)}, bf16[2,256,384]{2,1,0:T(8,128)(2,1)}, u32[]{:S(2)}, u32[]{:S(2)}) %collective-permute-start.15) | collective-permute-done | bytes 393248 | tf_op jit(solution)/shard_map/ppermute | solution.py:36
  57.5 3.8 %collective-permute-done.7.refs_2_ = bf16[2,256,384]{2,1,0:T(8,128)(2,1)} collective-permute-done((bf16[2,256,384]{2,1,0:T(8,128)(2,1)S(1)}, bf16[2,256,384]{2,1,0:T(8,128)(2,1)}, u32[]{:S(2)}, u32[]{:S(2)}) %collective-permute-start.7) | collective-permute-done | bytes 393248 | tf_op jit(solution)/shard_map/ppermute | solution.py:36
  61.3 7.2 %collective-permute-done.8.refs_5_ = bf16[2,256,384]{2,1,0:T(8,128)(2,1)} collective-permute-done((bf16[2,256,384]{2,1,0:T(8,128)(2,1)S(1)}, bf16[2,256,384]{2,1,0:T(8,128)(2,1)}, u32[]{:S(2)}, u32[]{:S(2)}) %collective-permute-start.8) | collective-permute-done | bytes 393248 | tf_op jit(solution)/shard_map/ppermute | solution.py:36
  74.1 5.8 %copy-done = bf16[2048,4096]{1,0:T(8,128)(2,1)S(1)} copy-done((bf16[2048,4096]{1,0:T(8,128)(2,1)S(1)}, bf16[2048,4096]{1,0:T(8,128)(2,1)}, u32[]{:S(2)}) %copy-start) | copy-done | bytes 16777240
  79.9 3.3 %shard_map.59.refs_6_ = f32[3,512,256]{2,1,0:T(8,128)S(1)} custom-call(s32[2]{0:T(128)S(1)} %pad_add_fusion.where_ref, bf16[2048,4096]{1,0:T(8,128)(2,1)S(1)} %copy-done, bf16[2048,4096]{1,0:T(8,128)(2,1)S(1)} %copy-done, bf16[2048,4096]{1,0:T(8,128)(2,1)S(1)} %copy-done, bf16[2048,4096]{1,0:T(8,128)(2,1)S(1)} %copy-done, ...), custom_call_target="tpu_custom_call" | custom-call | flops 1610612736 | bytes 6291456 | tf_op jit(solution)/shard_map/pallas_call | solution.py:213
  83.3 2.8 %shard_map.60.refs_2_ = f32[3,512,256]{2,1,0:T(8,128)S(1)} custom-call(s32[2]{0:T(128)S(1)} %pad_add_fusion.where_ref, bf16[2048,4096]{1,0:T(8,128)(2,1)S(1)} %copy-done, bf16[2048,4096]{1,0:T(8,128)(2,1)S(1)} %copy-done, bf16[2048,4096]{1,0:T(8,128)(2,1)S(1)} %copy-done, bf16[528,256]{1,0:T(8,128)(2,1)S(1)} %collective-permute-done.2.refs_3_.refs_11_, ...), custom_call_target="tpu_custom_call" | custom-call | flops 1207959552 | bytes 4718592 | tf_op jit(solution)/shard_map/pallas_call | solution.py:213
  104.1 10.1 %shard_map.56.refs_7_ = f32[512,4096]{1,0:T(8,128)S(1)} custom-call(s32[2]{0:T(128)S(1)} %pad_add_fusion.where_ref, s32[96]{0:T(128)S(1)} %reshape.34.tiles_ref, bf16[2,256,384]{2,1,0:T(8,128)(2,1)S(1)} %copy-done.15, bf16[2,256,384]{2,1,0:T(8,128)(2,1)S(1)} %copy-done.19, bf16[2,256,384]{2,1,0:T(8,128)(2,1)} %collective-permute-done.7.refs_2_, ...), custom_call_target="tpu_custom_call" | custom-call | flops 553648128 | bytes 21102592 | tf_op jit(solution)/shard_map/pallas_call | solution.py:170
  114.3 3.3 %copy-done.1 = f32[512,4096]{1,0:T(8,128)} copy-done((f32[512,4096]{1,0:T(8,128)}, f32[512,4096]{1,0:T(8,128)S(1)}, u32[]{:S(2)}) %copy-start.1) | copy-done | bytes 8388632
  117.7 3.4 %copy-done.2 = f32[512,4096]{1,0:T(8,128)S(1)} copy-done((f32[512,4096]{1,0:T(8,128)S(1)}, f32[512,4096]{1,0:T(8,128)}, u32[]{:S(2)}) %copy-start.2) | copy-done | bytes 8388632
  121.1 3.3 %shard_map.57.refs_0_.refs_1_.refs_2_.refs_3_.refs_4_.refs_5_.refs_6_.refs_7_ = bf16[512,4096]{1,0:T(8,128)(2,1)S(1)} custom-call(s32[2]{0:T(128)S(1)} %pad_add_fusion.where_ref, s32[96]{0:T(128)S(1)} %reshape.34.tiles_ref, bf16[2,256,384]{2,1,0:T(8,128)(2,1)} %collective-permute-done.16.refs_0_, bf16[2,256,384]{2,1,0:T(8,128)(2,1)S(1)} %copy-done.23, ...), custom_call_target="tpu_custom_call" | custom-call | flops 251658240 | bytes 18743296 | tf_op jit(solution)/shard_map/pallas_call | solution.py:170
  130.4 7.2 %collective-permute-start.24 = (bf16[512,256]{1,0:T(8,128)(2,1)S(1)}, bf16[512,256]{1,0:T(8,128)(2,1)S(1)}, u32[]{:S(2)}, u32[]{:S(2)}) collective-permute-start(bf16[512,256]{1,0:T(8,128)(2,1)S(1)} %fusion.1.refs_4_.refs_8_), channel_id=1, source_target_pairs={{0,4},{4,0},{8,12},{12,8},{16,20},{20,16},{24,28},{28,24},{1,5},{5... | collective-permute-start | bytes 786440 | tf_op jit(solution)/shard_map/ppermute | solution.py:36
  139.2 4.9 %collective-permute-start.28 = (bf16[512,256]{1,0:T(8,128)(2,1)S(1)}, bf16[512,256]{1,0:T(8,128)(2,1)S(1)}, u32[]{:S(2)}, u32[]{:S(2)}) collective-permute-start(bf16[512,256]{1,0:T(8,128)(2,1)S(1)} %collective-permute-done.27.refs_7_.refs_14_), channel_id=1, source_target_pairs={{0,8},{4,12},{8,0},{12,4},{16,24},{20,28},{24,16},{28,20},{1,9},{5... | collective-permute-start | bytes 786440 | tf_op jit(solution)/shard_map/ppermute | solution.py:36
  145.1 3.3 %shard_map.64.refs_6_ = f32[3,512,256]{2,1,0:T(8,128)S(1)} custom-call(s32[2]{0:T(128)S(1)} %pad_add_fusion.where_ref, bf16[2048,4096]{1,0:T(8,128)(2,1)S(1)} %bitcast.17, bf16[2048,4096]{1,0:T(8,128)(2,1)S(1)} %bitcast.17, bf16[2048,4096]{1,0:T(8,128)(2,1)S(1)} %bitcast.17, bf16[2048,4096]{1,0:T(8,128)(2,1)S(1)} %bitcast.17, ...), custom_call_target="tpu_custom_call" | custom-call | flops 1610612736 | bytes 6291456 | tf_op jit(solution)/shard_map/pallas_call | solution.py:213
  152.2 3.7 %collective-permute-done.26.refs_11_.refs_3_ = bf16[512,256]{1,0:T(8,128)(2,1)S(1)} collective-permute-done((bf16[512,256]{1,0:T(8,128)(2,1)S(1)}, bf16[512,256]{1,0:T(8,128)(2,1)S(1)}, u32[]{:S(2)}, u32[]{:S(2)}) %collective-permute-start.26) | collective-permute-done | bytes 262176 | tf_op jit(solution)/shard_map/ppermute | solution.py:36
  155.8 2.7 %shard_map.66.refs_2_ = f32[3,512,256]{2,1,0:T(8,128)S(1)} custom-call(s32[2]{0:T(128)S(1)} %pad_add_fusion.where_ref, bf16[2048,4096]{1,0:T(8,128)(2,1)S(1)} %bitcast.17, bf16[2048,4096]{1,0:T(8,128)(2,1)S(1)} %bitcast.17, bf16[2048,4096]{1,0:T(8,128)(2,1)S(1)} %bitcast.17, bf16[512,256]{1,0:T(8,128)(2,1)S(1)} %collective-permute-done.26.refs_11_.refs_3_, ...), custom_call_target="tpu_custom_call" | custom-call | flops 1207959552 | bytes 4718592 | tf_op jit(solution)/shard_map/pallas_call | solution.py:213
  166.8 7.2 %collective-permute-done.32 = bf16[512,256]{1,0:T(8,128)(2,1)S(1)} collective-permute-done((bf16[512,256]{1,0:T(8,128)(2,1)S(1)}, bf16[512,256]{1,0:T(8,128)(2,1)S(1)}, u32[]{:S(2)}, u32[]{:S(2)}) %collective-permute-start.32) | collective-permute-done | bytes 262176 | tf_op jit(solution)/shard_map/ppermute | solution.py:36
  178.7 6.7 %collective-permute-done.37.refs_7_.refs_14_ = bf16[512,256]{1,0:T(8,128)(2,1)S(1)} collective-permute-done((bf16[512,256]{1,0:T(8,128)(2,1)S(1)}, bf16[512,256]{1,0:T(8,128)(2,1)S(1)}, u32[]{:S(2)}, u32[]{:S(2)}) %collective-permute-start.37) | collective-permute-done | bytes 262176 | tf_op jit(solution)/shard_map/ppermute | solution.py:36
  187.2 4.0 %collective-permute-start.38 = (bf16[512,256]{1,0:T(8,128)(2,1)S(1)}, bf16[512,256]{1,0:T(8,128)(2,1)S(1)}, u32[]{:S(2)}, u32[]{:S(2)}) collective-permute-start(bf16[512,256]{1,0:T(8,128)(2,1)S(1)} %collective-permute-done.37.refs_7_.refs_14_), channel_id=1, source_target_pairs={{0,8},{4,12},{8,0},{12,4},{16,24},{20,28},{24,16},{28,20},{1,9},{5... | collective-permute-start | bytes 786440 | tf_op jit(solution)/shard_map/ppermute | solution.py:36
  191.5 3.3 %shard_map.70.refs_6_ = f32[3,512,256]{2,1,0:T(8,128)S(1)} custom-call(s32[2]{0:T(128)S(1)} %pad_add_fusion.where_ref, bf16[2048,4096]{1,0:T(8,128)(2,1)S(1)} %bitcast.17, bf16[2048,4096]{1,0:T(8,128)(2,1)S(1)} %bitcast.17, bf16[2048,4096]{1,0:T(8,128)(2,1)S(1)} %bitcast.17, bf16[2048,4096]{1,0:T(8,128)(2,1)S(1)} %bitcast.17, ...), custom_call_target="tpu_custom_call" | custom-call | flops 1610612736 | bytes 6291456 | tf_op jit(solution)/shard_map/pallas_call | solution.py:213
  194.8 3.9 %collective-permute-start.40 = (bf16[512,256]{1,0:T(8,128)(2,1)S(1)}, bf16[512,256]{1,0:T(8,128)(2,1)S(1)}, u32[]{:S(2)}, u32[]{:S(2)}) collective-permute-start(bf16[512,256]{1,0:T(8,128)(2,1)S(1)} %collective-permute-done.39.refs_15_.refs_5_), channel_id=1, source_target_pairs={{0,8},{4,12},{8,0},{12,4},{16,24},{20,28},{24,16},{28,20},{1,9},{5... | collective-permute-start | bytes 786440 | tf_op jit(solution)/shard_map/ppermute | solution.py:36
  198.9 2.7 %shard_map.72.refs_2_ = f32[3,512,256]{2,1,0:T(8,128)S(1)} custom-call(s32[2]{0:T(128)S(1)} %pad_add_fusion.where_ref, bf16[2048,4096]{1,0:T(8,128)(2,1)S(1)} %bitcast.17, bf16[2048,4096]{1,0:T(8,128)(2,1)S(1)} %bitcast.17, bf16[2048,4096]{1,0:T(8,128)(2,1)S(1)} %bitcast.17, bf16[512,256]{1,0:T(8,128)(2,1)S(1)} %collective-permute-done.36.refs_11_.refs_3_, ...), custom_call_target="tpu_custom_call" | custom-call | flops 1207959552 | bytes 4718592 | tf_op jit(solution)/shard_map/pallas_call | solution.py:213
  209.8 2.8 %collective-permute-done.41 = bf16[512,256]{1,0:T(8,128)(2,1)S(1)} collective-permute-done((bf16[512,256]{1,0:T(8,128)(2,1)S(1)}, bf16[512,256]{1,0:T(8,128)(2,1)S(1)}, u32[]{:S(2)}, u32[]{:S(2)}) %collective-permute-start.41) | collective-permute-done | bytes 262176 | tf_op jit(solution)/shard_map/ppermute | solution.py:36
  212.6 5.9 %collective-permute-done.42 = bf16[512,256]{1,0:T(8,128)(2,1)S(1)} collective-permute-done((bf16[512,256]{1,0:T(8,128)(2,1)S(1)}, bf16[512,256]{1,0:T(8,128)(2,1)S(1)}, u32[]{:S(2)}, u32[]{:S(2)}) %collective-permute-start.42) | collective-permute-done | bytes 262176 | tf_op jit(solution)/shard_map/ppermute | solution.py:36
  (166 shorter events, 73.6 us)
Async XLA Ops:
  2.5 12.5 %collective-permute-start.3 = (bf16[528,256]{1,0:T(8,128)(2,1)S(1)}, bf16[528,256]{1,0:T(8,128)(2,1)S(1)}, u32[]{:S(2)}, u32[]{:S(2)}) collective-permute-start(bf16[528,256]{1,0:T(8,128)(2,1)S(1)} %constant_dynamic-update-slice_fusion.refs_0_.refs_8_.refs_4_), channel_id=1, source_target_pairs={{0,24},{4,28},{8,16},{12,20},{16,8},{20,12},{24,0},{28,4},{1,25},{... | collective-permute-start | bytes 811016 | tf_op jit(solution)/shard_map/ppermute | solution.py:36
  7.6 14.0 %collective-permute-start.1 = (bf16[528,256]{1,0:T(8,128)(2,1)S(1)}, bf16[528,256]{1,0:T(8,128)(2,1)S(1)}, u32[]{:S(2)}, u32[]{:S(2)}) collective-permute-start(bf16[528,256]{1,0:T(8,128)(2,1)S(1)} %constant_dynamic-update-slice_fusion.refs_0_.refs_8_.refs_4_), channel_id=1, source_target_pairs={{0,8},{4,12},{8,0},{12,4},{16,24},{20,28},{24,16},{28,20},{1,9},{5... | collective-permute-start | bytes 811016 | tf_op jit(solution)/shard_map/ppermute | solution.py:36
  16.7 13.7 %collective-permute-start = (bf16[528,256]{1,0:T(8,128)(2,1)S(1)}, bf16[528,256]{1,0:T(8,128)(2,1)S(1)}, u32[]{:S(2)}, u32[]{:S(2)}) collective-permute-start(bf16[528,256]{1,0:T(8,128)(2,1)S(1)} %constant_dynamic-update-slice_fusion.refs_0_.refs_8_.refs_4_), channel_id=1, source_target_pairs={{0,4},{4,0},{8,12},{12,8},{16,20},{20,16},{24,28},{28,24},{1,5},{5... | collective-permute-start | bytes 811016 | tf_op jit(solution)/shard_map/ppermute | solution.py:36
  17.0 16.7 %collective-permute-start.4 = (bf16[528,256]{1,0:T(8,128)(2,1)S(1)}, bf16[528,256]{1,0:T(8,128)(2,1)S(1)}, u32[]{:S(2)}, u32[]{:S(2)}) collective-permute-start(bf16[528,256]{1,0:T(8,128)(2,1)S(1)} %collective-permute-done.3.refs_6_.refs_14_.refs_7_), channel_id=1, source_target_pairs={{0,8},{4,12},{8,0},{12,4},{16,24},{20,28},{24,16},{28,20},{1,9},{5... | collective-permute-start | bytes 811016 | tf_op jit(solution)/shard_map/ppermute | solution.py:36
  21.7 12.1 %collective-permute-start.2 = (bf16[528,256]{1,0:T(8,128)(2,1)S(1)}, bf16[528,256]{1,0:T(8,128)(2,1)S(1)}, u32[]{:S(2)}, u32[]{:S(2)}) collective-permute-start(bf16[528,256]{1,0:T(8,128)(2,1)S(1)} %collective-permute-done.1.refs_2_.refs_10_.refs_6_), channel_id=1, source_target_pairs={{0,4},{4,0},{8,12},{12,8},{16,20},{20,16},{24,28},{28,24},{1,5},{5... | collective-permute-start | bytes 811016 | tf_op jit(solution)/shard_map/ppermute | solution.py:36
  24.4 12.0 %collective-permute-start.6 = (bf16[528,256]{1,0:T(8,128)(2,1)S(1)}, bf16[528,256]{1,0:T(8,128)(2,1)S(1)}, u32[]{:S(2)}, u32[]{:S(2)}) collective-permute-start(bf16[528,256]{1,0:T(8,128)(2,1)S(1)} %collective-permute-done.5.refs_7_.refs_15_.refs_5_), channel_id=1, source_target_pairs={{0,8},{4,12},{8,0},{12,4},{16,24},{20,28},{24,16},{28,20},{1,9},{5... | collective-permute-start | bytes 811016 | tf_op jit(solution)/shard_map/ppermute | solution.py:36
  30.3 19.6 %collective-permute-start.14 = (bf16[2,256,384]{2,1,0:T(8,128)(2,1)S(1)}, bf16[2,256,384]{2,1,0:T(8,128)(2,1)}, u32[]{:S(2)}, u32[]{:S(2)}) collective-permute-start(bf16[2,256,384]{2,1,0:T(8,128)(2,1)S(1)} %get-tuple-element.31.refs_7_), channel_id=1, source_target_pairs={{0,8},{4,12},{8,0},{12,4},{16,24},{20,28},{24,16},{28,20},{1,9},{5... | collective-permute-start | bytes 1179656 | tf_op jit(solution)/shard_map/ppermute | solution.py:36
  30.4 25.5 %collective-permute-start.15 = (bf16[2,256,384]{2,1,0:T(8,128)(2,1)S(1)}, bf16[2,256,384]{2,1,0:T(8,128)(2,1)}, u32[]{:S(2)}, u32[]{:S(2)}) collective-permute-start(bf16[2,256,384]{2,1,0:T(8,128)(2,1)S(1)} %get-tuple-element.31.refs_7_), channel_id=1, source_target_pairs={{0,24},{4,28},{8,16},{12,20},{16,8},{20,12},{24,0},{28,4},{1,25},{... | collective-permute-start | bytes 1179656 | tf_op jit(solution)/shard_map/ppermute | solution.py:36
  36.4 24.8 %collective-permute-start.7 = (bf16[2,256,384]{2,1,0:T(8,128)(2,1)S(1)}, bf16[2,256,384]{2,1,0:T(8,128)(2,1)}, u32[]{:S(2)}, u32[]{:S(2)}) collective-permute-start(bf16[2,256,384]{2,1,0:T(8,128)(2,1)S(1)} %get-tuple-element.19.refs_0_), channel_id=1, source_target_pairs={{0,8},{4,12},{8,0},{12,4},{16,24},{20,28},{24,16},{28,20},{1,9},{5... | collective-permute-start | bytes 1179656 | tf_op jit(solution)/shard_map/ppermute | solution.py:36
  38.7 29.7 %collective-permute-start.8 = (bf16[2,256,384]{2,1,0:T(8,128)(2,1)S(1)}, bf16[2,256,384]{2,1,0:T(8,128)(2,1)}, u32[]{:S(2)}, u32[]{:S(2)}) collective-permute-start(bf16[2,256,384]{2,1,0:T(8,128)(2,1)S(1)} %get-tuple-element.19.refs_0_), channel_id=1, source_target_pairs={{0,24},{4,28},{8,16},{12,20},{16,8},{20,12},{24,0},{28,4},{1,25},{... | collective-permute-start | bytes 1179656 | tf_op jit(solution)/shard_map/ppermute | solution.py:36
  41.0 27.5 %collective-permute-start.9 = (bf16[2,256,384]{2,1,0:T(8,128)(2,1)S(1)}, bf16[2,256,384]{2,1,0:T(8,128)(2,1)S(1)}, u32[]{:S(2)}, u32[]{:S(2)}) collective-permute-start(bf16[2,256,384]{2,1,0:T(8,128)(2,1)S(1)} %get-tuple-element.19.refs_0_), channel_id=1, source_target_pairs={{0,4},{4,0},{8,12},{12,8},{16,20},{20,16},{24,28},{28,24},{1,5},{5... | collective-permute-start | bytes 1179656 | tf_op jit(solution)/shard_map/ppermute | solution.py:36
  49.8 20.8 %collective-permute-start.13 = (bf16[2,256,384]{2,1,0:T(8,128)(2,1)S(1)}, bf16[2,256,384]{2,1,0:T(8,128)(2,1)}, u32[]{:S(2)}, u32[]{:S(2)}) collective-permute-start(bf16[2,256,384]{2,1,0:T(8,128)(2,1)S(1)} %get-tuple-element.31.refs_7_), channel_id=1, source_target_pairs={{0,4},{4,0},{8,12},{12,8},{16,20},{20,16},{24,28},{28,24},{1,5},{5... | collective-permute-start | bytes 1179656 | tf_op jit(solution)/shard_map/ppermute | solution.py:36
  56.0 16.7 %collective-permute-start.19 = (bf16[2,256,384]{2,1,0:T(8,128)(2,1)}, bf16[2,256,384]{2,1,0:T(8,128)(2,1)}, u32[]{:S(2)}, u32[]{:S(2)}) collective-permute-start(bf16[2,256,384]{2,1,0:T(8,128)(2,1)} %collective-permute-done.15.refs_10_), channel_id=1, source_target_pairs={{0,4},{4,0},{8,12},{12,8},{16,20},{20,16},{24,28},{28,24},{1,5},{5... | collective-permute-start | bytes 1179656 | tf_op jit(solution)/shard_map/ppermute | solution.py:36
  68.5 20.7 %collective-permute-start.10 = (bf16[2,256,384]{2,1,0:T(8,128)(2,1)}, bf16[2,256,384]{2,1,0:T(8,128)(2,1)}, u32[]{:S(2)}, u32[]{:S(2)}) collective-permute-start(bf16[2,256,384]{2,1,0:T(8,128)(2,1)} %collective-permute-done.8.refs_5_), channel_id=1, source_target_pairs={{0,4},{4,0},{8,12},{12,8},{16,20},{20,16},{24,28},{28,24},{1,5},{5... | collective-permute-start | bytes 1179656 | tf_op jit(solution)/shard_map/ppermute | solution.py:36
  70.0 19.3 %collective-permute-start.11 = (bf16[2,256,384]{2,1,0:T(8,128)(2,1)}, bf16[2,256,384]{2,1,0:T(8,128)(2,1)}, u32[]{:S(2)}, u32[]{:S(2)}) collective-permute-start(bf16[2,256,384]{2,1,0:T(8,128)(2,1)} %collective-permute-done.7.refs_2_), channel_id=1, source_target_pairs={{0,4},{4,0},{8,12},{12,8},{16,20},{20,16},{24,28},{28,24},{1,5},{5... | collective-permute-start | bytes 1179656 | tf_op jit(solution)/shard_map/ppermute | solution.py:36
  70.5 18.8 %collective-permute-start.12 = (bf16[2,256,384]{2,1,0:T(8,128)(2,1)}, bf16[2,256,384]{2,1,0:T(8,128)(2,1)}, u32[]{:S(2)}, u32[]{:S(2)}) collective-permute-start(bf16[2,256,384]{2,1,0:T(8,128)(2,1)} %collective-permute-done.8.refs_5_), channel_id=1, source_target_pairs={{0,8},{4,12},{8,0},{12,4},{16,24},{20,28},{24,16},{28,20},{1,9},{5... | collective-permute-start | bytes 1179656 | tf_op jit(solution)/shard_map/ppermute | solution.py:36
  70.6 25.4 %collective-permute-start.18 = (bf16[2,256,384]{2,1,0:T(8,128)(2,1)}, bf16[2,256,384]{2,1,0:T(8,128)(2,1)S(1)}, u32[]{:S(2)}, u32[]{:S(2)}) collective-permute-start(bf16[2,256,384]{2,1,0:T(8,128)(2,1)} %collective-permute-done.15.refs_10_), channel_id=1, source_target_pairs={{0,8},{4,12},{8,0},{12,4},{16,24},{20,28},{24,16},{28,20},{1,9},{5... | collective-permute-start | bytes 1179656 | tf_op jit(solution)/shard_map/ppermute | solution.py:36
  72.6 25.6 %collective-permute-start.17 = (bf16[2,256,384]{2,1,0:T(8,128)(2,1)}, bf16[2,256,384]{2,1,0:T(8,128)(2,1)S(1)}, u32[]{:S(2)}, u32[]{:S(2)}) collective-permute-start(bf16[2,256,384]{2,1,0:T(8,128)(2,1)} %collective-permute-done.14.refs_9_), channel_id=1, source_target_pairs={{0,4},{4,0},{8,12},{12,8},{16,20},{20,16},{24,28},{28,24},{1,5},{5... | collective-permute-start | bytes 1179656 | tf_op jit(solution)/shard_map/ppermute | solution.py:36
  89.2 28.5 %collective-permute-start.20 = (bf16[2,256,384]{2,1,0:T(8,128)(2,1)}, bf16[2,256,384]{2,1,0:T(8,128)(2,1)}, u32[]{:S(2)}, u32[]{:S(2)}) collective-permute-start(bf16[2,256,384]{2,1,0:T(8,128)(2,1)} %collective-permute-done.19.refs_4_), channel_id=1, source_target_pairs={{0,8},{4,12},{8,0},{12,4},{16,24},{20,28},{24,16},{28,20},{1,9},{5... | collective-permute-start | bytes 1179656 | tf_op jit(solution)/shard_map/ppermute | solution.py:36
  89.3 28.3 %collective-permute-start.16 = (bf16[2,256,384]{2,1,0:T(8,128)(2,1)}, bf16[2,256,384]{2,1,0:T(8,128)(2,1)}, u32[]{:S(2)}, u32[]{:S(2)}) collective-permute-start(bf16[2,256,384]{2,1,0:T(8,128)(2,1)} %collective-permute-done.10.refs_6_), channel_id=1, source_target_pairs={{0,8},{4,12},{8,0},{12,4},{16,24},{20,28},{24,16},{28,20},{1,9},{5... | collective-permute-start | bytes 1179656 | tf_op jit(solution)/shard_map/ppermute | solution.py:36
  92.9 33.4 %collective-permute-start.21 = (bf16[512,256]{1,0:T(8,128)(2,1)}, bf16[512,256]{1,0:T(8,128)(2,1)}, u32[]{:S(2)}, u32[]{:S(2)}) collective-permute-start(bf16[512,256]{1,0:T(8,128)(2,1)} %shard_map.61), channel_id=1, source_target_pairs={{0,3},{1,2},{2,1},{3,0},{4,7},{5,6},{6,5},{7,4},{8,11},{9,10},{10,... | collective-permute-start | bytes 786440 | tf_op jit(solution)/shard_map/ppermute | solution.py:36
  96.7 29.6 %collective-permute-start.22 = (bf16[512,256]{1,0:T(8,128)(2,1)}, bf16[512,256]{1,0:T(8,128)(2,1)}, u32[]{:S(2)}, u32[]{:S(2)}) collective-permute-start(bf16[512,256]{1,0:T(8,128)(2,1)} %shard_map.62), channel_id=1, source_target_pairs={{0,2},{1,3},{2,0},{3,1},{4,6},{5,7},{6,4},{7,5},{8,10},{9,11},{10,... | collective-permute-start | bytes 786440 | tf_op jit(solution)/shard_map/ppermute | solution.py:36
  99.0 27.3 %collective-permute-start.23 = (bf16[512,256]{1,0:T(8,128)(2,1)}, bf16[512,256]{1,0:T(8,128)(2,1)}, u32[]{:S(2)}, u32[]{:S(2)}) collective-permute-start(bf16[512,256]{1,0:T(8,128)(2,1)} %shard_map.63), channel_id=1, source_target_pairs={{0,1},{1,0},{2,3},{3,2},{4,5},{5,4},{6,7},{7,6},{8,9},{9,8},{10,11... | collective-permute-start | bytes 786440 | tf_op jit(solution)/shard_map/ppermute | solution.py:36
  130.4 14.4 %collective-permute-start.25 = (bf16[512,256]{1,0:T(8,128)(2,1)S(1)}, bf16[512,256]{1,0:T(8,128)(2,1)S(1)}, u32[]{:S(2)}, u32[]{:S(2)}) collective-permute-start(bf16[512,256]{1,0:T(8,128)(2,1)S(1)} %fusion.1.refs_4_.refs_8_), channel_id=1, source_target_pairs={{0,8},{4,12},{8,0},{12,4},{16,24},{20,28},{24,16},{28,20},{1,9},{5... | collective-permute-start | bytes 786440 | tf_op jit(solution)/shard_map/ppermute | solution.py:36
  130.4 14.6 %collective-permute-start.24 = (bf16[512,256]{1,0:T(8,128)(2,1)S(1)}, bf16[512,256]{1,0:T(8,128)(2,1)S(1)}, u32[]{:S(2)}, u32[]{:S(2)}) collective-permute-start(bf16[512,256]{1,0:T(8,128)(2,1)S(1)} %fusion.1.refs_4_.refs_8_), channel_id=1, source_target_pairs={{0,4},{4,0},{8,12},{12,8},{16,20},{20,16},{24,28},{28,24},{1,5},{5... | collective-permute-start | bytes 786440 | tf_op jit(solution)/shard_map/ppermute | solution.py:36
  139.2 16.6 %collective-permute-start.28 = (bf16[512,256]{1,0:T(8,128)(2,1)S(1)}, bf16[512,256]{1,0:T(8,128)(2,1)S(1)}, u32[]{:S(2)}, u32[]{:S(2)}) collective-permute-start(bf16[512,256]{1,0:T(8,128)(2,1)S(1)} %collective-permute-done.27.refs_7_.refs_14_), channel_id=1, source_target_pairs={{0,8},{4,12},{8,0},{12,4},{16,24},{20,28},{24,16},{28,20},{1,9},{5... | collective-permute-start | bytes 786440 | tf_op jit(solution)/shard_map/ppermute | solution.py:36
  161.4 12.6 %collective-permute-start.32 = (bf16[512,256]{1,0:T(8,128)(2,1)S(1)}, bf16[512,256]{1,0:T(8,128)(2,1)S(1)}, u32[]{:S(2)}, u32[]{:S(2)}) collective-permute-start(bf16[512,256]{1,0:T(8,128)(2,1)S(1)} %shard_map.68), channel_id=1, source_target_pairs={{0,2},{1,3},{2,0},{3,1},{4,6},{5,7},{6,4},{7,5},{8,10},{9,11},{10,... | collective-permute-start | bytes 786440 | tf_op jit(solution)/shard_map/ppermute | solution.py:36
  174.2 11.2 %collective-permute-start.37 = (bf16[512,256]{1,0:T(8,128)(2,1)S(1)}, bf16[512,256]{1,0:T(8,128)(2,1)S(1)}, u32[]{:S(2)}, u32[]{:S(2)}) collective-permute-start(bf16[512,256]{1,0:T(8,128)(2,1)S(1)} %fusion.2.refs_4_.refs_8_), channel_id=1, source_target_pairs={{0,24},{4,28},{8,16},{12,20},{16,8},{20,12},{24,0},{28,4},{1,25},{... | collective-permute-start | bytes 786440 | tf_op jit(solution)/shard_map/ppermute | solution.py:36
  175.8 15.5 %collective-permute-start.35 = (bf16[512,256]{1,0:T(8,128)(2,1)S(1)}, bf16[512,256]{1,0:T(8,128)(2,1)S(1)}, u32[]{:S(2)}, u32[]{:S(2)}) collective-permute-start(bf16[512,256]{1,0:T(8,128)(2,1)S(1)} %fusion.2.refs_4_.refs_8_), channel_id=1, source_target_pairs={{0,8},{4,12},{8,0},{12,4},{16,24},{20,28},{24,16},{28,20},{1,9},{5... | collective-permute-start | bytes 786440 | tf_op jit(solution)/shard_map/ppermute | solution.py:36
  177.1 14.4 %collective-permute-start.34 = (bf16[512,256]{1,0:T(8,128)(2,1)S(1)}, bf16[512,256]{1,0:T(8,128)(2,1)S(1)}, u32[]{:S(2)}, u32[]{:S(2)}) collective-permute-start(bf16[512,256]{1,0:T(8,128)(2,1)S(1)} %fusion.2.refs_4_.refs_8_), channel_id=1, source_target_pairs={{0,4},{4,0},{8,12},{12,8},{16,20},{20,16},{24,28},{28,24},{1,5},{5... | collective-permute-start | bytes 786440 | tf_op jit(solution)/shard_map/ppermute | solution.py:36
  187.2 11.7 %collective-permute-start.38 = (bf16[512,256]{1,0:T(8,128)(2,1)S(1)}, bf16[512,256]{1,0:T(8,128)(2,1)S(1)}, u32[]{:S(2)}, u32[]{:S(2)}) collective-permute-start(bf16[512,256]{1,0:T(8,128)(2,1)S(1)} %collective-permute-done.37.refs_7_.refs_14_), channel_id=1, source_target_pairs={{0,8},{4,12},{8,0},{12,4},{16,24},{20,28},{24,16},{28,20},{1,9},{5... | collective-permute-start | bytes 786440 | tf_op jit(solution)/shard_map/ppermute | solution.py:36
  205.2 13.4 %collective-permute-start.42 = (bf16[512,256]{1,0:T(8,128)(2,1)S(1)}, bf16[512,256]{1,0:T(8,128)(2,1)S(1)}, u32[]{:S(2)}, u32[]{:S(2)}) collective-permute-start(bf16[512,256]{1,0:T(8,128)(2,1)S(1)} %shard_map.74), channel_id=1, source_target_pairs={{0,2},{1,3},{2,0},{3,1},{4,6},{5,7},{6,4},{7,5},{8,10},{9,11},{10,... | collective-permute-start | bytes 786440 | tf_op jit(solution)/shard_map/ppermute | solution.py:36
  (45 other events, 646.5 us)

commit v4 on v3

--- a/solution.py
+++ b/solution.py
@@ -8,8 +8,8 @@
 from jax.sharding import PartitionSpec as P
 
 TILE = 128
-SMALL_LIMIT = 16 * 2**20
-ROWS_LIMIT = 30 * 2**20
+SMALL_LIMIT = 18 * 2**20
+LARGE_LIMIT = 46 * 2**20
 center = 1.0
 spread = 2.5
 
@@ -53,12 +53,11 @@
 
 def hop(pieces, hops, after):
     order, depth = routes(lax.axis_size("row"))
-    chosen = [route for route in order if depth[route[0]] == hops]
-    sources = sorted({source for _, source, _ in chosen})
-    held, after = lax.optimization_barrier(([pieces[source] for source in sources], after))
-    held = dict(zip(sources, held))
-    for mask, source, step in chosen:
-        pieces[mask] = swap(held[source], "row", step)
+    held, after = lax.optimization_barrier((dict(pieces), after))
+    pieces.update(held)
+    for mask, source, step in order:
+        if depth[mask] == hops:
+            pieces[mask] = swap(pieces[source], "row", step)
     return after
 
 
@@ -98,7 +97,7 @@
     )(*[pieces[mask] for mask in masks])
 
 
-def rows_kernel(listed, firsts, last_call, where_ref, tiles_ref, *refs):
+def rows_kernel(listed, per_shard, firsts, last_call, where_ref, tiles_ref, *refs):
     values_refs, (external_ref, held_ref, start_ref), (out_ref, total) = (
         refs[: len(firsts)],
         refs[len(firsts) : len(firsts) + 3],
@@ -106,14 +105,13 @@
     )
     target = total if last_call else out_ref
     target[...] = start_ref[...].astype(jnp.float32)
-    per_shard = start_ref.shape[0] // TILE
-    mine = where_ref[1] * per_shard
+    mine = where_ref[1] * per_shard + pl.program_id(0)
 
     for values_ref, first in zip(values_refs, firsts):
 
         def one_batch(b, carry, values_ref=values_ref, first=first):
             spots = [tiles_ref[(first + b) * listed + i] for i in range(listed)]
-            owned = [(s >= mine) & (s < mine + per_shard) for s in spots]
+            owned = [s == mine for s in spots]
 
             @pl.when(functools.reduce(jnp.logical_or, owned))
             def _():
@@ -135,20 +133,16 @@
                 )
                 potential = external - root
                 weighted = (potential * values.astype(jnp.float32)).astype(jnp.bfloat16)
-                for i in range(listed):
-
-                    @pl.when(owned[i])
-                    def _(i=i):
-                        strip = lax.dot_general(
-                            values[:, i * TILE : (i + 1) * TILE],
-                            weighted,
-                            (((0,), (0,)), ((), ())),
-                            preferred_element_type=jnp.float32,
-                        )
-                        rows = pl.ds(pl.multiple_of((spots[i] - mine) * TILE, TILE), TILE)
-                        for j in range(listed):
-                            columns = pl.ds(pl.multiple_of(spots[j] * TILE, TILE), TILE)
-                            target[rows, columns] += strip[:, j * TILE : (j + 1) * TILE]
+                place = sum(jnp.where(o, i, 0) for i, o in enumerate(owned))
+                strip = lax.dot_general(
+                    values_ref[b, :, pl.ds(pl.multiple_of(place * TILE, TILE), TILE)],
+                    weighted,
+                    (((0,), (0,)), ((), ())),
+                    preferred_element_type=jnp.float32,
+                )
+                for j in range(listed):
+                    columns = pl.ds(pl.multiple_of(spots[j] * TILE, TILE), TILE)
+                    target[:, columns] += strip[:, j * TILE : (j + 1) * TILE]
 
             return carry
 
@@ -157,41 +151,34 @@
         out_ref[...] = total[...].astype(jnp.bfloat16)
 
 
-def add_rows(
-    where, tiles, pieces, firsts, external, held, start, shard_rows, first_call, last_call
-):
+def add_rows(where, tiles, pieces, firsts, external, held, start, last_call):
     batches, points, length = pieces[0].shape
     listed = length // TILE
-    width = start.shape[1]
+    shard_rows, width = start.shape
     once = pl.Buffered(1)
     whole = pl.BlockSpec(
         (batches, points, length), lambda i, w, t: (0, 0, 0), pipeline_mode=once
     )
+    rows = pl.BlockSpec((TILE, width), lambda i, w, t: (i, 0))
     return pl.pallas_call(
-        functools.partial(rows_kernel, listed, firsts, last_call),
-        out_shape=jax.ShapeDtypeStruct((shard_rows, width), jnp.bfloat16 if last_call else jnp.float32),
+        functools.partial(rows_kernel, listed, shard_rows // TILE, firsts, last_call),
+        out_shape=jax.ShapeDtypeStruct(start.shape, jnp.bfloat16 if last_call else jnp.float32),
         grid_spec=pltpu.PrefetchScalarGridSpec(
             num_scalar_prefetch=2,
-            grid=(1,),
+            grid=(shard_rows // TILE,),
             in_specs=[whole for _ in firsts]
             + [
                 pl.BlockSpec(external.shape, lambda i, w, t: (0, 0)),
                 pl.BlockSpec(held.shape, lambda i, w, t: (0, 0, 0), pipeline_mode=once),
-                pl.BlockSpec(
-                    (shard_rows, width),
-                    (lambda i, w, t: (w[0], 0)) if first_call else (lambda i, w, t: (0, 0)),
-                    pipeline_mode=once,
-                ),
+                rows,
             ],
-            out_specs=pl.BlockSpec((shard_rows, width), lambda i, w, t: (0, 0), pipeline_mode=once),
-            scratch_shapes=[
-                pltpu.VMEM((shard_rows, width) if last_call else (8, TILE), jnp.float32)
-            ],
-        ),
-        compiler_params=pltpu.CompilerParams(vmem_limit_bytes=ROWS_LIMIT),
+            out_specs=rows,
+            scratch_shapes=[pltpu.VMEM((TILE, width) if last_call else (8, TILE), jnp.float32)],
+        ),
+        compiler_params=pltpu.CompilerParams(vmem_limit_bytes=SMALL_LIMIT),
         cost_estimate=pl.CostEstimate(
             flops=len(firsts) * batches * 2 * points * length * TILE,
-            bytes_accessed=len(firsts) * pieces[0].size * 2 + shard_rows * width * 8,
+            bytes_accessed=2 * len(firsts) * batches * points * length + shard_rows * width * 8,
             transcendentals=0,
         ),
     )(where, tiles, *pieces, external, held, start)
@@ -207,7 +194,7 @@
     out_ref[0] = total
 
 
-def early_product(where, kinetic, pieces, masks, partners, before=None):
+def early_product(where, kinetic, pieces, masks, partners, limit, before=None):
     shard_rows, count = kinetic.shape[0] // (partners + 1), pieces[0].shape[1]
     whole = pl.BlockSpec((1, shard_rows, count), lambda s, w: (s, 0, 0))
     return pl.pallas_call(
@@ -227,7 +214,7 @@
             + [whole] * (before is not None),
             out_specs=whole,
         ),
-        compiler_params=pltpu.CompilerParams(vmem_limit_bytes=SMALL_LIMIT),
+        compiler_params=pltpu.CompilerParams(vmem_limit_bytes=limit),
         cost_estimate=pl.CostEstimate(
             flops=2 * partners * shard_rows * shard_rows * len(masks) * count,
             bytes_accessed=2 * partners * shard_rows * shard_rows * len(masks),
@@ -244,7 +231,7 @@
     out_ref[...] = total.astype(jnp.bfloat16)
 
 
-def late_product(where, kinetic, pieces, masks, early, partner):
+def late_product(where, kinetic, pieces, masks, early, partner, limit):
     shard_rows, count = early.shape[1:]
     return pl.pallas_call(
         functools.partial(late_kernel, len(masks)),
@@ -263,7 +250,7 @@
             + [pl.BlockSpec((1, shard_rows, count), lambda s, w: (partner - 1, 0, 0))],
             out_specs=pl.BlockSpec((shard_rows, count), lambda s, w: (0, 0)),
         ),
-        compiler_params=pltpu.CompilerParams(vmem_limit_bytes=SMALL_LIMIT),
+        compiler_params=pltpu.CompilerParams(vmem_limit_bytes=limit),
         cost_estimate=pl.CostEstimate(
             flops=2 * shard_rows * shard_rows * len(masks) * count,
             bytes_accessed=2 * shard_rows * shard_rows * len(masks),
@@ -318,18 +305,20 @@
     middle = [mask for mask in masks if depth[mask] == 2]
     last = [mask for mask in masks if depth[mask] > 2]
 
-    def first_products(pieces):
-        return early_product(where, kinetic, [pieces[m] for m in soon], soon, col_count - 1)
-
-    def send(pieces, early):
+    def first_products(pieces, limit=SMALL_LIMIT):
+        return early_product(where, kinetic, [pieces[m] for m in soon], soon, col_count - 1, limit)
+
+    def sums(pieces, early, limit=SMALL_LIMIT):
         early = early_product(
-            where, kinetic, [pieces[m] for m in middle], middle, col_count - 1, early
+            where, kinetic, [pieces[m] for m in middle], middle, col_count - 1, limit, early
         )
-        arrived = []
-        for partner in range(col_count - 1, 0, -1):
-            part = late_product(where, kinetic, [pieces[m] for m in last], last, early, partner)
-            arrived.append(swap(part, "col", partner))
-        return arrived
+        return [
+            late_product(where, kinetic, [pieces[m] for m in last], last, early, partner, limit)
+            for partner in range(col_count - 1, 0, -1)
+        ]
+
+    def send(parts):
+        return [swap(part, "col", len(parts) - i) for i, part in enumerate(parts)]
 
     orbital_pieces = spread_out(noted(orbitals, external, tiles))
     held, notes = stacked(orbital_pieces, shard_rows)
@@ -345,7 +334,7 @@
 
     half = batch_count // 2
 
-    def rows_of(chosen, start, first_call, last_call):
+    def rows_of(chosen, start, last_call):
         return add_rows(
             where,
             group_tiles,
@@ -354,8 +343,6 @@
             group_external,
             held,
             start,
-            shard_rows,
-            first_call,
             last_call,
         )
 
@@ -365,35 +352,42 @@
             reduced = reduced + part.astype(jnp.float32)
         return reduced / spread - center / spread * vectors.astype(jnp.float32)
 
-    arrived = send(orbital_pieces, first_products(orbital_pieces))
     value_pieces = [{0: grid_values[:half]}, {0: grid_values[half:]}]
+    parts = sums(orbital_pieces, first_products(orbital_pieces, LARGE_LIMIT), LARGE_LIMIT)
+    own_kinetic = lax.dynamic_slice_in_dim(kinetic, where[0] * shard_rows, shard_rows, 0)
     most = max(depth.values())
-    taken, total = [], kinetic
+    taken, total = [], own_kinetic
 
     def arrived_values():
         return [(m, p) for p in range(2) for m in sorted(value_pieces[p])]
 
-    for turn in range(1, most + 2):
-        after = [orbital_pieces, [value_pieces[p][m] for m, p in arrived_values()]]
-        if turn == most:
-            taken = arrived_values()
-            total = rows_of(taken, kinetic, True, False)
+    orbital_pieces = hop(value_pieces[0], 1, orbital_pieces)
+    for turn in range(2, most + 2):
+        fresh = [which for which in arrived_values() if which not in taken]
+        taken = taken + fresh
         if turn == most + 1:
-            after, total = lax.optimization_barrier((after, total))
+            total = hop(value_pieces[1], turn - 1, total)
+        else:
+            value_pieces[1], parts, total = hop(
+                value_pieces[0], turn, (value_pieces[1], parts, total)
+            )
+            total = hop(value_pieces[1], turn - 1, total)
         if turn <= most:
-            after = hop(value_pieces[0], turn, after)
-        if turn > 1:
-            hop(value_pieces[1], turn - 1, after)
+            total = rows_of(fresh, total, False)
+        else:
+            taken = [which for which in taken if which not in fresh]
+    arrived = send(parts)
+    arrived = send(parts)
     rest = [(m, p) for p in range(2) for m in masks if (m, p) not in taken]
-    own = rows_of(rest, total, False, True)
+    own = rows_of(rest, total, True)
     first_term = finish(orbital_pieces, arrived, orbitals).astype(jnp.bfloat16)
     first_pieces, early = spread_out(first_term, first_products)
     second_term = (
-        2.0 * finish(first_pieces, send(first_pieces, early), first_term)
+        2.0 * finish(first_pieces, send(sums(first_pieces, early)), first_term)
         - orbitals.astype(jnp.float32)
     ).astype(jnp.bfloat16)
     second_pieces, early = spread_out(second_term, first_products)
-    return 2.0 * finish(second_pieces, send(second_pieces, early), second_term) - first_term.astype(
+    return 2.0 * finish(second_pieces, send(sums(second_pieces, early)), second_term) - first_term.astype(
         jnp.float32
     )
 

time: 220 us -> 211 us (0.959)
  local copies, waits for them, and re-layouts: 24 us -> 14.2 us
  Pallas kernels: 46.7 us -> 52.4 us
  waiting for transfers between devices: 67.4 us -> 64.3 us
    unnamed x71 -> x61, local copies, waits for them, and re-layouts: 21.9 us -> 7.69 us
    dynamic_slice x0 -> x1, local copies, waits for them, and re-layouts: none -> 4.68 us  [body(): lax.dynamic_slice_in_dim(kinetic, where[0] * shard_rows, shard_rows, 0)]
    pallas_call x6, Pallas kernels: 18 us -> 21.8 us  [early_product(): pl.pallas_call(functools.partial(early_kernel, len(masks)), out_shape=jax...]
    ppermute x44, waiting for transfers between devices: 67.4 us -> 64.3 us  [swap(): lax.ppermute(array, axis, [(i, i ^ mask) for i in range(lax.axis_size(axi...]
    pallas_call x2 -> x3, Pallas kernels: 13.5 us -> 14.4 us  [add_rows(): pl.pallas_call(functools.partial(rows_kernel, listed, shard_rows // TILE,...]
  transfers between devices with their start and end apart: 44 -> 44, of which waited for: 19 -> 15; matrix products, arithmetic and copies ran while one was open for 1% -> 3% of each run, Pallas kernels for 21% -> 24%
where the time goes in v4:
time: 211 us; the launch traced here: 212 us
  starting transfers between devices  76.6 us (36%)
  waiting for transfers between devices  64.3 us (30%)
  Pallas kernels  52.4 us (25%)
  local copies, waits for them, and re-layouts  14.2 us (7%)
  other arithmetic  3.77 us (2%)
    ppermute x44, starting transfers between devices, swap(): lax.ppermute(array, axis, [(i, i ^ mask) for i in range(lax.axis_size(axi...  76.6 us
    ppermute x44, waiting for transfers between devices, swap(): lax.ppermute(array, axis, [(i, i ^ mask) for i in range(lax.axis_size(axi...  64.3 us
    pallas_call x6, Pallas kernels, early_product(): pl.pallas_call(functools.partial(early_kernel, len(masks)), out_shape=jax...  21.8 us
    pallas_call x3, Pallas kernels, add_rows(): pl.pallas_call(functools.partial(rows_kernel, listed, shard_rows // TILE,...  14.4 us
    pallas_call x9, Pallas kernels, late_product(): pl.pallas_call(functools.partial(late_kernel, len(masks)), out_shape=jax....  10.7 us
    unnamed x61, local copies, waits for them, and re-layouts  7.69 us
    pallas_call x3, Pallas kernels, own_product(): pl.pallas_call(functools.partial(own_kernel, len(masks)), out_shape=jax.S...  5.42 us
    dynamic_slice x1, local copies, waits for them, and re-layouts, body(): lax.dynamic_slice_in_dim(kinetic, where[0] * shard_rows, shard_rows, 0)  4.68 us
  transfers between devices with their start and end apart: 44, of which 15 were waited for; matrix products, arithmetic and copies ran while one was open for 3% of the time, Pallas kernels for 24%

profile of v4, /device:TPU:0, one launch (start us, length us, event | category | flops | bytes accessed | tf_op | source)
XLA Modules:
  0.0 211.8 jit_solution(4005289853547962923)
XLA Ops:
  2.5 5.1 %collective-permute-start.3 = (bf16[528,256]{1,0:T(8,128)(2,1)S(1)}, bf16[528,256]{1,0:T(8,128)(2,1)S(1)}, u32[]{:S(2)}, u32[]{:S(2)}) collective-permute-start(bf16[528,256]{1,0:T(8,128)(2,1)S(1)} %constant_dynamic-update-slice_fusion.refs_0_.refs_4_.refs_8_), channel_id=1, source_target_pairs={{0,24},{4,28},{8,16},{12,20},{16,8},{20,12},{24,0},{28,4},{1,25},{... | collective-permute-start | bytes 811016 | tf_op jit(solution)/shard_map/ppermute | solution.py:36
  7.6 7.4 %collective-permute-done.3.refs_6_.refs_7_.refs_14_ = bf16[528,256]{1,0:T(8,128)(2,1)S(1)} collective-permute-done((bf16[528,256]{1,0:T(8,128)(2,1)S(1)}, bf16[528,256]{1,0:T(8,128)(2,1)S(1)}, u32[]{:S(2)}, u32[]{:S(2)}) %collective-permute-start.3) | collective-permute-done | bytes 270368 | tf_op jit(solution)/shard_map/ppermute | solution.py:36
  17.0 4.6 %collective-permute-start.4 = (bf16[528,256]{1,0:T(8,128)(2,1)S(1)}, bf16[528,256]{1,0:T(8,128)(2,1)S(1)}, u32[]{:S(2)}, u32[]{:S(2)}) collective-permute-start(bf16[528,256]{1,0:T(8,128)(2,1)S(1)} %collective-permute-done.3.refs_6_.refs_7_.refs_14_), channel_id=1, source_target_pairs={{0,8},{4,12},{8,0},{12,4},{16,24},{20,28},{24,16},{28,20},{1,9},{5... | collective-permute-start | bytes 811016 | tf_op jit(solution)/shard_map/ppermute | solution.py:36
  24.4 4.6 %collective-permute-start.6 = (bf16[528,256]{1,0:T(8,128)(2,1)S(1)}, bf16[528,256]{1,0:T(8,128)(2,1)S(1)}, u32[]{:S(2)}, u32[]{:S(2)}) collective-permute-start(bf16[528,256]{1,0:T(8,128)(2,1)S(1)} %collective-permute-done.5.refs_7_.refs_5_.refs_15_), channel_id=1, source_target_pairs={{0,8},{4,12},{8,0},{12,4},{16,24},{20,28},{24,16},{28,20},{1,9},{5... | collective-permute-start | bytes 811016 | tf_op jit(solution)/shard_map/ppermute | solution.py:36
  29.1 4.7 %constant_dynamic-slice_fusion.refs_7_ = bf16[512,4096]{1,0:T(8,128)(2,1)} fusion(bf16[2048,4096]{1,0:T(8,128)(2,1)} %refs_0_.29, s32[]{:T(128)S(6)} %select_n.3), kind=kLoop, calls=%fused_computation.33 | loop fusion | bytes 8388612 | tf_op jit(solution)/shard_map/dynamic_slice | solution.py:357
  34.6 2.5 %collective-permute-start.9 = (bf16[2,256,384]{2,1,0:T(8,128)(2,1)S(1)}, bf16[2,256,384]{2,1,0:T(8,128)(2,1)}, u32[]{:S(2)}, u32[]{:S(2)}) collective-permute-start(bf16[2,256,384]{2,1,0:T(8,128)(2,1)S(1)} %get-tuple-element.51.refs_0_), channel_id=1, source_target_pairs={{0,24},{4,28},{8,16},{12,20},{16,8},{20,12},{24,0},{28,4},{1,25},{... | collective-permute-start | bytes 1179656 | tf_op jit(solution)/shard_map/ppermute | solution.py:36
  37.1 3.0 %collective-permute-start.8 = (bf16[2,256,384]{2,1,0:T(8,128)(2,1)S(1)}, bf16[2,256,384]{2,1,0:T(8,128)(2,1)}, u32[]{:S(2)}, u32[]{:S(2)}) collective-permute-start(bf16[2,256,384]{2,1,0:T(8,128)(2,1)S(1)} %get-tuple-element.51.refs_0_), channel_id=1, source_target_pairs={{0,8},{4,12},{8,0},{12,4},{16,24},{20,28},{24,16},{28,20},{1,9},{5... | collective-permute-start | bytes 1179656 | tf_op jit(solution)/shard_map/ppermute | solution.py:36
  41.7 5.1 %shard_map.56.refs_6_ = f32[3,512,256]{2,1,0:T(8,128)S(1)} custom-call(s32[2]{0:T(128)S(1)} %pad_add_fusion.where_ref, bf16[2048,4096]{1,0:T(8,128)(2,1)} %refs_0_.29, bf16[2048,4096]{1,0:T(8,128)(2,1)} %refs_0_.29, bf16[2048,4096]{1,0:T(8,128)(2,1)} %refs_0_.29, bf16[2048,4096]{1,0:T(8,128)(2,1)} %refs_0_.29, ...), custom_call_target="tpu_custom_call" | custom-call | flops 1610612736 | bytes 6291456 | tf_op jit(solution)/shard_map/pallas_call | solution.py:200
  46.9 4.5 %shard_map.57.refs_2_ = f32[3,512,256]{2,1,0:T(8,128)S(1)} custom-call(s32[2]{0:T(128)S(1)} %pad_add_fusion.where_ref, bf16[2048,4096]{1,0:T(8,128)(2,1)} %refs_0_.29, bf16[2048,4096]{1,0:T(8,128)(2,1)} %refs_0_.29, bf16[2048,4096]{1,0:T(8,128)(2,1)} %refs_0_.29, bf16[528,256]{1,0:T(8,128)(2,1)S(1)} %collective-permute-done.2.refs_3_.refs_11_, ...), custom_call_target="tpu_custom_call" | custom-call | flops 1207959552 | bytes 4718592 | tf_op jit(solution)/shard_map/pallas_call | solution.py:200
  64.5 8.3 %collective-permute-done.15.refs_5_ = bf16[2,256,384]{2,1,0:T(8,128)(2,1)} collective-permute-done((bf16[2,256,384]{2,1,0:T(8,128)(2,1)}, bf16[2,256,384]{2,1,0:T(8,128)(2,1)}, u32[]{:S(2)}, u32[]{:S(2)}) %collective-permute-start.15) | collective-permute-done | bytes 393248 | tf_op jit(solution)/shard_map/ppermute | solution.py:36
  75.0 2.2 %copy-done = bf16[512,4096]{1,0:T(8,128)(2,1)S(1)} copy-done((bf16[512,4096]{1,0:T(8,128)(2,1)S(1)}, bf16[512,4096]{1,0:T(8,128)(2,1)}, u32[]{:S(2)}) %copy-start) | copy-done | bytes 4194328
  80.0 5.8 %shard_map.61.refs_8_ = f32[512,4096]{1,0:T(8,128)S(1)} custom-call(s32[2]{0:T(128)S(1)} %pad_add_fusion.where_ref, s32[96]{0:T(128)S(1)} %reshape.34.tiles_ref, bf16[2,256,384]{2,1,0:T(8,128)(2,1)S(1)} %copy-done.12, bf16[2,256,384]{2,1,0:T(8,128)(2,1)S(1)} %copy-done.14, bf16[2,256,384]{2,1,0:T(8,128)(2,1)} %collective-permute-done.8.refs_2_, ...), custom_call_target="tpu_custom_call" | custom-call | flops 251658240 | bytes 18743296 | tf_op jit(solution)/shard_map/pallas_call | solution.py:163
  88.0 4.8 %collective-permute-start.18 = (bf16[2,256,384]{2,1,0:T(8,128)(2,1)}, bf16[2,256,384]{2,1,0:T(8,128)(2,1)S(1)}, u32[]{:S(2)}, u32[]{:S(2)}) collective-permute-start(bf16[2,256,384]{2,1,0:T(8,128)(2,1)} %collective-permute-done.15.refs_5_), channel_id=1, source_target_pairs={{0,8},{4,12},{8,0},{12,4},{16,24},{20,28},{24,16},{28,20},{1,9},{5... | collective-permute-start | bytes 1179656 | tf_op jit(solution)/shard_map/ppermute | solution.py:36
  92.8 5.2 %shard_map.62.refs_7_ = f32[512,4096]{1,0:T(8,128)S(1)} custom-call(s32[2]{0:T(128)S(1)} %pad_add_fusion.where_ref, s32[96]{0:T(128)S(1)} %reshape.34.tiles_ref, bf16[2,256,384]{2,1,0:T(8,128)(2,1)} %collective-permute-done.10.refs_0_, bf16[2,256,384]{2,1,0:T(8,128)(2,1)} %collective-permute-done.11.refs_1_, ...), custom_call_target="tpu_custom_call" | custom-call | flops 301989888 | bytes 19136512 | tf_op jit(solution)/shard_map/pallas_call | solution.py:163
  98.3 7.1 %collective-permute-done.19.refs_4_ = bf16[2,256,384]{2,1,0:T(8,128)(2,1)S(1)} collective-permute-done((bf16[2,256,384]{2,1,0:T(8,128)(2,1)}, bf16[2,256,384]{2,1,0:T(8,128)(2,1)S(1)}, u32[]{:S(2)}, u32[]{:S(2)}) %collective-permute-start.19) | collective-permute-done | bytes 393248 | tf_op jit(solution)/shard_map/ppermute | solution.py:36
  108.8 6.5 %collective-permute-done.20.refs_3_ = bf16[2,256,384]{2,1,0:T(8,128)(2,1)S(1)} collective-permute-done((bf16[2,256,384]{2,1,0:T(8,128)(2,1)S(1)}, bf16[2,256,384]{2,1,0:T(8,128)(2,1)S(1)}, u32[]{:S(2)}, u32[]{:S(2)}) %collective-permute-start.20) | collective-permute-done | bytes 393248 | tf_op jit(solution)/shard_map/ppermute | solution.py:36
  115.3 3.3 %shard_map.63.refs_0_.refs_1_.refs_2_.refs_3_.refs_4_.refs_5_.refs_6_.refs_7_ = bf16[512,4096]{1,0:T(8,128)(2,1)S(1)} custom-call(s32[2]{0:T(128)S(1)} %pad_add_fusion.where_ref, s32[96]{0:T(128)S(1)} %reshape.34.tiles_ref, bf16[2,256,384]{2,1,0:T(8,128)(2,1)S(1)} %collective-permute-done.16.refs_0_, ...), custom_call_target="tpu_custom_call" | custom-call | flops 251658240 | bytes 18743296 | tf_op jit(solution)/shard_map/pallas_call | solution.py:163
  124.9 7.5 %collective-permute-done.27.refs_7_.refs_14_ = bf16[512,256]{1,0:T(8,128)(2,1)S(1)} collective-permute-done((bf16[512,256]{1,0:T(8,128)(2,1)S(1)}, bf16[512,256]{1,0:T(8,128)(2,1)S(1)}, u32[]{:S(2)}, u32[]{:S(2)}) %collective-permute-start.27) | collective-permute-done | bytes 262176 | tf_op jit(solution)/shard_map/ppermute | solution.py:36
  133.8 3.9 %collective-permute-start.28 = (bf16[512,256]{1,0:T(8,128)(2,1)S(1)}, bf16[512,256]{1,0:T(8,128)(2,1)S(1)}, u32[]{:S(2)}, u32[]{:S(2)}) collective-permute-start(bf16[512,256]{1,0:T(8,128)(2,1)S(1)} %collective-permute-done.27.refs_7_.refs_14_), channel_id=1, source_target_pairs={{0,8},{4,12},{8,0},{12,4},{16,24},{20,28},{24,16},{28,20},{1,9},{5... | collective-permute-start | bytes 786440 | tf_op jit(solution)/shard_map/ppermute | solution.py:36
  139.7 3.4 %shard_map.65.refs_6_ = f32[3,512,256]{2,1,0:T(8,128)S(1)} custom-call(s32[2]{0:T(128)S(1)} %pad_add_fusion.where_ref, bf16[2048,4096]{1,0:T(8,128)(2,1)S(1)} %bitcast.15, bf16[2048,4096]{1,0:T(8,128)(2,1)S(1)} %bitcast.15, bf16[2048,4096]{1,0:T(8,128)(2,1)S(1)} %bitcast.15, bf16[2048,4096]{1,0:T(8,128)(2,1)S(1)} %bitcast.15, ...), custom_call_target="tpu_custom_call" | custom-call | flops 1610612736 | bytes 6291456 | tf_op jit(solution)/shard_map/pallas_call | solution.py:200
  143.2 3.6 %collective-permute-start.30 = (bf16[512,256]{1,0:T(8,128)(2,1)S(1)}, bf16[512,256]{1,0:T(8,128)(2,1)S(1)}, u32[]{:S(2)}, u32[]{:S(2)}) collective-permute-start(bf16[512,256]{1,0:T(8,128)(2,1)S(1)} %collective-permute-done.29.refs_15_.refs_5_), channel_id=1, source_target_pairs={{0,8},{4,12},{8,0},{12,4},{16,24},{20,28},{24,16},{28,20},{1,9},{5... | collective-permute-start | bytes 786440 | tf_op jit(solution)/shard_map/ppermute | solution.py:36
  146.8 2.7 %shard_map.67.refs_2_ = f32[3,512,256]{2,1,0:T(8,128)S(1)} custom-call(s32[2]{0:T(128)S(1)} %pad_add_fusion.where_ref, bf16[2048,4096]{1,0:T(8,128)(2,1)S(1)} %bitcast.15, bf16[2048,4096]{1,0:T(8,128)(2,1)S(1)} %bitcast.15, bf16[2048,4096]{1,0:T(8,128)(2,1)S(1)} %bitcast.15, bf16[512,256]{1,0:T(8,128)(2,1)S(1)} %collective-permute-done.26.refs_11_.refs_3_, ...), custom_call_target="tpu_custom_call" | custom-call | flops 1207959552 | bytes 4718592 | tf_op jit(solution)/shard_map/pallas_call | solution.py:200
  157.9 3.1 %collective-permute-done.31 = bf16[512,256]{1,0:T(8,128)(2,1)S(1)} collective-permute-done((bf16[512,256]{1,0:T(8,128)(2,1)S(1)}, bf16[512,256]{1,0:T(8,128)(2,1)S(1)}, u32[]{:S(2)}, u32[]{:S(2)}) %collective-permute-start.31) | collective-permute-done | bytes 262176 | tf_op jit(solution)/shard_map/ppermute | solution.py:36
  161.0 3.4 %collective-permute-done.32 = bf16[512,256]{1,0:T(8,128)(2,1)S(1)} collective-permute-done((bf16[512,256]{1,0:T(8,128)(2,1)S(1)}, bf16[512,256]{1,0:T(8,128)(2,1)S(1)}, u32[]{:S(2)}, u32[]{:S(2)}) %collective-permute-start.32) | collective-permute-done | bytes 262176 | tf_op jit(solution)/shard_map/ppermute | solution.py:36
  164.7 2.7 %collective-permute-start.37 = (bf16[512,256]{1,0:T(8,128)(2,1)S(1)}, bf16[512,256]{1,0:T(8,128)(2,1)S(1)}, u32[]{:S(2)}, u32[]{:S(2)}) collective-permute-start(bf16[512,256]{1,0:T(8,128)(2,1)S(1)} %fusion.2.refs_4_.refs_8_), channel_id=1, source_target_pairs={{0,24},{4,28},{8,16},{12,20},{16,8},{20,12},{24,0},{28,4},{1,25},{... | collective-permute-start | bytes 786440 | tf_op jit(solution)/shard_map/ppermute | solution.py:36
  169.5 6.3 %collective-permute-done.37.refs_7_.refs_14_ = bf16[512,256]{1,0:T(8,128)(2,1)S(1)} collective-permute-done((bf16[512,256]{1,0:T(8,128)(2,1)S(1)}, bf16[512,256]{1,0:T(8,128)(2,1)S(1)}, u32[]{:S(2)}, u32[]{:S(2)}) %collective-permute-start.37) | collective-permute-done | bytes 262176 | tf_op jit(solution)/shard_map/ppermute | solution.py:36
  176.4 6.0 %collective-permute-start.38 = (bf16[512,256]{1,0:T(8,128)(2,1)S(1)}, bf16[512,256]{1,0:T(8,128)(2,1)S(1)}, u32[]{:S(2)}, u32[]{:S(2)}) collective-permute-start(bf16[512,256]{1,0:T(8,128)(2,1)S(1)} %collective-permute-done.37.refs_7_.refs_14_), channel_id=1, source_target_pairs={{0,8},{4,12},{8,0},{12,4},{16,24},{20,28},{24,16},{28,20},{1,9},{5... | collective-permute-start | bytes 786440 | tf_op jit(solution)/shard_map/ppermute | solution.py:36
  183.8 3.3 %shard_map.71.refs_6_ = f32[3,512,256]{2,1,0:T(8,128)S(1)} custom-call(s32[2]{0:T(128)S(1)} %pad_add_fusion.where_ref, bf16[2048,4096]{1,0:T(8,128)(2,1)S(1)} %bitcast.15, bf16[2048,4096]{1,0:T(8,128)(2,1)S(1)} %bitcast.15, bf16[2048,4096]{1,0:T(8,128)(2,1)S(1)} %bitcast.15, bf16[2048,4096]{1,0:T(8,128)(2,1)S(1)} %bitcast.15, ...), custom_call_target="tpu_custom_call" | custom-call | flops 1610612736 | bytes 6291456 | tf_op jit(solution)/shard_map/pallas_call | solution.py:200
  187.1 3.9 %collective-permute-start.40 = (bf16[512,256]{1,0:T(8,128)(2,1)S(1)}, bf16[512,256]{1,0:T(8,128)(2,1)S(1)}, u32[]{:S(2)}, u32[]{:S(2)}) collective-permute-start(bf16[512,256]{1,0:T(8,128)(2,1)S(1)} %collective-permute-done.39.refs_15_.refs_5_), channel_id=1, source_target_pairs={{0,8},{4,12},{8,0},{12,4},{16,24},{20,28},{24,16},{28,20},{1,9},{5... | collective-permute-start | bytes 786440 | tf_op jit(solution)/shard_map/ppermute | solution.py:36
  191.0 2.7 %shard_map.73.refs_2_ = f32[3,512,256]{2,1,0:T(8,128)S(1)} custom-call(s32[2]{0:T(128)S(1)} %pad_add_fusion.where_ref, bf16[2048,4096]{1,0:T(8,128)(2,1)S(1)} %bitcast.15, bf16[2048,4096]{1,0:T(8,128)(2,1)S(1)} %bitcast.15, bf16[2048,4096]{1,0:T(8,128)(2,1)S(1)} %bitcast.15, bf16[512,256]{1,0:T(8,128)(2,1)S(1)} %collective-permute-done.36.refs_11_.refs_3_, ...), custom_call_target="tpu_custom_call" | custom-call | flops 1207959552 | bytes 4718592 | tf_op jit(solution)/shard_map/pallas_call | solution.py:200
  202.1 3.1 %collective-permute-done.41 = bf16[512,256]{1,0:T(8,128)(2,1)S(1)} collective-permute-done((bf16[512,256]{1,0:T(8,128)(2,1)S(1)}, bf16[512,256]{1,0:T(8,128)(2,1)S(1)}, u32[]{:S(2)}, u32[]{:S(2)}) %collective-permute-start.41) | collective-permute-done | bytes 262176 | tf_op jit(solution)/shard_map/ppermute | solution.py:36
  205.2 5.5 %collective-permute-done.42 = bf16[512,256]{1,0:T(8,128)(2,1)S(1)} collective-permute-done((bf16[512,256]{1,0:T(8,128)(2,1)S(1)}, bf16[512,256]{1,0:T(8,128)(2,1)S(1)}, u32[]{:S(2)}, u32[]{:S(2)}) %collective-permute-start.42) | collective-permute-done | bytes 262176 | tf_op jit(solution)/shard_map/ppermute | solution.py:36
  (157 shorter events, 65.2 us)
Async XLA Ops:
  2.5 12.5 %collective-permute-start.3 = (bf16[528,256]{1,0:T(8,128)(2,1)S(1)}, bf16[528,256]{1,0:T(8,128)(2,1)S(1)}, u32[]{:S(2)}, u32[]{:S(2)}) collective-permute-start(bf16[528,256]{1,0:T(8,128)(2,1)S(1)} %constant_dynamic-update-slice_fusion.refs_0_.refs_4_.refs_8_), channel_id=1, source_target_pairs={{0,24},{4,28},{8,16},{12,20},{16,8},{20,12},{24,0},{28,4},{1,25},{... | collective-permute-start | bytes 811016 | tf_op jit(solution)/shard_map/ppermute | solution.py:36
  7.6 14.0 %collective-permute-start.1 = (bf16[528,256]{1,0:T(8,128)(2,1)S(1)}, bf16[528,256]{1,0:T(8,128)(2,1)S(1)}, u32[]{:S(2)}, u32[]{:S(2)}) collective-permute-start(bf16[528,256]{1,0:T(8,128)(2,1)S(1)} %constant_dynamic-update-slice_fusion.refs_0_.refs_4_.refs_8_), channel_id=1, source_target_pairs={{0,8},{4,12},{8,0},{12,4},{16,24},{20,28},{24,16},{28,20},{1,9},{5... | collective-permute-start | bytes 811016 | tf_op jit(solution)/shard_map/ppermute | solution.py:36
  16.7 17.8 %collective-permute-start = (bf16[528,256]{1,0:T(8,128)(2,1)S(1)}, bf16[528,256]{1,0:T(8,128)(2,1)S(1)}, u32[]{:S(2)}, u32[]{:S(2)}) collective-permute-start(bf16[528,256]{1,0:T(8,128)(2,1)S(1)} %constant_dynamic-update-slice_fusion.refs_0_.refs_4_.refs_8_), channel_id=1, source_target_pairs={{0,4},{4,0},{8,12},{12,8},{16,20},{20,16},{24,28},{28,24},{1,5},{5... | collective-permute-start | bytes 811016 | tf_op jit(solution)/shard_map/ppermute | solution.py:36
  17.0 17.5 %collective-permute-start.4 = (bf16[528,256]{1,0:T(8,128)(2,1)S(1)}, bf16[528,256]{1,0:T(8,128)(2,1)S(1)}, u32[]{:S(2)}, u32[]{:S(2)}) collective-permute-start(bf16[528,256]{1,0:T(8,128)(2,1)S(1)} %collective-permute-done.3.refs_6_.refs_7_.refs_14_), channel_id=1, source_target_pairs={{0,8},{4,12},{8,0},{12,4},{16,24},{20,28},{24,16},{28,20},{1,9},{5... | collective-permute-start | bytes 811016 | tf_op jit(solution)/shard_map/ppermute | solution.py:36
  21.7 12.9 %collective-permute-start.2 = (bf16[528,256]{1,0:T(8,128)(2,1)S(1)}, bf16[528,256]{1,0:T(8,128)(2,1)S(1)}, u32[]{:S(2)}, u32[]{:S(2)}) collective-permute-start(bf16[528,256]{1,0:T(8,128)(2,1)S(1)} %collective-permute-done.1.refs_2_.refs_6_.refs_10_), channel_id=1, source_target_pairs={{0,4},{4,0},{8,12},{12,8},{16,20},{20,16},{24,28},{28,24},{1,5},{5... | collective-permute-start | bytes 811016 | tf_op jit(solution)/shard_map/ppermute | solution.py:36
  34.6 23.2 %collective-permute-start.9 = (bf16[2,256,384]{2,1,0:T(8,128)(2,1)S(1)}, bf16[2,256,384]{2,1,0:T(8,128)(2,1)}, u32[]{:S(2)}, u32[]{:S(2)}) collective-permute-start(bf16[2,256,384]{2,1,0:T(8,128)(2,1)S(1)} %get-tuple-element.51.refs_0_), channel_id=1, source_target_pairs={{0,24},{4,28},{8,16},{12,20},{16,8},{20,12},{24,0},{28,4},{1,25},{... | collective-permute-start | bytes 1179656 | tf_op jit(solution)/shard_map/ppermute | solution.py:36
  37.1 20.7 %collective-permute-start.8 = (bf16[2,256,384]{2,1,0:T(8,128)(2,1)S(1)}, bf16[2,256,384]{2,1,0:T(8,128)(2,1)}, u32[]{:S(2)}, u32[]{:S(2)}) collective-permute-start(bf16[2,256,384]{2,1,0:T(8,128)(2,1)S(1)} %get-tuple-element.51.refs_0_), channel_id=1, source_target_pairs={{0,8},{4,12},{8,0},{12,4},{16,24},{20,28},{24,16},{28,20},{1,9},{5... | collective-permute-start | bytes 1179656 | tf_op jit(solution)/shard_map/ppermute | solution.py:36
  40.1 17.7 %collective-permute-start.7 = (bf16[2,256,384]{2,1,0:T(8,128)(2,1)S(1)}, bf16[2,256,384]{2,1,0:T(8,128)(2,1)S(1)}, u32[]{:S(2)}, u32[]{:S(2)}) collective-permute-start(bf16[2,256,384]{2,1,0:T(8,128)(2,1)S(1)} %get-tuple-element.51.refs_0_), channel_id=1, source_target_pairs={{0,4},{4,0},{8,12},{12,8},{16,20},{20,16},{24,28},{28,24},{1,5},{5... | collective-permute-start | bytes 1179656 | tf_op jit(solution)/shard_map/ppermute | solution.py:36
  58.6 14.2 %collective-permute-start.15 = (bf16[2,256,384]{2,1,0:T(8,128)(2,1)}, bf16[2,256,384]{2,1,0:T(8,128)(2,1)}, u32[]{:S(2)}, u32[]{:S(2)}) collective-permute-start(bf16[2,256,384]{2,1,0:T(8,128)(2,1)} %get-tuple-element.57.refs_4_), channel_id=1, source_target_pairs={{0,24},{4,28},{8,16},{12,20},{16,8},{20,12},{24,0},{28,4},{1,25},{... | collective-permute-start | bytes 1179656 | tf_op jit(solution)/shard_map/ppermute | solution.py:36
  60.4 25.5 %collective-permute-start.14 = (bf16[2,256,384]{2,1,0:T(8,128)(2,1)}, bf16[2,256,384]{2,1,0:T(8,128)(2,1)}, u32[]{:S(2)}, u32[]{:S(2)}) collective-permute-start(bf16[2,256,384]{2,1,0:T(8,128)(2,1)} %get-tuple-element.57.refs_4_), channel_id=1, source_target_pairs={{0,8},{4,12},{8,0},{12,4},{16,24},{20,28},{24,16},{28,20},{1,9},{5... | collective-permute-start | bytes 1179656 | tf_op jit(solution)/shard_map/ppermute | solution.py:36
  60.5 25.4 %collective-permute-start.13 = (bf16[2,256,384]{2,1,0:T(8,128)(2,1)}, bf16[2,256,384]{2,1,0:T(8,128)(2,1)}, u32[]{:S(2)}, u32[]{:S(2)}) collective-permute-start(bf16[2,256,384]{2,1,0:T(8,128)(2,1)} %get-tuple-element.57.refs_4_), channel_id=1, source_target_pairs={{0,4},{4,0},{8,12},{12,8},{16,20},{20,16},{24,28},{28,24},{1,5},{5... | collective-permute-start | bytes 1179656 | tf_op jit(solution)/shard_map/ppermute | solution.py:36
  61.0 24.9 %collective-permute-start.12 = (bf16[2,256,384]{2,1,0:T(8,128)(2,1)}, bf16[2,256,384]{2,1,0:T(8,128)(2,1)}, u32[]{:S(2)}, u32[]{:S(2)}) collective-permute-start(bf16[2,256,384]{2,1,0:T(8,128)(2,1)} %collective-permute-done.9.refs_3_), channel_id=1, source_target_pairs={{0,4},{4,0},{8,12},{12,8},{16,20},{20,16},{24,28},{28,24},{1,5},{5... | collective-permute-start | bytes 1179656 | tf_op jit(solution)/shard_map/ppermute | solution.py:36
  62.6 23.4 %collective-permute-start.11 = (bf16[2,256,384]{2,1,0:T(8,128)(2,1)}, bf16[2,256,384]{2,1,0:T(8,128)(2,1)}, u32[]{:S(2)}, u32[]{:S(2)}) collective-permute-start(bf16[2,256,384]{2,1,0:T(8,128)(2,1)} %collective-permute-done.9.refs_3_), channel_id=1, source_target_pairs={{0,8},{4,12},{8,0},{12,4},{16,24},{20,28},{24,16},{28,20},{1,9},{5... | collective-permute-start | bytes 1179656 | tf_op jit(solution)/shard_map/ppermute | solution.py:36
  72.8 13.2 %collective-permute-start.10 = (bf16[2,256,384]{2,1,0:T(8,128)(2,1)}, bf16[2,256,384]{2,1,0:T(8,128)(2,1)}, u32[]{:S(2)}, u32[]{:S(2)}) collective-permute-start(bf16[2,256,384]{2,1,0:T(8,128)(2,1)} %collective-permute-done.8.refs_2_), channel_id=1, source_target_pairs={{0,4},{4,0},{8,12},{12,8},{16,20},{20,16},{24,28},{28,24},{1,5},{5... | collective-permute-start | bytes 1179656 | tf_op jit(solution)/shard_map/ppermute | solution.py:36
  86.0 12.3 %collective-permute-start.17 = (bf16[2,256,384]{2,1,0:T(8,128)(2,1)}, bf16[2,256,384]{2,1,0:T(8,128)(2,1)S(1)}, u32[]{:S(2)}, u32[]{:S(2)}) collective-permute-start(bf16[2,256,384]{2,1,0:T(8,128)(2,1)} %collective-permute-done.14.refs_4_), channel_id=1, source_target_pairs={{0,4},{4,0},{8,12},{12,8},{16,20},{20,16},{24,28},{28,24},{1,5},{5... | collective-permute-start | bytes 1179656 | tf_op jit(solution)/shard_map/ppermute | solution.py:36
  87.0 18.4 %collective-permute-start.19 = (bf16[2,256,384]{2,1,0:T(8,128)(2,1)}, bf16[2,256,384]{2,1,0:T(8,128)(2,1)S(1)}, u32[]{:S(2)}, u32[]{:S(2)}) collective-permute-start(bf16[2,256,384]{2,1,0:T(8,128)(2,1)} %collective-permute-done.15.refs_5_), channel_id=1, source_target_pairs={{0,4},{4,0},{8,12},{12,8},{16,20},{20,16},{24,28},{28,24},{1,5},{5... | collective-permute-start | bytes 1179656 | tf_op jit(solution)/shard_map/ppermute | solution.py:36
  88.0 17.3 %collective-permute-start.18 = (bf16[2,256,384]{2,1,0:T(8,128)(2,1)}, bf16[2,256,384]{2,1,0:T(8,128)(2,1)S(1)}, u32[]{:S(2)}, u32[]{:S(2)}) collective-permute-start(bf16[2,256,384]{2,1,0:T(8,128)(2,1)} %collective-permute-done.15.refs_5_), channel_id=1, source_target_pairs={{0,8},{4,12},{8,0},{12,4},{16,24},{20,28},{24,16},{28,20},{1,9},{5... | collective-permute-start | bytes 1179656 | tf_op jit(solution)/shard_map/ppermute | solution.py:36
  92.8 16.0 %collective-permute-start.16 = (bf16[2,256,384]{2,1,0:T(8,128)(2,1)}, bf16[2,256,384]{2,1,0:T(8,128)(2,1)S(1)}, u32[]{:S(2)}, u32[]{:S(2)}) collective-permute-start(bf16[2,256,384]{2,1,0:T(8,128)(2,1)} %collective-permute-done.12.refs_2_), channel_id=1, source_target_pairs={{0,8},{4,12},{8,0},{12,4},{16,24},{20,28},{24,16},{28,20},{1,9},{5... | collective-permute-start | bytes 1179656 | tf_op jit(solution)/shard_map/ppermute | solution.py:36
  106.9 13.6 %collective-permute-start.21 = (bf16[512,256]{1,0:T(8,128)(2,1)S(1)}, bf16[512,256]{1,0:T(8,128)(2,1)S(1)}, u32[]{:S(2)}, u32[]{:S(2)}) collective-permute-start(bf16[512,256]{1,0:T(8,128)(2,1)S(1)} %copy-done.20), channel_id=1, source_target_pairs={{0,3},{1,2},{2,1},{3,0},{4,7},{5,6},{6,5},{7,4},{8,11},{9,10},{10,... | collective-permute-start | bytes 786440 | tf_op jit(solution)/shard_map/ppermute | solution.py:36
  106.9 14.2 %collective-permute-start.22 = (bf16[512,256]{1,0:T(8,128)(2,1)S(1)}, bf16[512,256]{1,0:T(8,128)(2,1)S(1)}, u32[]{:S(2)}, u32[]{:S(2)}) collective-permute-start(bf16[512,256]{1,0:T(8,128)(2,1)S(1)} %copy-done.18), channel_id=1, source_target_pairs={{0,2},{1,3},{2,0},{3,1},{4,6},{5,7},{6,4},{7,5},{8,10},{9,11},{10,... | collective-permute-start | bytes 786440 | tf_op jit(solution)/shard_map/ppermute | solution.py:36
  108.5 12.6 %collective-permute-start.23 = (bf16[512,256]{1,0:T(8,128)(2,1)S(1)}, bf16[512,256]{1,0:T(8,128)(2,1)S(1)}, u32[]{:S(2)}, u32[]{:S(2)}) collective-permute-start(bf16[512,256]{1,0:T(8,128)(2,1)S(1)} %copy-done.16), channel_id=1, source_target_pairs={{0,1},{1,0},{2,3},{3,2},{4,5},{5,4},{6,7},{7,6},{8,9},{9,8},{10,11... | collective-permute-start | bytes 786440 | tf_op jit(solution)/shard_map/ppermute | solution.py:36
  121.3 11.1 %collective-permute-start.27 = (bf16[512,256]{1,0:T(8,128)(2,1)S(1)}, bf16[512,256]{1,0:T(8,128)(2,1)S(1)}, u32[]{:S(2)}, u32[]{:S(2)}) collective-permute-start(bf16[512,256]{1,0:T(8,128)(2,1)S(1)} %fusion.1.refs_4_.refs_8_), channel_id=1, source_target_pairs={{0,24},{4,28},{8,16},{12,20},{16,8},{20,12},{24,0},{28,4},{1,25},{... | collective-permute-start | bytes 786440 | tf_op jit(solution)/shard_map/ppermute | solution.py:36
  123.3 14.4 %collective-permute-start.25 = (bf16[512,256]{1,0:T(8,128)(2,1)S(1)}, bf16[512,256]{1,0:T(8,128)(2,1)S(1)}, u32[]{:S(2)}, u32[]{:S(2)}) collective-permute-start(bf16[512,256]{1,0:T(8,128)(2,1)S(1)} %fusion.1.refs_4_.refs_8_), channel_id=1, source_target_pairs={{0,8},{4,12},{8,0},{12,4},{16,24},{20,28},{24,16},{28,20},{1,9},{5... | collective-permute-start | bytes 786440 | tf_op jit(solution)/shard_map/ppermute | solution.py:36
  124.6 15.0 %collective-permute-start.24 = (bf16[512,256]{1,0:T(8,128)(2,1)S(1)}, bf16[512,256]{1,0:T(8,128)(2,1)S(1)}, u32[]{:S(2)}, u32[]{:S(2)}) collective-permute-start(bf16[512,256]{1,0:T(8,128)(2,1)S(1)} %fusion.1.refs_4_.refs_8_), channel_id=1, source_target_pairs={{0,4},{4,0},{8,12},{12,8},{16,20},{20,16},{24,28},{28,24},{1,5},{5... | collective-permute-start | bytes 786440 | tf_op jit(solution)/shard_map/ppermute | solution.py:36
  133.8 13.0 %collective-permute-start.28 = (bf16[512,256]{1,0:T(8,128)(2,1)S(1)}, bf16[512,256]{1,0:T(8,128)(2,1)S(1)}, u32[]{:S(2)}, u32[]{:S(2)}) collective-permute-start(bf16[512,256]{1,0:T(8,128)(2,1)S(1)} %collective-permute-done.27.refs_7_.refs_14_), channel_id=1, source_target_pairs={{0,8},{4,12},{8,0},{12,4},{16,24},{20,28},{24,16},{28,20},{1,9},{5... | collective-permute-start | bytes 786440 | tf_op jit(solution)/shard_map/ppermute | solution.py:36
  153.3 11.2 %collective-permute-start.32 = (bf16[512,256]{1,0:T(8,128)(2,1)S(1)}, bf16[512,256]{1,0:T(8,128)(2,1)S(1)}, u32[]{:S(2)}, u32[]{:S(2)}) collective-permute-start(bf16[512,256]{1,0:T(8,128)(2,1)S(1)} %shard_map.69), channel_id=1, source_target_pairs={{0,2},{1,3},{2,0},{3,1},{4,6},{5,7},{6,4},{7,5},{8,10},{9,11},{10,... | collective-permute-start | bytes 786440 | tf_op jit(solution)/shard_map/ppermute | solution.py:36
  164.7 11.1 %collective-permute-start.37 = (bf16[512,256]{1,0:T(8,128)(2,1)S(1)}, bf16[512,256]{1,0:T(8,128)(2,1)S(1)}, u32[]{:S(2)}, u32[]{:S(2)}) collective-permute-start(bf16[512,256]{1,0:T(8,128)(2,1)S(1)} %fusion.2.refs_4_.refs_8_), channel_id=1, source_target_pairs={{0,24},{4,28},{8,16},{12,20},{16,8},{20,12},{24,0},{28,4},{1,25},{... | collective-permute-start | bytes 786440 | tf_op jit(solution)/shard_map/ppermute | solution.py:36
  167.4 15.0 %collective-permute-start.35 = (bf16[512,256]{1,0:T(8,128)(2,1)S(1)}, bf16[512,256]{1,0:T(8,128)(2,1)S(1)}, u32[]{:S(2)}, u32[]{:S(2)}) collective-permute-start(bf16[512,256]{1,0:T(8,128)(2,1)S(1)} %fusion.2.refs_4_.refs_8_), channel_id=1, source_target_pairs={{0,8},{4,12},{8,0},{12,4},{16,24},{20,28},{24,16},{28,20},{1,9},{5... | collective-permute-start | bytes 786440 | tf_op jit(solution)/shard_map/ppermute | solution.py:36
  169.2 14.6 %collective-permute-start.34 = (bf16[512,256]{1,0:T(8,128)(2,1)S(1)}, bf16[512,256]{1,0:T(8,128)(2,1)S(1)}, u32[]{:S(2)}, u32[]{:S(2)}) collective-permute-start(bf16[512,256]{1,0:T(8,128)(2,1)S(1)} %fusion.2.refs_4_.refs_8_), channel_id=1, source_target_pairs={{0,4},{4,0},{8,12},{12,8},{16,20},{20,16},{24,28},{28,24},{1,5},{5... | collective-permute-start | bytes 786440 | tf_op jit(solution)/shard_map/ppermute | solution.py:36
  175.8 11.3 %collective-permute-start.39 = (bf16[512,256]{1,0:T(8,128)(2,1)S(1)}, bf16[512,256]{1,0:T(8,128)(2,1)S(1)}, u32[]{:S(2)}, u32[]{:S(2)}) collective-permute-start(bf16[512,256]{1,0:T(8,128)(2,1)S(1)} %collective-permute-done.37.refs_7_.refs_14_), channel_id=1, source_target_pairs={{0,4},{4,0},{8,12},{12,8},{16,20},{20,16},{24,28},{28,24},{1,5},{5... | collective-permute-start | bytes 786440 | tf_op jit(solution)/shard_map/ppermute | solution.py:36
  176.4 14.6 %collective-permute-start.38 = (bf16[512,256]{1,0:T(8,128)(2,1)S(1)}, bf16[512,256]{1,0:T(8,128)(2,1)S(1)}, u32[]{:S(2)}, u32[]{:S(2)}) collective-permute-start(bf16[512,256]{1,0:T(8,128)(2,1)S(1)} %collective-permute-done.37.refs_7_.refs_14_), channel_id=1, source_target_pairs={{0,8},{4,12},{8,0},{12,4},{16,24},{20,28},{24,16},{28,20},{1,9},{5... | collective-permute-start | bytes 786440 | tf_op jit(solution)/shard_map/ppermute | solution.py:36
  197.5 13.3 %collective-permute-start.42 = (bf16[512,256]{1,0:T(8,128)(2,1)S(1)}, bf16[512,256]{1,0:T(8,128)(2,1)S(1)}, u32[]{:S(2)}, u32[]{:S(2)}) collective-permute-start(bf16[512,256]{1,0:T(8,128)(2,1)S(1)} %shard_map.75), channel_id=1, source_target_pairs={{0,2},{1,3},{2,0},{3,1},{4,6},{5,7},{6,4},{7,5},{8,10},{9,11},{10,... | collective-permute-start | bytes 786440 | tf_op jit(solution)/shard_map/ppermute | solution.py:36
  (40 other events, 446.8 us)

commit v5 on v4

--- a/solution.py
+++ b/solution.py
@@ -51,14 +51,23 @@
     return pieces, between(pieces) if result is None else result
 
 
-def hop(pieces, hops, after):
-    order, depth = routes(lax.axis_size("row"))
+def hop(pieces, chosen, after):
     held, after = lax.optimization_barrier((dict(pieces), after))
     pieces.update(held)
-    for mask, source, step in order:
-        if depth[mask] == hops:
-            pieces[mask] = swap(pieces[source], "row", step)
+    for mask, source, step in chosen:
+        pieces[mask] = swap(pieces[source], "row", step)
     return after
+
+
+def turns(count):
+    order, _ = routes(count)
+    near = [route for route in order if route[0] % 2 == 0 and route[1] == 0]
+    side = [route for route in order if route[0] == 1]
+    near_side = [(mask + 1, mask, 1) for mask, _, _ in near]
+    far = [route for route in order if route[0] % 2 == 0 and route[1] != 0]
+    far_side = [route for route in order if route[0] - 1 in [mask for mask, _, _ in far]]
+    last_side = [(mask + 1, mask, 1) for mask, _, _ in far]
+    return [near + side, near_side, far, far_side], [side, near, near_side + far, last_side]
 
 
 def noted(orbitals, external, tiles):
@@ -151,31 +160,35 @@
         out_ref[...] = total[...].astype(jnp.bfloat16)
 
 
-def add_rows(where, tiles, pieces, firsts, external, held, start, last_call):
+def add_rows(where, tiles, pieces, firsts, external, held, start, shard_rows, last_call):
     batches, points, length = pieces[0].shape
     listed = length // TILE
-    shard_rows, width = start.shape
+    width = start.shape[1]
+    groups = shard_rows // TILE
+    first_call = start.shape[0] != shard_rows
     once = pl.Buffered(1)
     whole = pl.BlockSpec(
         (batches, points, length), lambda i, w, t: (0, 0, 0), pipeline_mode=once
     )
     rows = pl.BlockSpec((TILE, width), lambda i, w, t: (i, 0))
     return pl.pallas_call(
-        functools.partial(rows_kernel, listed, shard_rows // TILE, firsts, last_call),
-        out_shape=jax.ShapeDtypeStruct(start.shape, jnp.bfloat16 if last_call else jnp.float32),
+        functools.partial(rows_kernel, listed, groups, firsts, last_call),
+        out_shape=jax.ShapeDtypeStruct((shard_rows, width), jnp.bfloat16 if last_call else jnp.float32),
         grid_spec=pltpu.PrefetchScalarGridSpec(
             num_scalar_prefetch=2,
-            grid=(shard_rows // TILE,),
+            grid=(groups,),
             in_specs=[whole for _ in firsts]
             + [
                 pl.BlockSpec(external.shape, lambda i, w, t: (0, 0)),
                 pl.BlockSpec(held.shape, lambda i, w, t: (0, 0, 0), pipeline_mode=once),
-                rows,
+                pl.BlockSpec((TILE, width), lambda i, w, t: (w[0] * groups + i, 0))
+                if first_call
+                else rows,
             ],
             out_specs=rows,
             scratch_shapes=[pltpu.VMEM((TILE, width) if last_call else (8, TILE), jnp.float32)],
         ),
-        compiler_params=pltpu.CompilerParams(vmem_limit_bytes=SMALL_LIMIT),
+        compiler_params=pltpu.CompilerParams(vmem_limit_bytes=LARGE_LIMIT if first_call else SMALL_LIMIT),
         cost_estimate=pl.CostEstimate(
             flops=len(firsts) * batches * 2 * points * length * TILE,
             bytes_accessed=2 * len(firsts) * batches * points * length + shard_rows * width * 8,
@@ -308,10 +321,12 @@
     def first_products(pieces, limit=SMALL_LIMIT):
         return early_product(where, kinetic, [pieces[m] for m in soon], soon, col_count - 1, limit)
 
-    def sums(pieces, early, limit=SMALL_LIMIT):
-        early = early_product(
+    def second_products(pieces, early, limit=SMALL_LIMIT):
+        return early_product(
             where, kinetic, [pieces[m] for m in middle], middle, col_count - 1, limit, early
         )
+
+    def sums(pieces, early, limit=SMALL_LIMIT):
         return [
             late_product(where, kinetic, [pieces[m] for m in last], last, early, partner, limit)
             for partner in range(col_count - 1, 0, -1)
@@ -343,6 +358,7 @@
             group_external,
             held,
             start,
+            shard_rows,
             last_call,
         )
 
@@ -353,41 +369,39 @@
         return reduced / spread - center / spread * vectors.astype(jnp.float32)
 
     value_pieces = [{0: grid_values[:half]}, {0: grid_values[half:]}]
-    parts = sums(orbital_pieces, first_products(orbital_pieces, LARGE_LIMIT), LARGE_LIMIT)
-    own_kinetic = lax.dynamic_slice_in_dim(kinetic, where[0] * shard_rows, shard_rows, 0)
-    most = max(depth.values())
-    taken, total = [], own_kinetic
+    early = first_products(orbital_pieces, LARGE_LIMIT)
+    early = second_products(orbital_pieces, early, LARGE_LIMIT)
+    plans = turns(row_count)
+    taken, total = [], kinetic
 
     def arrived_values():
         return [(m, p) for p in range(2) for m in sorted(value_pieces[p])]
 
-    orbital_pieces = hop(value_pieces[0], 1, orbital_pieces)
-    for turn in range(2, most + 2):
+    for turn in range(len(plans[0])):
         fresh = [which for which in arrived_values() if which not in taken]
+        if turn == 0:
+            orbital_pieces = hop(value_pieces[0], plans[0][turn], orbital_pieces)
+            orbital_pieces = hop(value_pieces[1], plans[1][turn], orbital_pieces)
+            continue
+        value_pieces[1], early = hop(value_pieces[0], plans[0][turn], (value_pieces[1], early))
+        if turn == 1:
+            early = hop(value_pieces[1], plans[1][turn], early)
+            early = sums(orbital_pieces, early, LARGE_LIMIT)
+        else:
+            total = hop(value_pieces[1], plans[1][turn], total)
+        total = rows_of(fresh, total, False)
         taken = taken + fresh
-        if turn == most + 1:
-            total = hop(value_pieces[1], turn - 1, total)
-        else:
-            value_pieces[1], parts, total = hop(
-                value_pieces[0], turn, (value_pieces[1], parts, total)
-            )
-            total = hop(value_pieces[1], turn - 1, total)
-        if turn <= most:
-            total = rows_of(fresh, total, False)
-        else:
-            taken = [which for which in taken if which not in fresh]
-    arrived = send(parts)
-    arrived = send(parts)
-    rest = [(m, p) for p in range(2) for m in masks if (m, p) not in taken]
+    arrived = send(early)
+    rest = [which for which in arrived_values() if which not in taken]
     own = rows_of(rest, total, True)
     first_term = finish(orbital_pieces, arrived, orbitals).astype(jnp.bfloat16)
     first_pieces, early = spread_out(first_term, first_products)
     second_term = (
-        2.0 * finish(first_pieces, send(sums(first_pieces, early)), first_term)
+        2.0 * finish(first_pieces, send(sums(first_pieces, second_products(first_pieces, early))), first_term)
         - orbitals.astype(jnp.float32)
     ).astype(jnp.bfloat16)
     second_pieces, early = spread_out(second_term, first_products)
-    return 2.0 * finish(second_pieces, send(sums(second_pieces, early)), second_term) - first_term.astype(
+    return 2.0 * finish(second_pieces, send(sums(second_pieces, second_products(second_pieces, early))), second_term) - first_term.astype(
         jnp.float32
     )
 

time: 211 us -> 204 us (0.967)
  waiting for transfers between devices: 64.3 us -> 54.4 us
    ppermute x44, waiting for transfers between devices: 64.3 us -> 54.4 us  [swap(): lax.ppermute(array, axis, [(i, i ^ mask) for i in range(lax.axis_size(axi...]
    dynamic_slice x1 -> x0, local copies, waits for them, and re-layouts: 4.68 us -> none  [body(): lax.dynamic_slice_in_dim(kinetic, where[0] * shard_rows, shard_rows, 0)]
    unnamed x61 -> x45, local copies, waits for them, and re-layouts: 7.69 us -> 10.9 us
    pallas_call x3 -> x4, Pallas kernels: 14.4 us -> 15.4 us  [add_rows(): pl.pallas_call(functools.partial(rows_kernel, listed, groups, firsts, las...]
  transfers between devices with their start and end apart: 44 -> 44, of which waited for: 15 -> 20; matrix products, arithmetic and copies ran while one was open for 3% -> 1% of each run, Pallas kernels for 24% -> 25%
where the time goes in v5:
time: 204 us; the launch traced here: 203 us
  starting transfers between devices  78.6 us (39%)
  waiting for transfers between devices  54.4 us (27%)
  Pallas kernels  53.4 us (26%)
  local copies, waits for them, and re-layouts  13.3 us (7%)
  other arithmetic  2.97 us (1%)
    ppermute x44, starting transfers between devices, swap(): lax.ppermute(array, axis, [(i, i ^ mask) for i in range(lax.axis_size(axi...  78.6 us
    ppermute x44, waiting for transfers between devices, swap(): lax.ppermute(array, axis, [(i, i ^ mask) for i in range(lax.axis_size(axi...  54.4 us
    pallas_call x6, Pallas kernels, early_product(): pl.pallas_call(functools.partial(early_kernel, len(masks)), out_shape=jax...  21.8 us
    pallas_call x4, Pallas kernels, add_rows(): pl.pallas_call(functools.partial(rows_kernel, listed, groups, firsts, las...  15.4 us
    unnamed x45, local copies, waits for them, and re-layouts  10.9 us
    pallas_call x9, Pallas kernels, late_product(): pl.pallas_call(functools.partial(late_kernel, len(masks)), out_shape=jax....  10.7 us
    pallas_call x3, Pallas kernels, own_product(): pl.pallas_call(functools.partial(own_kernel, len(masks)), out_shape=jax.S...  5.43 us
  transfers between devices with their start and end apart: 44, of which 20 were waited for; matrix products, arithmetic and copies ran while one was open for 1% of the time, Pallas kernels for 25%

profile of v5, /device:TPU:0, one launch (start us, length us, event | category | flops | bytes accessed | tf_op | source)
XLA Modules:
  0.0 203.2 jit_solution(14800200348943162719)
XLA Ops:
  2.5 5.1 %collective-permute-start.3 = (bf16[528,256]{1,0:T(8,128)(2,1)S(1)}, bf16[528,256]{1,0:T(8,128)(2,1)S(1)}, u32[]{:S(2)}, u32[]{:S(2)}) collective-permute-start(bf16[528,256]{1,0:T(8,128)(2,1)S(1)} %constant_dynamic-update-slice_fusion.refs_0_.refs_4_.refs_8_), channel_id=1, source_target_pairs={{0,24},{4,28},{8,16},{12,20},{16,8},{20,12},{24,0},{28,4},{1,25},{... | collective-permute-start | bytes 811016 | tf_op jit(solution)/shard_map/ppermute | solution.py:36
  7.6 7.4 %collective-permute-done.3.refs_6_.refs_7_.refs_14_ = bf16[528,256]{1,0:T(8,128)(2,1)S(1)} collective-permute-done((bf16[528,256]{1,0:T(8,128)(2,1)S(1)}, bf16[528,256]{1,0:T(8,128)(2,1)S(1)}, u32[]{:S(2)}, u32[]{:S(2)}) %collective-permute-start.3) | collective-permute-done | bytes 270368 | tf_op jit(solution)/shard_map/ppermute | solution.py:36
  17.0 4.6 %collective-permute-start.4 = (bf16[528,256]{1,0:T(8,128)(2,1)S(1)}, bf16[528,256]{1,0:T(8,128)(2,1)S(1)}, u32[]{:S(2)}, u32[]{:S(2)}) collective-permute-start(bf16[528,256]{1,0:T(8,128)(2,1)S(1)} %collective-permute-done.3.refs_6_.refs_7_.refs_14_), channel_id=1, source_target_pairs={{0,8},{4,12},{8,0},{12,4},{16,24},{20,28},{24,16},{28,20},{1,9},{5... | collective-permute-start | bytes 811016 | tf_op jit(solution)/shard_map/ppermute | solution.py:36
  24.4 4.6 %collective-permute-start.6 = (bf16[528,256]{1,0:T(8,128)(2,1)S(1)}, bf16[528,256]{1,0:T(8,128)(2,1)S(1)}, u32[]{:S(2)}, u32[]{:S(2)}) collective-permute-start(bf16[528,256]{1,0:T(8,128)(2,1)S(1)} %collective-permute-done.5.refs_7_.refs_5_.refs_15_), channel_id=1, source_target_pairs={{0,8},{4,12},{8,0},{12,4},{16,24},{20,28},{24,16},{28,20},{1,9},{5... | collective-permute-start | bytes 811016 | tf_op jit(solution)/shard_map/ppermute | solution.py:36
  35.5 5.2 %collective-permute-start.8 = (bf16[2,256,384]{2,1,0:T(8,128)(2,1)}, bf16[2,256,384]{2,1,0:T(8,128)(2,1)}, u32[]{:S(2)}, u32[]{:S(2)}) collective-permute-start(bf16[2,256,384]{2,1,0:T(8,128)(2,1)} %get-tuple-element.73.refs_0_), channel_id=1, source_target_pairs={{0,8},{4,12},{8,0},{12,4},{16,24},{20,28},{24,16},{28,20},{1,9},{5... | collective-permute-start | bytes 1179656 | tf_op jit(solution)/shard_map/ppermute | solution.py:36
  43.1 5.1 %shard_map.56.refs_6_ = f32[3,512,256]{2,1,0:T(8,128)S(1)} custom-call(s32[2]{0:T(128)S(1)} %pad_add_fusion.where_ref, bf16[2048,4096]{1,0:T(8,128)(2,1)} %refs_0_.29, bf16[2048,4096]{1,0:T(8,128)(2,1)} %refs_0_.29, bf16[2048,4096]{1,0:T(8,128)(2,1)} %refs_0_.29, bf16[2048,4096]{1,0:T(8,128)(2,1)} %refs_0_.29, ...), custom_call_target="tpu_custom_call" | custom-call | flops 1610612736 | bytes 6291456 | tf_op jit(solution)/shard_map/pallas_call | solution.py:213
  48.3 4.5 %shard_map.57.refs_2_ = f32[3,512,256]{2,1,0:T(8,128)S(1)} custom-call(s32[2]{0:T(128)S(1)} %pad_add_fusion.where_ref, bf16[2048,4096]{1,0:T(8,128)(2,1)} %refs_0_.29, bf16[2048,4096]{1,0:T(8,128)(2,1)} %refs_0_.29, bf16[2048,4096]{1,0:T(8,128)(2,1)} %refs_0_.29, bf16[528,256]{1,0:T(8,128)(2,1)S(1)} %collective-permute-done.2.refs_3_.refs_11_, ...), custom_call_target="tpu_custom_call" | custom-call | flops 1207959552 | bytes 4718592 | tf_op jit(solution)/shard_map/pallas_call | solution.py:213
  69.3 7.8 %shard_map.61.refs_6_ = f32[512,4096]{1,0:T(8,128)} custom-call(s32[2]{0:T(128)S(1)} %pad_add_fusion.where_ref, s32[96]{0:T(128)S(1)} %reshape.34.tiles_ref, bf16[2,256,384]{2,1,0:T(8,128)(2,1)} %get-tuple-element.73.refs_0_, bf16[2,256,384]{2,1,0:T(8,128)(2,1)} %collective-permute-done.7.refs_1_, bf16[2,256,384]{2,1,0:T(8,128)(2,1)} %collective-permute-done.8.refs_2_, ...), custom_call_target="tpu_custom_call" | custom-call | flops 301989888 | bytes 19136512 | tf_op jit(solution)/shard_map/pallas_call | solution.py:174
  77.1 3.1 %collective-permute-start.16 = (bf16[2,256,384]{2,1,0:T(8,128)(2,1)}, bf16[2,256,384]{2,1,0:T(8,128)(2,1)S(1)}, u32[]{:S(2)}, u32[]{:S(2)}) collective-permute-start(bf16[2,256,384]{2,1,0:T(8,128)(2,1)} %collective-permute-done.13.refs_2_), channel_id=1, source_target_pairs={{0,4},{4,0},{8,12},{12,8},{16,20},{20,16},{24,28},{28,24},{1,5},{5... | collective-permute-start | bytes 1179656 | tf_op jit(solution)/shard_map/ppermute | solution.py:36
  82.3 3.4 %copy-done = f32[512,4096]{1,0:T(8,128)S(1)} copy-done((f32[512,4096]{1,0:T(8,128)S(1)}, f32[512,4096]{1,0:T(8,128)}, u32[]{:S(2)}) %copy-start) | copy-done | bytes 8388632
  85.7 3.0 %shard_map.62.refs_6_ = f32[512,4096]{1,0:T(8,128)S(1)} custom-call(s32[2]{0:T(128)S(1)} %pad_add_fusion.where_ref, s32[96]{0:T(128)S(1)} %reshape.34.tiles_ref, bf16[2,256,384]{2,1,0:T(8,128)(2,1)} %collective-permute-done.11.refs_0_, bf16[2,256,384]{2,1,0:T(8,128)(2,1)} %collective-permute-done.12.refs_1_, ...), custom_call_target="tpu_custom_call" | custom-call | flops 201326592 | bytes 18350080 | tf_op jit(solution)/shard_map/pallas_call | solution.py:174
  91.3 4.6 %collective-permute-done.18.refs_3_ = bf16[2,256,384]{2,1,0:T(8,128)(2,1)S(1)} collective-permute-done((bf16[2,256,384]{2,1,0:T(8,128)(2,1)}, bf16[2,256,384]{2,1,0:T(8,128)(2,1)S(1)}, u32[]{:S(2)}, u32[]{:S(2)}) %collective-permute-start.18) | collective-permute-done | bytes 393248 | tf_op jit(solution)/shard_map/ppermute | solution.py:36
  105.5 2.4 %shard_map.64.refs_0_.refs_1_.refs_2_.refs_3_.refs_4_.refs_5_.refs_6_.refs_7_ = bf16[512,4096]{1,0:T(8,128)(2,1)S(1)} custom-call(s32[2]{0:T(128)S(1)} %pad_add_fusion.where_ref, s32[96]{0:T(128)S(1)} %reshape.34.tiles_ref, bf16[2,256,384]{2,1,0:T(8,128)(2,1)S(1)} %collective-permute-done.19.refs_0_, ...), custom_call_target="tpu_custom_call" | custom-call | flops 100663296 | bytes 17563648 | tf_op jit(solution)/shard_map/pallas_call | solution.py:174
  109.8 2.5 %collective-permute-done.22 = bf16[512,256]{1,0:T(8,128)(2,1)S(1)} collective-permute-done((bf16[512,256]{1,0:T(8,128)(2,1)S(1)}, bf16[512,256]{1,0:T(8,128)(2,1)S(1)}, u32[]{:S(2)}, u32[]{:S(2)}) %collective-permute-start.22) | collective-permute-done | bytes 262176 | tf_op jit(solution)/shard_map/ppermute | solution.py:36
  112.5 3.2 %collective-permute-start.27 = (bf16[512,256]{1,0:T(8,128)(2,1)S(1)}, bf16[512,256]{1,0:T(8,128)(2,1)S(1)}, u32[]{:S(2)}, u32[]{:S(2)}) collective-permute-start(bf16[512,256]{1,0:T(8,128)(2,1)S(1)} %fusion.1.refs_4_.refs_8_), channel_id=1, source_target_pairs={{0,24},{4,28},{8,16},{12,20},{16,8},{20,12},{24,0},{28,4},{1,25},{... | collective-permute-start | bytes 786440 | tf_op jit(solution)/shard_map/ppermute | solution.py:36
  116.8 2.4 %collective-permute-start.24 = (bf16[512,256]{1,0:T(8,128)(2,1)S(1)}, bf16[512,256]{1,0:T(8,128)(2,1)S(1)}, u32[]{:S(2)}, u32[]{:S(2)}) collective-permute-start(bf16[512,256]{1,0:T(8,128)(2,1)S(1)} %fusion.1.refs_4_.refs_8_), channel_id=1, source_target_pairs={{0,4},{4,0},{8,12},{12,8},{16,20},{20,16},{24,28},{28,24},{1,5},{5... | collective-permute-start | bytes 786440 | tf_op jit(solution)/shard_map/ppermute | solution.py:36
  119.2 4.3 %collective-permute-done.27.refs_7_.refs_14_ = bf16[512,256]{1,0:T(8,128)(2,1)S(1)} collective-permute-done((bf16[512,256]{1,0:T(8,128)(2,1)S(1)}, bf16[512,256]{1,0:T(8,128)(2,1)S(1)}, u32[]{:S(2)}, u32[]{:S(2)}) %collective-permute-start.27) | collective-permute-done | bytes 262176 | tf_op jit(solution)/shard_map/ppermute | solution.py:36
  123.6 2.9 %collective-permute-start.29 = (bf16[512,256]{1,0:T(8,128)(2,1)S(1)}, bf16[512,256]{1,0:T(8,128)(2,1)S(1)}, u32[]{:S(2)}, u32[]{:S(2)}) collective-permute-start(bf16[512,256]{1,0:T(8,128)(2,1)S(1)} %collective-permute-done.27.refs_7_.refs_14_), channel_id=1, source_target_pairs={{0,4},{4,0},{8,12},{12,8},{16,20},{20,16},{24,28},{28,24},{1,5},{5... | collective-permute-start | bytes 786440 | tf_op jit(solution)/shard_map/ppermute | solution.py:36
  126.5 3.7 %collective-permute-start.28 = (bf16[512,256]{1,0:T(8,128)(2,1)S(1)}, bf16[512,256]{1,0:T(8,128)(2,1)S(1)}, u32[]{:S(2)}, u32[]{:S(2)}) collective-permute-start(bf16[512,256]{1,0:T(8,128)(2,1)S(1)} %collective-permute-done.27.refs_7_.refs_14_), channel_id=1, source_target_pairs={{0,8},{4,12},{8,0},{12,4},{16,24},{20,28},{24,16},{28,20},{1,9},{5... | collective-permute-start | bytes 786440 | tf_op jit(solution)/shard_map/ppermute | solution.py:36
  130.9 3.4 %shard_map.66.refs_6_ = f32[3,512,256]{2,1,0:T(8,128)S(1)} custom-call(s32[2]{0:T(128)S(1)} %pad_add_fusion.where_ref, bf16[2048,4096]{1,0:T(8,128)(2,1)S(1)} %bitcast.15, bf16[2048,4096]{1,0:T(8,128)(2,1)S(1)} %bitcast.15, bf16[2048,4096]{1,0:T(8,128)(2,1)S(1)} %bitcast.15, bf16[2048,4096]{1,0:T(8,128)(2,1)S(1)} %bitcast.15, ...), custom_call_target="tpu_custom_call" | custom-call | flops 1610612736 | bytes 6291456 | tf_op jit(solution)/shard_map/pallas_call | solution.py:213
  134.4 3.6 %collective-permute-start.30 = (bf16[512,256]{1,0:T(8,128)(2,1)S(1)}, bf16[512,256]{1,0:T(8,128)(2,1)S(1)}, u32[]{:S(2)}, u32[]{:S(2)}) collective-permute-start(bf16[512,256]{1,0:T(8,128)(2,1)S(1)} %collective-permute-done.29.refs_15_.refs_5_), channel_id=1, source_target_pairs={{0,8},{4,12},{8,0},{12,4},{16,24},{20,28},{24,16},{28,20},{1,9},{5... | collective-permute-start | bytes 786440 | tf_op jit(solution)/shard_map/ppermute | solution.py:36
  138.0 2.8 %shard_map.68.refs_2_ = f32[3,512,256]{2,1,0:T(8,128)S(1)} custom-call(s32[2]{0:T(128)S(1)} %pad_add_fusion.where_ref, bf16[2048,4096]{1,0:T(8,128)(2,1)S(1)} %bitcast.15, bf16[2048,4096]{1,0:T(8,128)(2,1)S(1)} %bitcast.15, bf16[2048,4096]{1,0:T(8,128)(2,1)S(1)} %bitcast.15, bf16[512,256]{1,0:T(8,128)(2,1)S(1)} %collective-permute-done.26.refs_11_.refs_3_, ...), custom_call_target="tpu_custom_call" | custom-call | flops 1207959552 | bytes 4718592 | tf_op jit(solution)/shard_map/pallas_call | solution.py:213
  149.3 3.1 %collective-permute-done.31 = bf16[512,256]{1,0:T(8,128)(2,1)S(1)} collective-permute-done((bf16[512,256]{1,0:T(8,128)(2,1)S(1)}, bf16[512,256]{1,0:T(8,128)(2,1)S(1)}, u32[]{:S(2)}, u32[]{:S(2)}) %collective-permute-start.31) | collective-permute-done | bytes 262176 | tf_op jit(solution)/shard_map/ppermute | solution.py:36
  152.3 4.6 %collective-permute-done.32 = bf16[512,256]{1,0:T(8,128)(2,1)S(1)} collective-permute-done((bf16[512,256]{1,0:T(8,128)(2,1)S(1)}, bf16[512,256]{1,0:T(8,128)(2,1)S(1)}, u32[]{:S(2)}, u32[]{:S(2)}) %collective-permute-start.32) | collective-permute-done | bytes 262176 | tf_op jit(solution)/shard_map/ppermute | solution.py:36
  157.1 3.1 %collective-permute-start.37 = (bf16[512,256]{1,0:T(8,128)(2,1)S(1)}, bf16[512,256]{1,0:T(8,128)(2,1)S(1)}, u32[]{:S(2)}, u32[]{:S(2)}) collective-permute-start(bf16[512,256]{1,0:T(8,128)(2,1)S(1)} %fusion.2.refs_4_.refs_8_), channel_id=1, source_target_pairs={{0,24},{4,28},{8,16},{12,20},{16,8},{20,12},{24,0},{28,4},{1,25},{... | collective-permute-start | bytes 786440 | tf_op jit(solution)/shard_map/ppermute | solution.py:36
  162.8 5.3 %collective-permute-done.37.refs_7_.refs_14_ = bf16[512,256]{1,0:T(8,128)(2,1)S(1)} collective-permute-done((bf16[512,256]{1,0:T(8,128)(2,1)S(1)}, bf16[512,256]{1,0:T(8,128)(2,1)S(1)}, u32[]{:S(2)}, u32[]{:S(2)}) %collective-permute-start.37) | collective-permute-done | bytes 262176 | tf_op jit(solution)/shard_map/ppermute | solution.py:36
  170.2 5.3 %collective-permute-start.38 = (bf16[512,256]{1,0:T(8,128)(2,1)S(1)}, bf16[512,256]{1,0:T(8,128)(2,1)S(1)}, u32[]{:S(2)}, u32[]{:S(2)}) collective-permute-start(bf16[512,256]{1,0:T(8,128)(2,1)S(1)} %collective-permute-done.37.refs_7_.refs_14_), channel_id=1, source_target_pairs={{0,8},{4,12},{8,0},{12,4},{16,24},{20,28},{24,16},{28,20},{1,9},{5... | collective-permute-start | bytes 786440 | tf_op jit(solution)/shard_map/ppermute | solution.py:36
  175.8 3.3 %shard_map.72.refs_6_ = f32[3,512,256]{2,1,0:T(8,128)S(1)} custom-call(s32[2]{0:T(128)S(1)} %pad_add_fusion.where_ref, bf16[2048,4096]{1,0:T(8,128)(2,1)S(1)} %bitcast.15, bf16[2048,4096]{1,0:T(8,128)(2,1)S(1)} %bitcast.15, bf16[2048,4096]{1,0:T(8,128)(2,1)S(1)} %bitcast.15, bf16[2048,4096]{1,0:T(8,128)(2,1)S(1)} %bitcast.15, ...), custom_call_target="tpu_custom_call" | custom-call | flops 1610612736 | bytes 6291456 | tf_op jit(solution)/shard_map/pallas_call | solution.py:213
  179.1 3.9 %collective-permute-start.40 = (bf16[512,256]{1,0:T(8,128)(2,1)S(1)}, bf16[512,256]{1,0:T(8,128)(2,1)S(1)}, u32[]{:S(2)}, u32[]{:S(2)}) collective-permute-start(bf16[512,256]{1,0:T(8,128)(2,1)S(1)} %collective-permute-done.39.refs_15_.refs_5_), channel_id=1, source_target_pairs={{0,8},{4,12},{8,0},{12,4},{16,24},{20,28},{24,16},{28,20},{1,9},{5... | collective-permute-start | bytes 786440 | tf_op jit(solution)/shard_map/ppermute | solution.py:36
  183.2 2.7 %shard_map.74.refs_2_ = f32[3,512,256]{2,1,0:T(8,128)S(1)} custom-call(s32[2]{0:T(128)S(1)} %pad_add_fusion.where_ref, bf16[2048,4096]{1,0:T(8,128)(2,1)S(1)} %bitcast.15, bf16[2048,4096]{1,0:T(8,128)(2,1)S(1)} %bitcast.15, bf16[2048,4096]{1,0:T(8,128)(2,1)S(1)} %bitcast.15, bf16[512,256]{1,0:T(8,128)(2,1)S(1)} %collective-permute-done.36.refs_11_.refs_3_, ...), custom_call_target="tpu_custom_call" | custom-call | flops 1207959552 | bytes 4718592 | tf_op jit(solution)/shard_map/pallas_call | solution.py:213
  194.1 3.0 %collective-permute-done.41 = bf16[512,256]{1,0:T(8,128)(2,1)S(1)} collective-permute-done((bf16[512,256]{1,0:T(8,128)(2,1)S(1)}, bf16[512,256]{1,0:T(8,128)(2,1)S(1)}, u32[]{:S(2)}, u32[]{:S(2)}) %collective-permute-start.41) | collective-permute-done | bytes 262176 | tf_op jit(solution)/shard_map/ppermute | solution.py:36
  197.2 5.0 %collective-permute-done.42 = bf16[512,256]{1,0:T(8,128)(2,1)S(1)} collective-permute-done((bf16[512,256]{1,0:T(8,128)(2,1)S(1)}, bf16[512,256]{1,0:T(8,128)(2,1)S(1)}, u32[]{:S(2)}, u32[]{:S(2)}) %collective-permute-start.42) | collective-permute-done | bytes 262176 | tf_op jit(solution)/shard_map/ppermute | solution.py:36
  (141 shorter events, 73.8 us)
Async XLA Ops:
  2.5 12.5 %collective-permute-start.3 = (bf16[528,256]{1,0:T(8,128)(2,1)S(1)}, bf16[528,256]{1,0:T(8,128)(2,1)S(1)}, u32[]{:S(2)}, u32[]{:S(2)}) collective-permute-start(bf16[528,256]{1,0:T(8,128)(2,1)S(1)} %constant_dynamic-update-slice_fusion.refs_0_.refs_4_.refs_8_), channel_id=1, source_target_pairs={{0,24},{4,28},{8,16},{12,20},{16,8},{20,12},{24,0},{28,4},{1,25},{... | collective-permute-start | bytes 811016 | tf_op jit(solution)/shard_map/ppermute | solution.py:36
  7.6 14.0 %collective-permute-start.1 = (bf16[528,256]{1,0:T(8,128)(2,1)S(1)}, bf16[528,256]{1,0:T(8,128)(2,1)S(1)}, u32[]{:S(2)}, u32[]{:S(2)}) collective-permute-start(bf16[528,256]{1,0:T(8,128)(2,1)S(1)} %constant_dynamic-update-slice_fusion.refs_0_.refs_4_.refs_8_), channel_id=1, source_target_pairs={{0,8},{4,12},{8,0},{12,4},{16,24},{20,28},{24,16},{28,20},{1,9},{5... | collective-permute-start | bytes 811016 | tf_op jit(solution)/shard_map/ppermute | solution.py:36
  16.7 14.4 %collective-permute-start = (bf16[528,256]{1,0:T(8,128)(2,1)S(1)}, bf16[528,256]{1,0:T(8,128)(2,1)S(1)}, u32[]{:S(2)}, u32[]{:S(2)}) collective-permute-start(bf16[528,256]{1,0:T(8,128)(2,1)S(1)} %constant_dynamic-update-slice_fusion.refs_0_.refs_4_.refs_8_), channel_id=1, source_target_pairs={{0,4},{4,0},{8,12},{12,8},{16,20},{20,16},{24,28},{28,24},{1,5},{5... | collective-permute-start | bytes 811016 | tf_op jit(solution)/shard_map/ppermute | solution.py:36
  17.0 14.1 %collective-permute-start.4 = (bf16[528,256]{1,0:T(8,128)(2,1)S(1)}, bf16[528,256]{1,0:T(8,128)(2,1)S(1)}, u32[]{:S(2)}, u32[]{:S(2)}) collective-permute-start(bf16[528,256]{1,0:T(8,128)(2,1)S(1)} %collective-permute-done.3.refs_6_.refs_7_.refs_14_), channel_id=1, source_target_pairs={{0,8},{4,12},{8,0},{12,4},{16,24},{20,28},{24,16},{28,20},{1,9},{5... | collective-permute-start | bytes 811016 | tf_op jit(solution)/shard_map/ppermute | solution.py:36
  21.7 11.8 %collective-permute-start.2 = (bf16[528,256]{1,0:T(8,128)(2,1)S(1)}, bf16[528,256]{1,0:T(8,128)(2,1)S(1)}, u32[]{:S(2)}, u32[]{:S(2)}) collective-permute-start(bf16[528,256]{1,0:T(8,128)(2,1)S(1)} %collective-permute-done.1.refs_2_.refs_6_.refs_10_), channel_id=1, source_target_pairs={{0,4},{4,0},{8,12},{12,8},{16,20},{20,16},{24,28},{28,24},{1,5},{5... | collective-permute-start | bytes 811016 | tf_op jit(solution)/shard_map/ppermute | solution.py:36
  33.5 24.6 %collective-permute-start.10 = (bf16[2,256,384]{2,1,0:T(8,128)(2,1)}, bf16[2,256,384]{2,1,0:T(8,128)(2,1)}, u32[]{:S(2)}, u32[]{:S(2)}) collective-permute-start(bf16[2,256,384]{2,1,0:T(8,128)(2,1)} %get-tuple-element.80.refs_4_), channel_id=1, source_target_pairs={{0,4},{4,0},{8,12},{12,8},{16,20},{20,16},{24,28},{28,24},{1,5},{5... | collective-permute-start | bytes 1179656 | tf_op jit(solution)/shard_map/ppermute | solution.py:36
  35.0 23.1 %collective-permute-start.7 = (bf16[2,256,384]{2,1,0:T(8,128)(2,1)}, bf16[2,256,384]{2,1,0:T(8,128)(2,1)}, u32[]{:S(2)}, u32[]{:S(2)}) collective-permute-start(bf16[2,256,384]{2,1,0:T(8,128)(2,1)} %get-tuple-element.73.refs_0_), channel_id=1, source_target_pairs={{0,4},{4,0},{8,12},{12,8},{16,20},{20,16},{24,28},{28,24},{1,5},{5... | collective-permute-start | bytes 1179656 | tf_op jit(solution)/shard_map/ppermute | solution.py:36
  35.5 22.5 %collective-permute-start.8 = (bf16[2,256,384]{2,1,0:T(8,128)(2,1)}, bf16[2,256,384]{2,1,0:T(8,128)(2,1)}, u32[]{:S(2)}, u32[]{:S(2)}) collective-permute-start(bf16[2,256,384]{2,1,0:T(8,128)(2,1)} %get-tuple-element.73.refs_0_), channel_id=1, source_target_pairs={{0,8},{4,12},{8,0},{12,4},{16,24},{20,28},{24,16},{28,20},{1,9},{5... | collective-permute-start | bytes 1179656 | tf_op jit(solution)/shard_map/ppermute | solution.py:36
  40.8 17.8 %collective-permute-start.9 = (bf16[2,256,384]{2,1,0:T(8,128)(2,1)}, bf16[2,256,384]{2,1,0:T(8,128)(2,1)}, u32[]{:S(2)}, u32[]{:S(2)}) collective-permute-start(bf16[2,256,384]{2,1,0:T(8,128)(2,1)} %get-tuple-element.73.refs_0_), channel_id=1, source_target_pairs={{0,24},{4,28},{8,16},{12,20},{16,8},{20,12},{24,0},{28,4},{1,25},{... | collective-permute-start | bytes 1179656 | tf_op jit(solution)/shard_map/ppermute | solution.py:36
  58.5 18.5 %collective-permute-start.13 = (bf16[2,256,384]{2,1,0:T(8,128)(2,1)}, bf16[2,256,384]{2,1,0:T(8,128)(2,1)}, u32[]{:S(2)}, u32[]{:S(2)}) collective-permute-start(bf16[2,256,384]{2,1,0:T(8,128)(2,1)} %get-tuple-element.80.refs_4_), channel_id=1, source_target_pairs={{0,8},{4,12},{8,0},{12,4},{16,24},{20,28},{24,16},{28,20},{1,9},{5... | collective-permute-start | bytes 1179656 | tf_op jit(solution)/shard_map/ppermute | solution.py:36
  58.5 18.5 %collective-permute-start.14 = (bf16[2,256,384]{2,1,0:T(8,128)(2,1)}, bf16[2,256,384]{2,1,0:T(8,128)(2,1)}, u32[]{:S(2)}, u32[]{:S(2)}) collective-permute-start(bf16[2,256,384]{2,1,0:T(8,128)(2,1)} %get-tuple-element.80.refs_4_), channel_id=1, source_target_pairs={{0,24},{4,28},{8,16},{12,20},{16,8},{20,12},{24,0},{28,4},{1,25},{... | collective-permute-start | bytes 1179656 | tf_op jit(solution)/shard_map/ppermute | solution.py:36
  60.0 17.1 %collective-permute-start.11 = (bf16[2,256,384]{2,1,0:T(8,128)(2,1)}, bf16[2,256,384]{2,1,0:T(8,128)(2,1)}, u32[]{:S(2)}, u32[]{:S(2)}) collective-permute-start(bf16[2,256,384]{2,1,0:T(8,128)(2,1)} %collective-permute-done.8.refs_2_), channel_id=1, source_target_pairs={{0,4},{4,0},{8,12},{12,8},{16,20},{20,16},{24,28},{28,24},{1,5},{5... | collective-permute-start | bytes 1179656 | tf_op jit(solution)/shard_map/ppermute | solution.py:36
  61.5 15.6 %collective-permute-start.12 = (bf16[2,256,384]{2,1,0:T(8,128)(2,1)}, bf16[2,256,384]{2,1,0:T(8,128)(2,1)}, u32[]{:S(2)}, u32[]{:S(2)}) collective-permute-start(bf16[2,256,384]{2,1,0:T(8,128)(2,1)} %collective-permute-done.9.refs_3_), channel_id=1, source_target_pairs={{0,4},{4,0},{8,12},{12,8},{16,20},{20,16},{24,28},{28,24},{1,5},{5... | collective-permute-start | bytes 1179656 | tf_op jit(solution)/shard_map/ppermute | solution.py:36
  77.1 13.1 %collective-permute-start.16 = (bf16[2,256,384]{2,1,0:T(8,128)(2,1)}, bf16[2,256,384]{2,1,0:T(8,128)(2,1)S(1)}, u32[]{:S(2)}, u32[]{:S(2)}) collective-permute-start(bf16[2,256,384]{2,1,0:T(8,128)(2,1)} %collective-permute-done.13.refs_2_), channel_id=1, source_target_pairs={{0,4},{4,0},{8,12},{12,8},{16,20},{20,16},{24,28},{28,24},{1,5},{5... | collective-permute-start | bytes 1179656 | tf_op jit(solution)/shard_map/ppermute | solution.py:36
  80.2 11.1 %collective-permute-start.17 = (bf16[2,256,384]{2,1,0:T(8,128)(2,1)}, bf16[2,256,384]{2,1,0:T(8,128)(2,1)S(1)}, u32[]{:S(2)}, u32[]{:S(2)}) collective-permute-start(bf16[2,256,384]{2,1,0:T(8,128)(2,1)} %collective-permute-done.14.refs_3_), channel_id=1, source_target_pairs={{0,8},{4,12},{8,0},{12,4},{16,24},{20,28},{24,16},{28,20},{1,9},{5... | collective-permute-start | bytes 1179656 | tf_op jit(solution)/shard_map/ppermute | solution.py:36
  80.8 15.1 %collective-permute-start.18 = (bf16[2,256,384]{2,1,0:T(8,128)(2,1)}, bf16[2,256,384]{2,1,0:T(8,128)(2,1)S(1)}, u32[]{:S(2)}, u32[]{:S(2)}) collective-permute-start(bf16[2,256,384]{2,1,0:T(8,128)(2,1)} %collective-permute-done.14.refs_3_), channel_id=1, source_target_pairs={{0,4},{4,0},{8,12},{12,8},{16,20},{20,16},{24,28},{28,24},{1,5},{5... | collective-permute-start | bytes 1179656 | tf_op jit(solution)/shard_map/ppermute | solution.py:36
  81.3 15.7 %collective-permute-start.15 = (bf16[2,256,384]{2,1,0:T(8,128)(2,1)}, bf16[2,256,384]{2,1,0:T(8,128)(2,1)S(1)}, u32[]{:S(2)}, u32[]{:S(2)}) collective-permute-start(bf16[2,256,384]{2,1,0:T(8,128)(2,1)} %collective-permute-done.9.refs_3_), channel_id=1, source_target_pairs={{0,8},{4,12},{8,0},{12,4},{16,24},{20,28},{24,16},{28,20},{1,9},{5... | collective-permute-start | bytes 1179656 | tf_op jit(solution)/shard_map/ppermute | solution.py:36
  98.7 11.1 %collective-permute-start.21 = (bf16[512,256]{1,0:T(8,128)(2,1)S(1)}, bf16[512,256]{1,0:T(8,128)(2,1)S(1)}, u32[]{:S(2)}, u32[]{:S(2)}) collective-permute-start(bf16[512,256]{1,0:T(8,128)(2,1)S(1)} %shard_map.58), channel_id=1, source_target_pairs={{0,3},{1,2},{2,1},{3,0},{4,7},{5,6},{6,5},{7,4},{8,11},{9,10},{10,... | collective-permute-start | bytes 786440 | tf_op jit(solution)/shard_map/ppermute | solution.py:36
  98.7 13.6 %collective-permute-start.22 = (bf16[512,256]{1,0:T(8,128)(2,1)S(1)}, bf16[512,256]{1,0:T(8,128)(2,1)S(1)}, u32[]{:S(2)}, u32[]{:S(2)}) collective-permute-start(bf16[512,256]{1,0:T(8,128)(2,1)S(1)} %shard_map.59), channel_id=1, source_target_pairs={{0,2},{1,3},{2,0},{3,1},{4,6},{5,7},{6,4},{7,5},{8,10},{9,11},{10,... | collective-permute-start | bytes 786440 | tf_op jit(solution)/shard_map/ppermute | solution.py:36
  99.8 12.5 %collective-permute-start.23 = (bf16[512,256]{1,0:T(8,128)(2,1)S(1)}, bf16[512,256]{1,0:T(8,128)(2,1)S(1)}, u32[]{:S(2)}, u32[]{:S(2)}) collective-permute-start(bf16[512,256]{1,0:T(8,128)(2,1)S(1)} %shard_map.60), channel_id=1, source_target_pairs={{0,1},{1,0},{2,3},{3,2},{4,5},{5,4},{6,7},{7,6},{8,9},{9,8},{10,11... | collective-permute-start | bytes 786440 | tf_op jit(solution)/shard_map/ppermute | solution.py:36
  112.5 11.1 %collective-permute-start.27 = (bf16[512,256]{1,0:T(8,128)(2,1)S(1)}, bf16[512,256]{1,0:T(8,128)(2,1)S(1)}, u32[]{:S(2)}, u32[]{:S(2)}) collective-permute-start(bf16[512,256]{1,0:T(8,128)(2,1)S(1)} %fusion.1.refs_4_.refs_8_), channel_id=1, source_target_pairs={{0,24},{4,28},{8,16},{12,20},{16,8},{20,12},{24,0},{28,4},{1,25},{... | collective-permute-start | bytes 786440 | tf_op jit(solution)/shard_map/ppermute | solution.py:36
  115.7 14.5 %collective-permute-start.25 = (bf16[512,256]{1,0:T(8,128)(2,1)S(1)}, bf16[512,256]{1,0:T(8,128)(2,1)S(1)}, u32[]{:S(2)}, u32[]{:S(2)}) collective-permute-start(bf16[512,256]{1,0:T(8,128)(2,1)S(1)} %fusion.1.refs_4_.refs_8_), channel_id=1, source_target_pairs={{0,8},{4,12},{8,0},{12,4},{16,24},{20,28},{24,16},{28,20},{1,9},{5... | collective-permute-start | bytes 786440 | tf_op jit(solution)/shard_map/ppermute | solution.py:36
  116.8 14.1 %collective-permute-start.24 = (bf16[512,256]{1,0:T(8,128)(2,1)S(1)}, bf16[512,256]{1,0:T(8,128)(2,1)S(1)}, u32[]{:S(2)}, u32[]{:S(2)}) collective-permute-start(bf16[512,256]{1,0:T(8,128)(2,1)S(1)} %fusion.1.refs_4_.refs_8_), channel_id=1, source_target_pairs={{0,4},{4,0},{8,12},{12,8},{16,20},{20,16},{24,28},{28,24},{1,5},{5... | collective-permute-start | bytes 786440 | tf_op jit(solution)/shard_map/ppermute | solution.py:36
  123.6 10.8 %collective-permute-start.29 = (bf16[512,256]{1,0:T(8,128)(2,1)S(1)}, bf16[512,256]{1,0:T(8,128)(2,1)S(1)}, u32[]{:S(2)}, u32[]{:S(2)}) collective-permute-start(bf16[512,256]{1,0:T(8,128)(2,1)S(1)} %collective-permute-done.27.refs_7_.refs_14_), channel_id=1, source_target_pairs={{0,4},{4,0},{8,12},{12,8},{16,20},{20,16},{24,28},{28,24},{1,5},{5... | collective-permute-start | bytes 786440 | tf_op jit(solution)/shard_map/ppermute | solution.py:36
  126.5 11.6 %collective-permute-start.28 = (bf16[512,256]{1,0:T(8,128)(2,1)S(1)}, bf16[512,256]{1,0:T(8,128)(2,1)S(1)}, u32[]{:S(2)}, u32[]{:S(2)}) collective-permute-start(bf16[512,256]{1,0:T(8,128)(2,1)S(1)} %collective-permute-done.27.refs_7_.refs_14_), channel_id=1, source_target_pairs={{0,8},{4,12},{8,0},{12,4},{16,24},{20,28},{24,16},{28,20},{1,9},{5... | collective-permute-start | bytes 786440 | tf_op jit(solution)/shard_map/ppermute | solution.py:36
  144.6 12.3 %collective-permute-start.32 = (bf16[512,256]{1,0:T(8,128)(2,1)S(1)}, bf16[512,256]{1,0:T(8,128)(2,1)S(1)}, u32[]{:S(2)}, u32[]{:S(2)}) collective-permute-start(bf16[512,256]{1,0:T(8,128)(2,1)S(1)} %shard_map.70), channel_id=1, source_target_pairs={{0,2},{1,3},{2,0},{3,1},{4,6},{5,7},{6,4},{7,5},{8,10},{9,11},{10,... | collective-permute-start | bytes 786440 | tf_op jit(solution)/shard_map/ppermute | solution.py:36
  157.1 11.0 %collective-permute-start.37 = (bf16[512,256]{1,0:T(8,128)(2,1)S(1)}, bf16[512,256]{1,0:T(8,128)(2,1)S(1)}, u32[]{:S(2)}, u32[]{:S(2)}) collective-permute-start(bf16[512,256]{1,0:T(8,128)(2,1)S(1)} %fusion.2.refs_4_.refs_8_), channel_id=1, source_target_pairs={{0,24},{4,28},{8,16},{12,20},{16,8},{20,12},{24,0},{28,4},{1,25},{... | collective-permute-start | bytes 786440 | tf_op jit(solution)/shard_map/ppermute | solution.py:36
  160.2 15.3 %collective-permute-start.35 = (bf16[512,256]{1,0:T(8,128)(2,1)S(1)}, bf16[512,256]{1,0:T(8,128)(2,1)S(1)}, u32[]{:S(2)}, u32[]{:S(2)}) collective-permute-start(bf16[512,256]{1,0:T(8,128)(2,1)S(1)} %fusion.2.refs_4_.refs_8_), channel_id=1, source_target_pairs={{0,8},{4,12},{8,0},{12,4},{16,24},{20,28},{24,16},{28,20},{1,9},{5... | collective-permute-start | bytes 786440 | tf_op jit(solution)/shard_map/ppermute | solution.py:36
  162.0 13.7 %collective-permute-start.34 = (bf16[512,256]{1,0:T(8,128)(2,1)S(1)}, bf16[512,256]{1,0:T(8,128)(2,1)S(1)}, u32[]{:S(2)}, u32[]{:S(2)}) collective-permute-start(bf16[512,256]{1,0:T(8,128)(2,1)S(1)} %fusion.2.refs_4_.refs_8_), channel_id=1, source_target_pairs={{0,4},{4,0},{8,12},{12,8},{16,20},{20,16},{24,28},{28,24},{1,5},{5... | collective-permute-start | bytes 786440 | tf_op jit(solution)/shard_map/ppermute | solution.py:36
  168.2 10.9 %collective-permute-start.39 = (bf16[512,256]{1,0:T(8,128)(2,1)S(1)}, bf16[512,256]{1,0:T(8,128)(2,1)S(1)}, u32[]{:S(2)}, u32[]{:S(2)}) collective-permute-start(bf16[512,256]{1,0:T(8,128)(2,1)S(1)} %collective-permute-done.37.refs_7_.refs_14_), channel_id=1, source_target_pairs={{0,4},{4,0},{8,12},{12,8},{16,20},{20,16},{24,28},{28,24},{1,5},{5... | collective-permute-start | bytes 786440 | tf_op jit(solution)/shard_map/ppermute | solution.py:36
  170.2 13.0 %collective-permute-start.38 = (bf16[512,256]{1,0:T(8,128)(2,1)S(1)}, bf16[512,256]{1,0:T(8,128)(2,1)S(1)}, u32[]{:S(2)}, u32[]{:S(2)}) collective-permute-start(bf16[512,256]{1,0:T(8,128)(2,1)S(1)} %collective-permute-done.37.refs_7_.refs_14_), channel_id=1, source_target_pairs={{0,8},{4,12},{8,0},{12,4},{16,24},{20,28},{24,16},{28,20},{1,9},{5... | collective-permute-start | bytes 786440 | tf_op jit(solution)/shard_map/ppermute | solution.py:36
  189.5 12.7 %collective-permute-start.42 = (bf16[512,256]{1,0:T(8,128)(2,1)S(1)}, bf16[512,256]{1,0:T(8,128)(2,1)S(1)}, u32[]{:S(2)}, u32[]{:S(2)}) collective-permute-start(bf16[512,256]{1,0:T(8,128)(2,1)S(1)} %shard_map.76), channel_id=1, source_target_pairs={{0,2},{1,3},{2,0},{3,1},{4,6},{5,7},{6,4},{7,5},{8,10},{9,11},{10,... | collective-permute-start | bytes 786440 | tf_op jit(solution)/shard_map/ppermute | solution.py:36
  (32 other events, 309.5 us)

commit v6 on v5

--- a/solution.py
+++ b/solution.py
@@ -9,7 +9,7 @@
 
 TILE = 128
 SMALL_LIMIT = 18 * 2**20
-LARGE_LIMIT = 46 * 2**20
+LARGE_LIMIT = 36 * 2**20
 center = 1.0
 spread = 2.5
 

time: 204 us -> 202 us (level)
  starting transfers between devices: 78.6 us -> 71.5 us
  waiting for transfers between devices: 54.4 us -> 61.4 us
  local copies, waits for them, and re-layouts: 13.3 us -> 9.89 us
    ppermute x44, starting transfers between devices: 78.6 us -> 71.5 us  [swap(): lax.ppermute(array, axis, [(i, i ^ mask) for i in range(lax.axis_size(axi...]
    ppermute x44, waiting for transfers between devices: 54.4 us -> 61.4 us  [swap(): lax.ppermute(array, axis, [(i, i ^ mask) for i in range(lax.axis_size(axi...]
    unnamed x45 -> x43, local copies, waits for them, and re-layouts: 10.9 us -> 7.52 us
  transfers between devices with their start and end apart: 44 -> 44, of which waited for: 20 -> 19; matrix products, arithmetic and copies ran while one was open for 1% -> 1% of each run, Pallas kernels for 25% -> 26%
where the time goes in v6:
time: 202 us; the launch traced here: 200 us
  starting transfers between devices  71.5 us (35%)
  waiting for transfers between devices  61.4 us (30%)
  Pallas kernels  53.9 us (27%)
  local copies, waits for them, and re-layouts  9.89 us (5%)
  other arithmetic  2.97 us (1%)
    ppermute x44, starting transfers between devices, swap(): lax.ppermute(array, axis, [(i, i ^ mask) for i in range(lax.axis_size(axi...  71.5 us
    ppermute x44, waiting for transfers between devices, swap(): lax.ppermute(array, axis, [(i, i ^ mask) for i in range(lax.axis_size(axi...  61.4 us
    pallas_call x6, Pallas kernels, early_product(): pl.pallas_call(functools.partial(early_kernel, len(masks)), out_shape=jax...  21.8 us
    pallas_call x4, Pallas kernels, add_rows(): pl.pallas_call(functools.partial(rows_kernel, listed, groups, firsts, las...  15.8 us
    pallas_call x9, Pallas kernels, late_product(): pl.pallas_call(functools.partial(late_kernel, len(masks)), out_shape=jax....  10.7 us
    unnamed x43, local copies, waits for them, and re-layouts  7.52 us
    pallas_call x3, Pallas kernels, own_product(): pl.pallas_call(functools.partial(own_kernel, len(masks)), out_shape=jax.S...  5.43 us
  transfers between devices with their start and end apart: 44, of which 19 were waited for; matrix products, arithmetic and copies ran while one was open for 1% of the time, Pallas kernels for 26%

profile of v6, /device:TPU:0, one launch (start us, length us, event | category | flops | bytes accessed | tf_op | source)
XLA Modules:
  0.0 200.2 jit_solution(15079815287061657088)
XLA Ops:
  2.5 5.1 %collective-permute-start.3 = (bf16[528,256]{1,0:T(8,128)(2,1)S(1)}, bf16[528,256]{1,0:T(8,128)(2,1)S(1)}, u32[]{:S(2)}, u32[]{:S(2)}) collective-permute-start(bf16[528,256]{1,0:T(8,128)(2,1)S(1)} %constant_dynamic-update-slice_fusion.refs_0_.refs_4_.refs_8_), channel_id=1, source_target_pairs={{0,24},{4,28},{8,16},{12,20},{16,8},{20,12},{24,0},{28,4},{1,25},{... | collective-permute-start | bytes 811016 | tf_op jit(solution)/shard_map/ppermute | solution.py:36
  7.6 7.4 %collective-permute-done.3.refs_6_.refs_7_.refs_14_ = bf16[528,256]{1,0:T(8,128)(2,1)S(1)} collective-permute-done((bf16[528,256]{1,0:T(8,128)(2,1)S(1)}, bf16[528,256]{1,0:T(8,128)(2,1)S(1)}, u32[]{:S(2)}, u32[]{:S(2)}) %collective-permute-start.3) | collective-permute-done | bytes 270368 | tf_op jit(solution)/shard_map/ppermute | solution.py:36
  17.0 4.6 %collective-permute-start.4 = (bf16[528,256]{1,0:T(8,128)(2,1)S(1)}, bf16[528,256]{1,0:T(8,128)(2,1)S(1)}, u32[]{:S(2)}, u32[]{:S(2)}) collective-permute-start(bf16[528,256]{1,0:T(8,128)(2,1)S(1)} %collective-permute-done.3.refs_6_.refs_7_.refs_14_), channel_id=1, source_target_pairs={{0,8},{4,12},{8,0},{12,4},{16,24},{20,28},{24,16},{28,20},{1,9},{5... | collective-permute-start | bytes 811016 | tf_op jit(solution)/shard_map/ppermute | solution.py:36
  24.4 4.6 %collective-permute-start.6 = (bf16[528,256]{1,0:T(8,128)(2,1)S(1)}, bf16[528,256]{1,0:T(8,128)(2,1)S(1)}, u32[]{:S(2)}, u32[]{:S(2)}) collective-permute-start(bf16[528,256]{1,0:T(8,128)(2,1)S(1)} %collective-permute-done.5.refs_7_.refs_5_.refs_15_), channel_id=1, source_target_pairs={{0,8},{4,12},{8,0},{12,4},{16,24},{20,28},{24,16},{28,20},{1,9},{5... | collective-permute-start | bytes 811016 | tf_op jit(solution)/shard_map/ppermute | solution.py:36
  31.1 2.3 %collective-permute-done.2.refs_3_.refs_11_ = bf16[528,256]{1,0:T(8,128)(2,1)S(1)} collective-permute-done((bf16[528,256]{1,0:T(8,128)(2,1)S(1)}, bf16[528,256]{1,0:T(8,128)(2,1)S(1)}, u32[]{:S(2)}, u32[]{:S(2)}) %collective-permute-start.2) | collective-permute-done | bytes 270368 | tf_op jit(solution)/shard_map/ppermute | solution.py:36
  35.5 5.2 %collective-permute-start.8 = (bf16[2,256,384]{2,1,0:T(8,128)(2,1)}, bf16[2,256,384]{2,1,0:T(8,128)(2,1)}, u32[]{:S(2)}, u32[]{:S(2)}) collective-permute-start(bf16[2,256,384]{2,1,0:T(8,128)(2,1)} %get-tuple-element.73.refs_0_), channel_id=1, source_target_pairs={{0,8},{4,12},{8,0},{12,4},{16,24},{20,28},{24,16},{28,20},{1,9},{5... | collective-permute-start | bytes 1179656 | tf_op jit(solution)/shard_map/ppermute | solution.py:36
  40.8 2.3 %collective-permute-start.9 = (bf16[2,256,384]{2,1,0:T(8,128)(2,1)}, bf16[2,256,384]{2,1,0:T(8,128)(2,1)}, u32[]{:S(2)}, u32[]{:S(2)}) collective-permute-start(bf16[2,256,384]{2,1,0:T(8,128)(2,1)} %get-tuple-element.73.refs_0_), channel_id=1, source_target_pairs={{0,24},{4,28},{8,16},{12,20},{16,8},{20,12},{24,0},{28,4},{1,25},{... | collective-permute-start | bytes 1179656 | tf_op jit(solution)/shard_map/ppermute | solution.py:36
  43.1 5.1 %shard_map.56.refs_6_ = f32[3,512,256]{2,1,0:T(8,128)S(1)} custom-call(s32[2]{0:T(128)S(1)} %pad_add_fusion.where_ref, bf16[2048,4096]{1,0:T(8,128)(2,1)} %refs_0_.29, bf16[2048,4096]{1,0:T(8,128)(2,1)} %refs_0_.29, bf16[2048,4096]{1,0:T(8,128)(2,1)} %refs_0_.29, bf16[2048,4096]{1,0:T(8,128)(2,1)} %refs_0_.29, ...), custom_call_target="tpu_custom_call" | custom-call | flops 1610612736 | bytes 6291456 | tf_op jit(solution)/shard_map/pallas_call | solution.py:213
  48.3 4.5 %shard_map.57.refs_2_ = f32[3,512,256]{2,1,0:T(8,128)S(1)} custom-call(s32[2]{0:T(128)S(1)} %pad_add_fusion.where_ref, bf16[2048,4096]{1,0:T(8,128)(2,1)} %refs_0_.29, bf16[2048,4096]{1,0:T(8,128)(2,1)} %refs_0_.29, bf16[2048,4096]{1,0:T(8,128)(2,1)} %refs_0_.29, bf16[528,256]{1,0:T(8,128)(2,1)S(1)} %collective-permute-done.2.refs_3_.refs_11_, ...), custom_call_target="tpu_custom_call" | custom-call | flops 1207959552 | bytes 4718592 | tf_op jit(solution)/shard_map/pallas_call | solution.py:213
  69.3 7.1 %shard_map.61.refs_6_ = f32[512,4096]{1,0:T(8,128)S(1)} custom-call(s32[2]{0:T(128)S(1)} %pad_add_fusion.where_ref, s32[96]{0:T(128)S(1)} %reshape.34.tiles_ref, bf16[2,256,384]{2,1,0:T(8,128)(2,1)} %get-tuple-element.73.refs_0_, bf16[2,256,384]{2,1,0:T(8,128)(2,1)} %collective-permute-done.7.refs_1_, bf16[2,256,384]{2,1,0:T(8,128)(2,1)} %collective-permute-done.8.refs_2_, ...), custom_call_target="tpu_custom_call" | custom-call | flops 301989888 | bytes 19136512 | tf_op jit(solution)/shard_map/pallas_call | solution.py:174
  76.4 3.2 %collective-permute-start.16 = (bf16[2,256,384]{2,1,0:T(8,128)(2,1)}, bf16[2,256,384]{2,1,0:T(8,128)(2,1)S(1)}, u32[]{:S(2)}, u32[]{:S(2)}) collective-permute-start(bf16[2,256,384]{2,1,0:T(8,128)(2,1)} %collective-permute-done.13.refs_2_), channel_id=1, source_target_pairs={{0,4},{4,0},{8,12},{12,8},{16,20},{20,16},{24,28},{28,24},{1,5},{5... | collective-permute-start | bytes 1179656 | tf_op jit(solution)/shard_map/ppermute | solution.py:36
  81.7 4.2 %shard_map.62.refs_6_ = f32[512,4096]{1,0:T(8,128)S(1)} custom-call(s32[2]{0:T(128)S(1)} %pad_add_fusion.where_ref, s32[96]{0:T(128)S(1)} %reshape.34.tiles_ref, bf16[2,256,384]{2,1,0:T(8,128)(2,1)} %collective-permute-done.11.refs_0_, bf16[2,256,384]{2,1,0:T(8,128)(2,1)} %collective-permute-done.12.refs_1_, ...), custom_call_target="tpu_custom_call" | custom-call | flops 201326592 | bytes 18350080 | tf_op jit(solution)/shard_map/pallas_call | solution.py:174
  85.9 4.0 %collective-permute-done.16.refs_1_ = bf16[2,256,384]{2,1,0:T(8,128)(2,1)S(1)} collective-permute-done((bf16[2,256,384]{2,1,0:T(8,128)(2,1)}, bf16[2,256,384]{2,1,0:T(8,128)(2,1)S(1)}, u32[]{:S(2)}, u32[]{:S(2)}) %collective-permute-start.16) | collective-permute-done | bytes 393248 | tf_op jit(solution)/shard_map/ppermute | solution.py:36
  91.9 3.2 %collective-permute-done.18.refs_3_ = bf16[2,256,384]{2,1,0:T(8,128)(2,1)S(1)} collective-permute-done((bf16[2,256,384]{2,1,0:T(8,128)(2,1)}, bf16[2,256,384]{2,1,0:T(8,128)(2,1)S(1)}, u32[]{:S(2)}, u32[]{:S(2)}) %collective-permute-start.18) | collective-permute-done | bytes 393248 | tf_op jit(solution)/shard_map/ppermute | solution.py:36
  97.5 2.6 %collective-permute-start.22 = (bf16[512,256]{1,0:T(8,128)(2,1)S(1)}, bf16[512,256]{1,0:T(8,128)(2,1)S(1)}, u32[]{:S(2)}, u32[]{:S(2)}) collective-permute-start(bf16[512,256]{1,0:T(8,128)(2,1)S(1)} %shard_map.59), channel_id=1, source_target_pairs={{0,2},{1,3},{2,0},{3,1},{4,6},{5,7},{6,4},{7,5},{8,10},{9,11},{10,... | collective-permute-start | bytes 786440 | tf_op jit(solution)/shard_map/ppermute | solution.py:36
  101.9 2.8 %collective-permute-done.20.refs_1_ = bf16[2,256,384]{2,1,0:T(8,128)(2,1)S(1)} collective-permute-done((bf16[2,256,384]{2,1,0:T(8,128)(2,1)S(1)}, bf16[2,256,384]{2,1,0:T(8,128)(2,1)S(1)}, u32[]{:S(2)}, u32[]{:S(2)}) %collective-permute-start.20) | collective-permute-done | bytes 393248 | tf_op jit(solution)/shard_map/ppermute | solution.py:36
  105.5 2.9 %shard_map.64.refs_0_.refs_1_.refs_2_.refs_3_.refs_4_.refs_5_.refs_6_.refs_7_ = bf16[512,4096]{1,0:T(8,128)(2,1)S(1)} custom-call(s32[2]{0:T(128)S(1)} %pad_add_fusion.where_ref, s32[96]{0:T(128)S(1)} %reshape.34.tiles_ref, bf16[2,256,384]{2,1,0:T(8,128)(2,1)S(1)} %collective-permute-done.19.refs_0_, ...), custom_call_target="tpu_custom_call" | custom-call | flops 100663296 | bytes 17563648 | tf_op jit(solution)/shard_map/pallas_call | solution.py:174
  115.6 7.4 %collective-permute-done.27.refs_7_.refs_14_ = bf16[512,256]{1,0:T(8,128)(2,1)S(1)} collective-permute-done((bf16[512,256]{1,0:T(8,128)(2,1)S(1)}, bf16[512,256]{1,0:T(8,128)(2,1)S(1)}, u32[]{:S(2)}, u32[]{:S(2)}) %collective-permute-start.27) | collective-permute-done | bytes 262176 | tf_op jit(solution)/shard_map/ppermute | solution.py:36
  125.3 3.0 %collective-permute-start.28 = (bf16[512,256]{1,0:T(8,128)(2,1)S(1)}, bf16[512,256]{1,0:T(8,128)(2,1)S(1)}, u32[]{:S(2)}, u32[]{:S(2)}) collective-permute-start(bf16[512,256]{1,0:T(8,128)(2,1)S(1)} %collective-permute-done.27.refs_7_.refs_14_), channel_id=1, source_target_pairs={{0,8},{4,12},{8,0},{12,4},{16,24},{20,28},{24,16},{28,20},{1,9},{5... | collective-permute-start | bytes 786440 | tf_op jit(solution)/shard_map/ppermute | solution.py:36
  128.8 3.4 %shard_map.66.refs_6_ = f32[3,512,256]{2,1,0:T(8,128)S(1)} custom-call(s32[2]{0:T(128)S(1)} %pad_add_fusion.where_ref, bf16[2048,4096]{1,0:T(8,128)(2,1)S(1)} %bitcast.15, bf16[2048,4096]{1,0:T(8,128)(2,1)S(1)} %bitcast.15, bf16[2048,4096]{1,0:T(8,128)(2,1)S(1)} %bitcast.15, bf16[2048,4096]{1,0:T(8,128)(2,1)S(1)} %bitcast.15, ...), custom_call_target="tpu_custom_call" | custom-call | flops 1610612736 | bytes 6291456 | tf_op jit(solution)/shard_map/pallas_call | solution.py:213
  132.3 3.7 %collective-permute-start.30 = (bf16[512,256]{1,0:T(8,128)(2,1)S(1)}, bf16[512,256]{1,0:T(8,128)(2,1)S(1)}, u32[]{:S(2)}, u32[]{:S(2)}) collective-permute-start(bf16[512,256]{1,0:T(8,128)(2,1)S(1)} %collective-permute-done.29.refs_15_.refs_5_), channel_id=1, source_target_pairs={{0,8},{4,12},{8,0},{12,4},{16,24},{20,28},{24,16},{28,20},{1,9},{5... | collective-permute-start | bytes 786440 | tf_op jit(solution)/shard_map/ppermute | solution.py:36
  136.0 2.8 %shard_map.68.refs_2_ = f32[3,512,256]{2,1,0:T(8,128)S(1)} custom-call(s32[2]{0:T(128)S(1)} %pad_add_fusion.where_ref, bf16[2048,4096]{1,0:T(8,128)(2,1)S(1)} %bitcast.15, bf16[2048,4096]{1,0:T(8,128)(2,1)S(1)} %bitcast.15, bf16[2048,4096]{1,0:T(8,128)(2,1)S(1)} %bitcast.15, bf16[512,256]{1,0:T(8,128)(2,1)S(1)} %collective-permute-done.26.refs_11_.refs_3_, ...), custom_call_target="tpu_custom_call" | custom-call | flops 1207959552 | bytes 4718592 | tf_op jit(solution)/shard_map/pallas_call | solution.py:213
  146.8 2.8 %collective-permute-done.31 = bf16[512,256]{1,0:T(8,128)(2,1)S(1)} collective-permute-done((bf16[512,256]{1,0:T(8,128)(2,1)S(1)}, bf16[512,256]{1,0:T(8,128)(2,1)S(1)}, u32[]{:S(2)}, u32[]{:S(2)}) %collective-permute-start.31) | collective-permute-done | bytes 262176 | tf_op jit(solution)/shard_map/ppermute | solution.py:36
  149.6 5.9 %collective-permute-done.32 = bf16[512,256]{1,0:T(8,128)(2,1)S(1)} collective-permute-done((bf16[512,256]{1,0:T(8,128)(2,1)S(1)}, bf16[512,256]{1,0:T(8,128)(2,1)S(1)}, u32[]{:S(2)}, u32[]{:S(2)}) %collective-permute-start.32) | collective-permute-done | bytes 262176 | tf_op jit(solution)/shard_map/ppermute | solution.py:36
  156.5 2.4 %collective-permute-start.35 = (bf16[512,256]{1,0:T(8,128)(2,1)S(1)}, bf16[512,256]{1,0:T(8,128)(2,1)S(1)}, u32[]{:S(2)}, u32[]{:S(2)}) collective-permute-start(bf16[512,256]{1,0:T(8,128)(2,1)S(1)} %fusion.2.refs_4_.refs_8_), channel_id=1, source_target_pairs={{0,8},{4,12},{8,0},{12,4},{16,24},{20,28},{24,16},{28,20},{1,9},{5... | collective-permute-start | bytes 786440 | tf_op jit(solution)/shard_map/ppermute | solution.py:36
  159.7 7.1 %collective-permute-done.37.refs_7_.refs_14_ = bf16[512,256]{1,0:T(8,128)(2,1)S(1)} collective-permute-done((bf16[512,256]{1,0:T(8,128)(2,1)S(1)}, bf16[512,256]{1,0:T(8,128)(2,1)S(1)}, u32[]{:S(2)}, u32[]{:S(2)}) %collective-permute-start.37) | collective-permute-done | bytes 262176 | tf_op jit(solution)/shard_map/ppermute | solution.py:36
  168.3 4.3 %collective-permute-start.38 = (bf16[512,256]{1,0:T(8,128)(2,1)S(1)}, bf16[512,256]{1,0:T(8,128)(2,1)S(1)}, u32[]{:S(2)}, u32[]{:S(2)}) collective-permute-start(bf16[512,256]{1,0:T(8,128)(2,1)S(1)} %collective-permute-done.37.refs_7_.refs_14_), channel_id=1, source_target_pairs={{0,8},{4,12},{8,0},{12,4},{16,24},{20,28},{24,16},{28,20},{1,9},{5... | collective-permute-start | bytes 786440 | tf_op jit(solution)/shard_map/ppermute | solution.py:36
  173.9 3.3 %shard_map.72.refs_6_ = f32[3,512,256]{2,1,0:T(8,128)S(1)} custom-call(s32[2]{0:T(128)S(1)} %pad_add_fusion.where_ref, bf16[2048,4096]{1,0:T(8,128)(2,1)S(1)} %bitcast.15, bf16[2048,4096]{1,0:T(8,128)(2,1)S(1)} %bitcast.15, bf16[2048,4096]{1,0:T(8,128)(2,1)S(1)} %bitcast.15, bf16[2048,4096]{1,0:T(8,128)(2,1)S(1)} %bitcast.15, ...), custom_call_target="tpu_custom_call" | custom-call | flops 1610612736 | bytes 6291456 | tf_op jit(solution)/shard_map/pallas_call | solution.py:213
  177.1 3.9 %collective-permute-start.40 = (bf16[512,256]{1,0:T(8,128)(2,1)S(1)}, bf16[512,256]{1,0:T(8,128)(2,1)S(1)}, u32[]{:S(2)}, u32[]{:S(2)}) collective-permute-start(bf16[512,256]{1,0:T(8,128)(2,1)S(1)} %collective-permute-done.39.refs_15_.refs_5_), channel_id=1, source_target_pairs={{0,8},{4,12},{8,0},{12,4},{16,24},{20,28},{24,16},{28,20},{1,9},{5... | collective-permute-start | bytes 786440 | tf_op jit(solution)/shard_map/ppermute | solution.py:36
  181.0 2.7 %shard_map.74.refs_2_ = f32[3,512,256]{2,1,0:T(8,128)S(1)} custom-call(s32[2]{0:T(128)S(1)} %pad_add_fusion.where_ref, bf16[2048,4096]{1,0:T(8,128)(2,1)S(1)} %bitcast.15, bf16[2048,4096]{1,0:T(8,128)(2,1)S(1)} %bitcast.15, bf16[2048,4096]{1,0:T(8,128)(2,1)S(1)} %bitcast.15, bf16[512,256]{1,0:T(8,128)(2,1)S(1)} %collective-permute-done.36.refs_11_.refs_3_, ...), custom_call_target="tpu_custom_call" | custom-call | flops 1207959552 | bytes 4718592 | tf_op jit(solution)/shard_map/pallas_call | solution.py:213
  192.1 3.1 %collective-permute-done.41 = bf16[512,256]{1,0:T(8,128)(2,1)S(1)} collective-permute-done((bf16[512,256]{1,0:T(8,128)(2,1)S(1)}, bf16[512,256]{1,0:T(8,128)(2,1)S(1)}, u32[]{:S(2)}, u32[]{:S(2)}) %collective-permute-start.41) | collective-permute-done | bytes 262176 | tf_op jit(solution)/shard_map/ppermute | solution.py:36
  195.2 3.9 %collective-permute-done.42 = bf16[512,256]{1,0:T(8,128)(2,1)S(1)} collective-permute-done((bf16[512,256]{1,0:T(8,128)(2,1)S(1)}, bf16[512,256]{1,0:T(8,128)(2,1)S(1)}, u32[]{:S(2)}, u32[]{:S(2)}) %collective-permute-start.42) | collective-permute-done | bytes 262176 | tf_op jit(solution)/shard_map/ppermute | solution.py:36
  (139 shorter events, 68.7 us)
Async XLA Ops:
  2.5 12.5 %collective-permute-start.3 = (bf16[528,256]{1,0:T(8,128)(2,1)S(1)}, bf16[528,256]{1,0:T(8,128)(2,1)S(1)}, u32[]{:S(2)}, u32[]{:S(2)}) collective-permute-start(bf16[528,256]{1,0:T(8,128)(2,1)S(1)} %constant_dynamic-update-slice_fusion.refs_0_.refs_4_.refs_8_), channel_id=1, source_target_pairs={{0,24},{4,28},{8,16},{12,20},{16,8},{20,12},{24,0},{28,4},{1,25},{... | collective-permute-start | bytes 811016 | tf_op jit(solution)/shard_map/ppermute | solution.py:36
  7.6 14.0 %collective-permute-start.1 = (bf16[528,256]{1,0:T(8,128)(2,1)S(1)}, bf16[528,256]{1,0:T(8,128)(2,1)S(1)}, u32[]{:S(2)}, u32[]{:S(2)}) collective-permute-start(bf16[528,256]{1,0:T(8,128)(2,1)S(1)} %constant_dynamic-update-slice_fusion.refs_0_.refs_4_.refs_8_), channel_id=1, source_target_pairs={{0,8},{4,12},{8,0},{12,4},{16,24},{20,28},{24,16},{28,20},{1,9},{5... | collective-permute-start | bytes 811016 | tf_op jit(solution)/shard_map/ppermute | solution.py:36
  16.7 14.4 %collective-permute-start = (bf16[528,256]{1,0:T(8,128)(2,1)S(1)}, bf16[528,256]{1,0:T(8,128)(2,1)S(1)}, u32[]{:S(2)}, u32[]{:S(2)}) collective-permute-start(bf16[528,256]{1,0:T(8,128)(2,1)S(1)} %constant_dynamic-update-slice_fusion.refs_0_.refs_4_.refs_8_), channel_id=1, source_target_pairs={{0,4},{4,0},{8,12},{12,8},{16,20},{20,16},{24,28},{28,24},{1,5},{5... | collective-permute-start | bytes 811016 | tf_op jit(solution)/shard_map/ppermute | solution.py:36
  17.0 14.1 %collective-permute-start.4 = (bf16[528,256]{1,0:T(8,128)(2,1)S(1)}, bf16[528,256]{1,0:T(8,128)(2,1)S(1)}, u32[]{:S(2)}, u32[]{:S(2)}) collective-permute-start(bf16[528,256]{1,0:T(8,128)(2,1)S(1)} %collective-permute-done.3.refs_6_.refs_7_.refs_14_), channel_id=1, source_target_pairs={{0,8},{4,12},{8,0},{12,4},{16,24},{20,28},{24,16},{28,20},{1,9},{5... | collective-permute-start | bytes 811016 | tf_op jit(solution)/shard_map/ppermute | solution.py:36
  21.7 11.8 %collective-permute-start.2 = (bf16[528,256]{1,0:T(8,128)(2,1)S(1)}, bf16[528,256]{1,0:T(8,128)(2,1)S(1)}, u32[]{:S(2)}, u32[]{:S(2)}) collective-permute-start(bf16[528,256]{1,0:T(8,128)(2,1)S(1)} %collective-permute-done.1.refs_2_.refs_6_.refs_10_), channel_id=1, source_target_pairs={{0,4},{4,0},{8,12},{12,8},{16,20},{20,16},{24,28},{28,24},{1,5},{5... | collective-permute-start | bytes 811016 | tf_op jit(solution)/shard_map/ppermute | solution.py:36
  33.5 24.5 %collective-permute-start.10 = (bf16[2,256,384]{2,1,0:T(8,128)(2,1)}, bf16[2,256,384]{2,1,0:T(8,128)(2,1)}, u32[]{:S(2)}, u32[]{:S(2)}) collective-permute-start(bf16[2,256,384]{2,1,0:T(8,128)(2,1)} %get-tuple-element.80.refs_4_), channel_id=1, source_target_pairs={{0,4},{4,0},{8,12},{12,8},{16,20},{20,16},{24,28},{28,24},{1,5},{5... | collective-permute-start | bytes 1179656 | tf_op jit(solution)/shard_map/ppermute | solution.py:36
  35.0 23.1 %collective-permute-start.7 = (bf16[2,256,384]{2,1,0:T(8,128)(2,1)}, bf16[2,256,384]{2,1,0:T(8,128)(2,1)}, u32[]{:S(2)}, u32[]{:S(2)}) collective-permute-start(bf16[2,256,384]{2,1,0:T(8,128)(2,1)} %get-tuple-element.73.refs_0_), channel_id=1, source_target_pairs={{0,4},{4,0},{8,12},{12,8},{16,20},{20,16},{24,28},{28,24},{1,5},{5... | collective-permute-start | bytes 1179656 | tf_op jit(solution)/shard_map/ppermute | solution.py:36
  35.5 22.5 %collective-permute-start.8 = (bf16[2,256,384]{2,1,0:T(8,128)(2,1)}, bf16[2,256,384]{2,1,0:T(8,128)(2,1)}, u32[]{:S(2)}, u32[]{:S(2)}) collective-permute-start(bf16[2,256,384]{2,1,0:T(8,128)(2,1)} %get-tuple-element.73.refs_0_), channel_id=1, source_target_pairs={{0,8},{4,12},{8,0},{12,4},{16,24},{20,28},{24,16},{28,20},{1,9},{5... | collective-permute-start | bytes 1179656 | tf_op jit(solution)/shard_map/ppermute | solution.py:36
  40.8 17.8 %collective-permute-start.9 = (bf16[2,256,384]{2,1,0:T(8,128)(2,1)}, bf16[2,256,384]{2,1,0:T(8,128)(2,1)}, u32[]{:S(2)}, u32[]{:S(2)}) collective-permute-start(bf16[2,256,384]{2,1,0:T(8,128)(2,1)} %get-tuple-element.73.refs_0_), channel_id=1, source_target_pairs={{0,24},{4,28},{8,16},{12,20},{16,8},{20,12},{24,0},{28,4},{1,25},{... | collective-permute-start | bytes 1179656 | tf_op jit(solution)/shard_map/ppermute | solution.py:36
  58.5 17.8 %collective-permute-start.13 = (bf16[2,256,384]{2,1,0:T(8,128)(2,1)}, bf16[2,256,384]{2,1,0:T(8,128)(2,1)}, u32[]{:S(2)}, u32[]{:S(2)}) collective-permute-start(bf16[2,256,384]{2,1,0:T(8,128)(2,1)} %get-tuple-element.80.refs_4_), channel_id=1, source_target_pairs={{0,8},{4,12},{8,0},{12,4},{16,24},{20,28},{24,16},{28,20},{1,9},{5... | collective-permute-start | bytes 1179656 | tf_op jit(solution)/shard_map/ppermute | solution.py:36
  58.5 17.8 %collective-permute-start.14 = (bf16[2,256,384]{2,1,0:T(8,128)(2,1)}, bf16[2,256,384]{2,1,0:T(8,128)(2,1)}, u32[]{:S(2)}, u32[]{:S(2)}) collective-permute-start(bf16[2,256,384]{2,1,0:T(8,128)(2,1)} %get-tuple-element.80.refs_4_), channel_id=1, source_target_pairs={{0,24},{4,28},{8,16},{12,20},{16,8},{20,12},{24,0},{28,4},{1,25},{... | collective-permute-start | bytes 1179656 | tf_op jit(solution)/shard_map/ppermute | solution.py:36
  60.0 16.4 %collective-permute-start.11 = (bf16[2,256,384]{2,1,0:T(8,128)(2,1)}, bf16[2,256,384]{2,1,0:T(8,128)(2,1)}, u32[]{:S(2)}, u32[]{:S(2)}) collective-permute-start(bf16[2,256,384]{2,1,0:T(8,128)(2,1)} %collective-permute-done.8.refs_2_), channel_id=1, source_target_pairs={{0,4},{4,0},{8,12},{12,8},{16,20},{20,16},{24,28},{28,24},{1,5},{5... | collective-permute-start | bytes 1179656 | tf_op jit(solution)/shard_map/ppermute | solution.py:36
  61.5 14.9 %collective-permute-start.12 = (bf16[2,256,384]{2,1,0:T(8,128)(2,1)}, bf16[2,256,384]{2,1,0:T(8,128)(2,1)}, u32[]{:S(2)}, u32[]{:S(2)}) collective-permute-start(bf16[2,256,384]{2,1,0:T(8,128)(2,1)} %collective-permute-done.9.refs_3_), channel_id=1, source_target_pairs={{0,4},{4,0},{8,12},{12,8},{16,20},{20,16},{24,28},{28,24},{1,5},{5... | collective-permute-start | bytes 1179656 | tf_op jit(solution)/shard_map/ppermute | solution.py:36
  76.4 13.5 %collective-permute-start.16 = (bf16[2,256,384]{2,1,0:T(8,128)(2,1)}, bf16[2,256,384]{2,1,0:T(8,128)(2,1)S(1)}, u32[]{:S(2)}, u32[]{:S(2)}) collective-permute-start(bf16[2,256,384]{2,1,0:T(8,128)(2,1)} %collective-permute-done.13.refs_2_), channel_id=1, source_target_pairs={{0,4},{4,0},{8,12},{12,8},{16,20},{20,16},{24,28},{28,24},{1,5},{5... | collective-permute-start | bytes 1179656 | tf_op jit(solution)/shard_map/ppermute | solution.py:36
  79.6 12.3 %collective-permute-start.17 = (bf16[2,256,384]{2,1,0:T(8,128)(2,1)}, bf16[2,256,384]{2,1,0:T(8,128)(2,1)S(1)}, u32[]{:S(2)}, u32[]{:S(2)}) collective-permute-start(bf16[2,256,384]{2,1,0:T(8,128)(2,1)} %collective-permute-done.14.refs_3_), channel_id=1, source_target_pairs={{0,8},{4,12},{8,0},{12,4},{16,24},{20,28},{24,16},{28,20},{1,9},{5... | collective-permute-start | bytes 1179656 | tf_op jit(solution)/shard_map/ppermute | solution.py:36
  80.0 15.1 %collective-permute-start.18 = (bf16[2,256,384]{2,1,0:T(8,128)(2,1)}, bf16[2,256,384]{2,1,0:T(8,128)(2,1)S(1)}, u32[]{:S(2)}, u32[]{:S(2)}) collective-permute-start(bf16[2,256,384]{2,1,0:T(8,128)(2,1)} %collective-permute-done.14.refs_3_), channel_id=1, source_target_pairs={{0,4},{4,0},{8,12},{12,8},{16,20},{20,16},{24,28},{28,24},{1,5},{5... | collective-permute-start | bytes 1179656 | tf_op jit(solution)/shard_map/ppermute | solution.py:36
  81.5 15.5 %collective-permute-start.15 = (bf16[2,256,384]{2,1,0:T(8,128)(2,1)}, bf16[2,256,384]{2,1,0:T(8,128)(2,1)S(1)}, u32[]{:S(2)}, u32[]{:S(2)}) collective-permute-start(bf16[2,256,384]{2,1,0:T(8,128)(2,1)} %collective-permute-done.9.refs_3_), channel_id=1, source_target_pairs={{0,8},{4,12},{8,0},{12,4},{16,24},{20,28},{24,16},{28,20},{1,9},{5... | collective-permute-start | bytes 1179656 | tf_op jit(solution)/shard_map/ppermute | solution.py:36
  97.5 12.8 %collective-permute-start.21 = (bf16[512,256]{1,0:T(8,128)(2,1)S(1)}, bf16[512,256]{1,0:T(8,128)(2,1)S(1)}, u32[]{:S(2)}, u32[]{:S(2)}) collective-permute-start(bf16[512,256]{1,0:T(8,128)(2,1)S(1)} %shard_map.58), channel_id=1, source_target_pairs={{0,3},{1,2},{2,1},{3,0},{4,7},{5,6},{6,5},{7,4},{8,11},{9,10},{10,... | collective-permute-start | bytes 786440 | tf_op jit(solution)/shard_map/ppermute | solution.py:36
  97.5 14.2 %collective-permute-start.22 = (bf16[512,256]{1,0:T(8,128)(2,1)S(1)}, bf16[512,256]{1,0:T(8,128)(2,1)S(1)}, u32[]{:S(2)}, u32[]{:S(2)}) collective-permute-start(bf16[512,256]{1,0:T(8,128)(2,1)S(1)} %shard_map.59), channel_id=1, source_target_pairs={{0,2},{1,3},{2,0},{3,1},{4,6},{5,7},{6,4},{7,5},{8,10},{9,11},{10,... | collective-permute-start | bytes 786440 | tf_op jit(solution)/shard_map/ppermute | solution.py:36
  100.1 11.6 %collective-permute-start.23 = (bf16[512,256]{1,0:T(8,128)(2,1)S(1)}, bf16[512,256]{1,0:T(8,128)(2,1)S(1)}, u32[]{:S(2)}, u32[]{:S(2)}) collective-permute-start(bf16[512,256]{1,0:T(8,128)(2,1)S(1)} %shard_map.60), channel_id=1, source_target_pairs={{0,1},{1,0},{2,3},{3,2},{4,5},{5,4},{6,7},{7,6},{8,9},{9,8},{10,11... | collective-permute-start | bytes 786440 | tf_op jit(solution)/shard_map/ppermute | solution.py:36
  111.9 11.2 %collective-permute-start.27 = (bf16[512,256]{1,0:T(8,128)(2,1)S(1)}, bf16[512,256]{1,0:T(8,128)(2,1)S(1)}, u32[]{:S(2)}, u32[]{:S(2)}) collective-permute-start(bf16[512,256]{1,0:T(8,128)(2,1)S(1)} %fusion.1.refs_4_.refs_8_), channel_id=1, source_target_pairs={{0,24},{4,28},{8,16},{12,20},{16,8},{20,12},{24,0},{28,4},{1,25},{... | collective-permute-start | bytes 786440 | tf_op jit(solution)/shard_map/ppermute | solution.py:36
  112.6 15.8 %collective-permute-start.25 = (bf16[512,256]{1,0:T(8,128)(2,1)S(1)}, bf16[512,256]{1,0:T(8,128)(2,1)S(1)}, u32[]{:S(2)}, u32[]{:S(2)}) collective-permute-start(bf16[512,256]{1,0:T(8,128)(2,1)S(1)} %fusion.1.refs_4_.refs_8_), channel_id=1, source_target_pairs={{0,8},{4,12},{8,0},{12,4},{16,24},{20,28},{24,16},{28,20},{1,9},{5... | collective-permute-start | bytes 786440 | tf_op jit(solution)/shard_map/ppermute | solution.py:36
  114.1 14.7 %collective-permute-start.24 = (bf16[512,256]{1,0:T(8,128)(2,1)S(1)}, bf16[512,256]{1,0:T(8,128)(2,1)S(1)}, u32[]{:S(2)}, u32[]{:S(2)}) collective-permute-start(bf16[512,256]{1,0:T(8,128)(2,1)S(1)} %fusion.1.refs_4_.refs_8_), channel_id=1, source_target_pairs={{0,4},{4,0},{8,12},{12,8},{16,20},{20,16},{24,28},{28,24},{1,5},{5... | collective-permute-start | bytes 786440 | tf_op jit(solution)/shard_map/ppermute | solution.py:36
  125.3 10.7 %collective-permute-start.28 = (bf16[512,256]{1,0:T(8,128)(2,1)S(1)}, bf16[512,256]{1,0:T(8,128)(2,1)S(1)}, u32[]{:S(2)}, u32[]{:S(2)}) collective-permute-start(bf16[512,256]{1,0:T(8,128)(2,1)S(1)} %collective-permute-done.27.refs_7_.refs_14_), channel_id=1, source_target_pairs={{0,8},{4,12},{8,0},{12,4},{16,24},{20,28},{24,16},{28,20},{1,9},{5... | collective-permute-start | bytes 786440 | tf_op jit(solution)/shard_map/ppermute | solution.py:36
  142.1 13.4 %collective-permute-start.32 = (bf16[512,256]{1,0:T(8,128)(2,1)S(1)}, bf16[512,256]{1,0:T(8,128)(2,1)S(1)}, u32[]{:S(2)}, u32[]{:S(2)}) collective-permute-start(bf16[512,256]{1,0:T(8,128)(2,1)S(1)} %shard_map.70), channel_id=1, source_target_pairs={{0,2},{1,3},{2,0},{3,1},{4,6},{5,7},{6,4},{7,5},{8,10},{9,11},{10,... | collective-permute-start | bytes 786440 | tf_op jit(solution)/shard_map/ppermute | solution.py:36
  144.7 10.7 %collective-permute-start.33 = (bf16[512,256]{1,0:T(8,128)(2,1)S(1)}, bf16[512,256]{1,0:T(8,128)(2,1)S(1)}, u32[]{:S(2)}, u32[]{:S(2)}) collective-permute-start(bf16[512,256]{1,0:T(8,128)(2,1)S(1)} %shard_map.71), channel_id=1, source_target_pairs={{0,1},{1,0},{2,3},{3,2},{4,5},{5,4},{6,7},{7,6},{8,9},{9,8},{10,11... | collective-permute-start | bytes 786440 | tf_op jit(solution)/shard_map/ppermute | solution.py:36
  155.7 11.1 %collective-permute-start.37 = (bf16[512,256]{1,0:T(8,128)(2,1)S(1)}, bf16[512,256]{1,0:T(8,128)(2,1)S(1)}, u32[]{:S(2)}, u32[]{:S(2)}) collective-permute-start(bf16[512,256]{1,0:T(8,128)(2,1)S(1)} %fusion.2.refs_4_.refs_8_), channel_id=1, source_target_pairs={{0,24},{4,28},{8,16},{12,20},{16,8},{20,12},{24,0},{28,4},{1,25},{... | collective-permute-start | bytes 786440 | tf_op jit(solution)/shard_map/ppermute | solution.py:36
  156.5 16.1 %collective-permute-start.35 = (bf16[512,256]{1,0:T(8,128)(2,1)S(1)}, bf16[512,256]{1,0:T(8,128)(2,1)S(1)}, u32[]{:S(2)}, u32[]{:S(2)}) collective-permute-start(bf16[512,256]{1,0:T(8,128)(2,1)S(1)} %fusion.2.refs_4_.refs_8_), channel_id=1, source_target_pairs={{0,8},{4,12},{8,0},{12,4},{16,24},{20,28},{24,16},{28,20},{1,9},{5... | collective-permute-start | bytes 786440 | tf_op jit(solution)/shard_map/ppermute | solution.py:36
  158.9 15.0 %collective-permute-start.34 = (bf16[512,256]{1,0:T(8,128)(2,1)S(1)}, bf16[512,256]{1,0:T(8,128)(2,1)S(1)}, u32[]{:S(2)}, u32[]{:S(2)}) collective-permute-start(bf16[512,256]{1,0:T(8,128)(2,1)S(1)} %fusion.2.refs_4_.refs_8_), channel_id=1, source_target_pairs={{0,4},{4,0},{8,12},{12,8},{16,20},{20,16},{24,28},{28,24},{1,5},{5... | collective-permute-start | bytes 786440 | tf_op jit(solution)/shard_map/ppermute | solution.py:36
  166.8 10.3 %collective-permute-start.39 = (bf16[512,256]{1,0:T(8,128)(2,1)S(1)}, bf16[512,256]{1,0:T(8,128)(2,1)S(1)}, u32[]{:S(2)}, u32[]{:S(2)}) collective-permute-start(bf16[512,256]{1,0:T(8,128)(2,1)S(1)} %collective-permute-done.37.refs_7_.refs_14_), channel_id=1, source_target_pairs={{0,4},{4,0},{8,12},{12,8},{16,20},{20,16},{24,28},{28,24},{1,5},{5... | collective-permute-start | bytes 786440 | tf_op jit(solution)/shard_map/ppermute | solution.py:36
  168.3 12.7 %collective-permute-start.38 = (bf16[512,256]{1,0:T(8,128)(2,1)S(1)}, bf16[512,256]{1,0:T(8,128)(2,1)S(1)}, u32[]{:S(2)}, u32[]{:S(2)}) collective-permute-start(bf16[512,256]{1,0:T(8,128)(2,1)S(1)} %collective-permute-done.37.refs_7_.refs_14_), channel_id=1, source_target_pairs={{0,8},{4,12},{8,0},{12,4},{16,24},{20,28},{24,16},{28,20},{1,9},{5... | collective-permute-start | bytes 786440 | tf_op jit(solution)/shard_map/ppermute | solution.py:36
  187.5 11.7 %collective-permute-start.42 = (bf16[512,256]{1,0:T(8,128)(2,1)S(1)}, bf16[512,256]{1,0:T(8,128)(2,1)S(1)}, u32[]{:S(2)}, u32[]{:S(2)}) collective-permute-start(bf16[512,256]{1,0:T(8,128)(2,1)S(1)} %shard_map.76), channel_id=1, source_target_pairs={{0,2},{1,3},{2,0},{3,1},{4,6},{5,7},{6,4},{7,5},{8,10},{9,11},{10,... | collective-permute-start | bytes 786440 | tf_op jit(solution)/shard_map/ppermute | solution.py:36
  (31 other events, 299.5 us)
